TPU v7x, 256 devices: a whole 4x4x8 slice. The times are simulated.
256 devices in a mesh: row: 8 (over y, x_lo), col: 32 (over x_hi, z, core).
Axes of the slice: x: 4 (x_hi: 2, x_lo: 2; x = x_hi * 2 + x_lo), y: 4, z: 8, core: 2. Of those that a mesh axis runs over, the one named last changes fastest.
Arguments:
- embeddings: float32 [24576, 1024], P(('col', 'row')), may hold values from -8 to 8
Outputs:
- smoothed: float32 [24576, 1024], P(('col', 'row'))
- log_density: float32 [24576], P(('col', 'row'))
All inputs are finite; a program needn't handle non-finite values.
Results may differ from a plain program's by a relative error of at most 0.022.
Values may be sent and summed in bfloat16 or wider, within the bound.
No kernel may reach another device: no remote copies, remote signals or barrier semaphores. Data moves between devices by JAX's collectives and lax.ppermute only.
A program may use at most 64 MiB of HBM per device.

v0:
```python
import jax
import jax.numpy as jnp
from jax import lax
from jax.sharding import PartitionSpec as P

SHARPNESS = 24.0


def kernel_terms(queries, q_squares, query_index, keys, key_index, width):
    keys_f = keys.astype(jnp.float32)
    k_squares = jnp.sum(keys_f * keys_f, axis=1)
    dots = lax.dot_general(
        queries, keys, (((1,), (1,)), ((), ())), preferred_element_type=jnp.float32
    )
    expo = SHARPNESS * (2.0 - (q_squares[:, None] + k_squares[None, :] - 2.0 * dots) / width)
    kern = jnp.where(query_index[:, None] == key_index[None, :], 0.0, jnp.exp(expo))
    total = jnp.sum(kern, axis=1)
    numer = jnp.dot(kern.astype(jnp.bfloat16), keys, preferred_element_type=jnp.float32)
    return (numer, total)


def shards(embeddings):
    rows = embeddings.shape[0]
    width = embeddings.shape[1]
    row_count = lax.axis_size("row")
    col_count = lax.axis_size("col")
    row_pos = lax.axis_index("row")
    col_pos = lax.axis_index("col")
    count = rows * row_count * col_count
    first = jnp.sum(embeddings, axis=0)
    second = jnp.dot(
        embeddings.T,
        embeddings,
        precision=lax.Precision.HIGHEST,
        preferred_element_type=jnp.float32,
    )
    first_all, second_all = lax.psum((first, second), ("row", "col"))
    mean = first_all / count
    cov = second_all / count - jnp.outer(mean, mean)
    chol = jnp.linalg.cholesky(cov)
    centred = embeddings - mean[None, :]
    white = lax.linalg.triangular_solve(
        chol, centred, left_side=False, lower=True, transpose_a=True
    ).astype(jnp.bfloat16)
    queries = lax.all_gather(white, "row", axis=0, tiled=True)
    queries_f = queries.astype(jnp.float32)
    q_squares = jnp.sum(queries_f * queries_f, axis=1)
    query_index = col_pos * row_count * rows + jnp.arange(row_count * rows, dtype=jnp.int32)
    piece = lax.all_gather(white, "col", axis=0, tiled=True)
    place = jnp.arange(piece.shape[0], dtype=jnp.int32)
    key_index = (place // rows * row_count + row_pos) * rows + place % rows
    numer, total = kernel_terms(queries, q_squares, query_index, piece, key_index, width)
    numer_part = numer
    total_part = total
    numer, total = (
        lax.psum_scatter(
            numer_part.astype(jnp.bfloat16), "row", scatter_dimension=0, tiled=True
        ).astype(jnp.float32),
        lax.psum_scatter(
            total_part.astype(jnp.bfloat16), "row", scatter_dimension=0, tiled=True
        ).astype(jnp.float32),
    )
    smoothed = numer / total[:, None]
    log_density = jnp.log(total / (count - 1))
    return (smoothed, log_density)


def solution(mesh):
    in_specs = (P(("col", "row"), None),)
    out_specs = (P(("col", "row"), None), P(("col", "row")))
    return jax.shard_map(shards, mesh=mesh, in_specs=in_specs, out_specs=out_specs, check_vma=False)
```

profile of v0, /device:TPU:1, one launch (start us, length us, event | category | flops | bytes accessed | tf_op | source)
XLA Modules:
  0.0 835.4 jit_solution(2614689208604362718)
XLA Ops:
  7.2 6.7 fusion.80
  14.0 81.5 %psum.14 = f32[1024]{0:T(1024)S(1)} all-reduce(f32[1024]{0:T(1024)S(1)} %reduce_sum.36), channel_id=1, replica_groups=mesh['row'=8,'col'=32] {'row','col'}, use_global_device_ids=true, to_apply=%region_1.0 | all-reduce | flops 1024 | bytes 8192 | tf_op jit(solution)/shard_map/psum | solution.py:37
  95.5 189.7 %all-reduce.4.cloned.1.call-done = f32[1024,1024]{0,1:T(8,128)} async-done(((f32[1024,1024]{0,1:T(8,128)}), f32[1024,1024]{0,1:T(8,128)}) %all-reduce.4.cloned.1.call-update) | async-done | bytes 4194320 | tf_op jit(solution)/shard_map/psum | solution.py:37
  285.2 4.6 multiply_subtract_fusion
  289.8 5.8 copy.6
  295.6 4.2 fusion.2
  299.8 1.9 copy-done
  301.8 11.7 %cholesky.223 = f32[128,128]{1,0:T(8,128)S(1)} custom-call(f32[128,128]{1,0:T(8,128)S(1)} %cholesky.580), custom_call_target="Cholesky" | custom-call | tf_op jit(solution)/shard_map/jit(cholesky)/cholesky | solution.py:40
  313.5 2.5 cholesky.255
  316.0 9.8 %custom-call.62 = f32[1,128,128]{1,2,0:T(8,128)S(1)} custom-call(f32[1,128,128]{2,1,0:T(8,128)S(1)} %get-tuple-element.43), custom_call_target="InvertDiagBlocksLowerTriangular" | custom-call | tf_op jit(solution)/shard_map/jit(cholesky)/cholesky | solution.py:40
  325.8 2.4 constant_dynamic-update-slice_fusion.31
  328.2 1.5 convolution_subtract_fusion
  329.8 11.7 %cholesky.244 = f32[128,128]{1,0:T(8,128)S(1)} custom-call(f32[128,128]{1,0:T(8,128)S(1)} %cholesky.584), custom_call_target="Cholesky" | custom-call | tf_op jit(solution)/shard_map/jit(cholesky)/cholesky | solution.py:40
  342.1 9.9 %custom-call.63 = f32[1,128,128]{1,2,0:T(8,128)S(1)} custom-call(f32[1,128,128]{2,1,0:T(8,128)S(1)} %get-tuple-element.40), custom_call_target="InvertDiagBlocksLowerTriangular" | custom-call | tf_op jit(solution)/shard_map/jit(cholesky)/cholesky | solution.py:40
  352.1 1.2 convolution_dynamic-update-slice_fusion
  353.3 2.1 convolution_subtract_fusion.1
  355.4 11.7 %cholesky.468 = f32[128,128]{1,0:T(8,128)S(1)} custom-call(f32[128,128]{1,0:T(8,128)S(1)} %cholesky.589), custom_call_target="Cholesky" | custom-call | tf_op jit(solution)/shard_map/jit(cholesky)/cholesky | solution.py:40
  368.4 9.8 %custom-call.64 = f32[1,128,128]{1,2,0:T(8,128)S(1)} custom-call(f32[1,128,128]{2,1,0:T(8,128)S(1)} %get-tuple-element.37), custom_call_target="InvertDiagBlocksLowerTriangular" | custom-call | tf_op jit(solution)/shard_map/jit(cholesky)/cholesky | solution.py:40
  378.2 1.2 convolution_dynamic-update-slice_fusion.1
  379.4 2.3 convolution_subtract_fusion.2
  381.7 11.9 %cholesky.487 = f32[128,128]{1,0:T(8,128)S(1)} custom-call(f32[128,128]{1,0:T(8,128)S(1)} %cholesky.594), custom_call_target="Cholesky" | custom-call | tf_op jit(solution)/shard_map/jit(cholesky)/cholesky | solution.py:40
  394.9 9.8 %custom-call.65 = f32[1,128,128]{1,2,0:T(8,128)S(1)} custom-call(f32[1,128,128]{2,1,0:T(8,128)S(1)} %get-tuple-element.34), custom_call_target="InvertDiagBlocksLowerTriangular" | custom-call | tf_op jit(solution)/shard_map/jit(cholesky)/cholesky | solution.py:40
  404.7 1.1 convolution_dynamic-update-slice_fusion.2
  405.8 2.3 convolution_subtract_fusion.3
  408.2 11.7 %cholesky.506 = f32[128,128]{1,0:T(8,128)S(1)} custom-call(f32[128,128]{1,0:T(8,128)S(1)} %cholesky.599), custom_call_target="Cholesky" | custom-call | tf_op jit(solution)/shard_map/jit(cholesky)/cholesky | solution.py:40
  421.2 9.8 %custom-call.66 = f32[1,128,128]{1,2,0:T(8,128)S(1)} custom-call(f32[1,128,128]{2,1,0:T(8,128)S(1)} %get-tuple-element.31), custom_call_target="InvertDiagBlocksLowerTriangular" | custom-call | tf_op jit(solution)/shard_map/jit(cholesky)/cholesky | solution.py:40
  431.0 1.4 convolution_dynamic-update-slice_fusion.3
  432.4 2.3 convolution_subtract_fusion.4
  434.7 11.7 %cholesky.526 = f32[128,128]{1,0:T(8,128)S(1)} custom-call(f32[128,128]{1,0:T(8,128)S(1)} %cholesky.604), custom_call_target="Cholesky" | custom-call | tf_op jit(solution)/shard_map/jit(cholesky)/cholesky | solution.py:40
  447.7 9.8 %custom-call.67 = f32[1,128,128]{1,2,0:T(8,128)S(1)} custom-call(f32[1,128,128]{2,1,0:T(8,128)S(1)} %get-tuple-element.28), custom_call_target="InvertDiagBlocksLowerTriangular" | custom-call | tf_op jit(solution)/shard_map/jit(cholesky)/cholesky | solution.py:40
  457.5 0.9 convolution_dynamic-update-slice_fusion.4
  458.5 2.0 convolution_subtract_fusion.5
  460.5 11.7 %cholesky.546 = f32[128,128]{1,0:T(8,128)S(1)} custom-call(f32[128,128]{1,0:T(8,128)S(1)} %cholesky.609), custom_call_target="Cholesky" | custom-call | tf_op jit(solution)/shard_map/jit(cholesky)/cholesky | solution.py:40
  473.5 9.9 %custom-call.68 = f32[1,128,128]{1,2,0:T(8,128)S(1)} custom-call(f32[1,128,128]{2,1,0:T(8,128)S(1)} %get-tuple-element.25), custom_call_target="InvertDiagBlocksLowerTriangular" | custom-call | tf_op jit(solution)/shard_map/jit(cholesky)/cholesky | solution.py:40
  483.4 0.8 convolution_dynamic-update-slice_fusion.5
  484.2 1.8 convolution_subtract_fusion.6
  486.0 11.7 %cholesky.564 = f32[128,128]{1,0:T(8,128)S(1)} custom-call(f32[128,128]{1,0:T(8,128)S(1)} %convolution_subtract_fusion.6), custom_call_target="Cholesky" | custom-call | tf_op jit(solution)/shard_map/jit(cholesky)/cholesky | solution.py:40
  504.5 4.8 select_select_fusion
  509.3 23.0 %while.1 = (s32[]{:T(128)}, f32[1024,1024]{1,0:T(8,128)}, s32[8,2]{0,1:T(2,128)S(1)}, f32[8,128,128]{2,1,0:T(8,128)S(1)}, s32[]{:T(128)}) while((s32[]{:T(128)}, f32[1024,1024]{1,0:T(8,128)}, s32[8,2]{0,1:T(2,128)S(1)}, f32[8,128,128]{2,1,0:T(8,128)S(1)}, s32[]{:T(128)}) %tuple.60), condition=%wide.while_cond, body=%wide.while_body.sunk | while | flops 2 | bytes 131181 | solution.py:42
  509.9 2.3 bitcast_dynamic-update-slice_fusion.2
  512.8 2.3 bitcast_dynamic-update-slice_fusion.2
  515.7 2.3 bitcast_dynamic-update-slice_fusion.2
  518.6 2.3 bitcast_dynamic-update-slice_fusion.2
  521.5 2.3 bitcast_dynamic-update-slice_fusion.2
  524.4 2.3 bitcast_dynamic-update-slice_fusion.2
  527.2 2.3 bitcast_dynamic-update-slice_fusion.2
  530.1 2.2 bitcast_dynamic-update-slice_fusion.2
  532.3 78.8 %custom-call.69 = f32[8,128,128]{1,2,0:T(8,128)S(1)} custom-call(f32[8,128,128]{2,1,0:T(8,128)S(1)} %get-tuple-element.9), custom_call_target="InvertDiagBlocksLowerTriangular" | custom-call | tf_op jit(solution)/shard_map/triangular_solve | solution.py:42
  611.4 1.1 convolution_subtract_fusion.10
  612.7 1.2 convolution_subtract_fusion.9
  614.1 1.3 convolution_subtract_fusion.13
  615.6 1.3 convolution_subtract_fusion.12
  617.2 1.5 convolution_subtract_fusion.11
  618.9 1.5 convolution_subtract_fusion.8
  620.7 1.7 convolution_subtract_fusion.7
  624.1 43.4 %all-gather.3.cloned.1.call-done = bf16[768,1024]{1,0:T(8,128)(2,1)} async-done(((bf16[96,1024]{1,0:T(8,128)(2,1)}), bf16[768,1024]{1,0:T(8,128)(2,1)}) %all-gather.3.cloned.1.call-update) | async-done | bytes 1572880 | tf_op jit(solution)/shard_map/all_gather | solution.py:45
  667.5 1.9 multiply_reduce_fusion.1
  669.4 98.4 %all-gather.5.cloned.1.call-done = bf16[3072,1024]{1,0:T(8,128)(2,1)} async-done(((bf16[96,1024]{1,0:T(8,128)(2,1)}), bf16[3072,1024]{1,0:T(8,128)(2,1)}) %all-gather.5.cloned.1.call-update) | async-done | bytes 6291472 | tf_op jit(solution)/shard_map/all_gather | solution.py:49
  767.8 4.2 multiply_reduce_fusion
  772.4 8.2 fusion.79
  780.7 6.2 fusion.3
  788.2 16.0 %all-reduce.1 = bf16[768]{0:T(1024)(128)(2,1)S(1)} all-reduce(bf16[768]{0:T(1024)(128)(2,1)S(1)} %get-tuple-element.77), channel_id=3, replica_groups=mesh['row'=8,'col'=32] {'row'}, use_global_device_ids=true, to_apply=%region_23.24.clone | all-reduce | flops 768 | bytes 3072
  804.8 22.1 %reduce-scatter.2.cloned.1.call-done = bf16[96,1024]{1,0:T(8,128)(2,1)} async-done(((bf16[768,1024]{1,0:T(8,128)(2,1)}), bf16[96,1024]{1,0:T(8,128)(2,1)}) %reduce-scatter.2.cloned.1.call-update) | async-done | bytes 196624 | tf_op jit(solution)/shard_map/reduce_scatter | solution.py:56
  826.9 1.8 convert_divide_fusion
  (82 shorter events, 18.8 us)
Async XLA Ops:
  7.2 6.8 copy-start.1
  7.2 278.0 %all-reduce.4.cloned.1.call-start = ((), (), s32[]{:S(2)}) async-start(), calls=%async_computation.1 | async-start | bytes 8388608 | tf_op jit(solution)/shard_map/psum | solution.py:37
  13.9 653.6 %all-gather.3.cloned.1.call-start = ((), (), s32[]{:S(2)}) async-start(), calls=%async_computation.2 | async-start | bytes 1769472 | tf_op jit(solution)/shard_map/all_gather | solution.py:45
  299.8 1.9 copy-start
  622.6 0.7 copy-start.4
  623.3 144.6 %all-gather.5.cloned.1.call-start = ((), (), s32[]{:S(2)}) async-start(), calls=%async_computation.3 | async-start | bytes 6488064 | tf_op jit(solution)/shard_map/all_gather | solution.py:49
  624.0 202.9 %reduce-scatter.2.cloned.1.call-start = ((), (), s32[]{:S(2)}) async-start(), calls=%async_computation.4 | async-start | bytes 1769472 | tf_op jit(solution)/shard_map/reduce_scatter | solution.py:56
  667.5 104.6 %copy-start.3 = (bf16[768,1024]{1,0:T(8,128)(2,1)S(1)}, bf16[768,1024]{1,0:T(8,128)(2,1)}, u32[]{:S(2)}) copy-start(bf16[768,1024]{1,0:T(8,128)(2,1)} %all-gather.3.cloned.1.call-done) | copy-start | bytes 4718596
  767.8 4.6 copy-start.2
  780.6 6.3 copy-start.5
Sparse Core Ops, SparseCore 0:
  14.0 271.1 all-reduce.3
  623.4 44.0 all-gather.2
  671.2 96.5 all-gather.4
  787.1 39.7 reduce-scatter.1
where the time goes:
time: 844 us; the launch traced here: 835 us
  waiting for transfers between devices  354 us (42%)
  other arithmetic  273 us (32%)
  blocking collectives  97.4 us (12%)
  matrix products  55.8 us (7%)
  local copies, waits for them, and re-layouts  34.8 us (4%)
  between operations  19.9 us (2%)
    psum x1, waiting for transfers between devices, shards(): first_all, second_all = lax.psum((first, second), ('row', 'col'))  190 us
    another operation x30, other arithmetic, shards(): chol = jnp.linalg.cholesky(cov)  172 us
    all_gather x1, waiting for transfers between devices, shards(): piece = lax.all_gather(white, 'col', axis=0, tiled=True)  98.4 us
    another operation x3, other arithmetic, shards(): lax.linalg.triangular_solve(chol, centred, left_side=False, lower=True, t...  83.6 us
    psum x1, blocking collectives, shards(): first_all, second_all = lax.psum((first, second), ('row', 'col'))  81.5 us
    all_gather x1, waiting for transfers between devices, shards(): queries = lax.all_gather(white, 'row', axis=0, tiled=True)  43.4 us
    another operation x14, matrix products, shards(): chol = jnp.linalg.cholesky(cov)  23.5 us
    another operation x24, local copies, waits for them, and re-layouts  22.8 us
  transfers between devices with their start and end apart: 4, of which 4 were waited for; matrix products, arithmetic and copies ran while one was open for 0% of the time, Pallas kernels for 0%

commit v1 on v0

v1 whole, which is shorter than its diff:
```python
import functools
import math
import jax
import jax.numpy as jnp
from jax import lax
from jax.experimental import pallas as pl
from jax.experimental.pallas import tpu as pltpu
from jax.sharding import PartitionSpec as P

SHARPNESS = 24.0
BLOCK = 128
PANEL = 16
EXTRA = 128
VMEM = 56 * 2**20
AXES = ("row", "col")
NN = ((1,), (0,))
NT = ((1,), (1,))
BF16 = jnp.bfloat16
F32 = jnp.float32


def split(a):
    hi = a.astype(BF16)
    return hi, (a - hi.astype(F32)).astype(BF16)


def mul(a, b, dims):
    return lax.dot_general(a, b, (dims, ((), ())), preferred_element_type=F32)


def dot3(a, b, dims):
    a_hi, a_lo = split(a)
    b_hi, b_lo = split(b)
    return mul(a_hi, b_hi, dims) + (mul(a_hi, b_lo, dims) + mul(a_lo, b_hi, dims))


def iota(shape, dim):
    return lax.broadcasted_iota(jnp.int32, shape, dim)


def moments_kernel(core_ref, x_ref, keep_ref, send_ref, packed):
    rows, width = x_ref.shape
    half = width // 2
    x = jnp.concatenate([x_ref[...], jnp.zeros((BLOCK - rows, width), F32)], 0)
    hi, lo = split(x)
    xt = jnp.concatenate([x[:, c : c + BLOCK].T for c in range(0, width, BLOCK)], 0)
    xt_hi, xt_lo = split(xt)
    left = jnp.concatenate([xt_hi, xt_lo], 1)
    ones = jnp.where(iota((BLOCK, EXTRA), 1) == 0, 1.0, 0.0).astype(BF16)
    none = jnp.zeros((BLOCK, EXTRA), BF16)
    one = jnp.concatenate([jnp.concatenate([hi, ones], 1), jnp.concatenate([lo, ones], 1)], 0)
    two = jnp.concatenate([jnp.concatenate([lo, none], 1), jnp.concatenate([hi, none], 1)], 0)
    low = mul(left[half:], one, NN) + mul(left[half:], two, NN)
    up = mul(left[:half], one[:, :half], NN) + mul(left[:half], two[:, :half], NN)
    up_sum = mul(left[:half], one[:, width:], NN)
    r, c = iota((half, half), 0), iota((half, half), 1)
    diag = jnp.sum(jnp.where(r == c, up, 0.0), axis=1, keepdims=True)
    lane = iota((half, EXTRA), 1)
    packed[:, :half] = low[:, :half]
    packed[:, half:width] = jnp.where(r >= c, low[:, half:width], up)
    packed[:, width:] = jnp.where(
        lane == 0,
        low[:, width:],
        jnp.where(lane == 1, up_sum[:, :1], jnp.where(lane == 2, diag, 0.0)),
    )
    part = half // 2
    core = core_ref[0]
    keep_ref[...] = packed[pl.ds(pl.multiple_of(core * part, part), part), :]
    send_ref[...] = packed[pl.ds(pl.multiple_of((1 - core) * part, part), part), :]


def moments(core, x):
    width = x.shape[1]
    half = width // 2
    out = jax.ShapeDtypeStruct((half // 2, width + EXTRA), F32)
    return pl.pallas_call(
        moments_kernel,
        out_shape=(out, out),
        in_specs=[
            pl.BlockSpec(memory_space=pltpu.SMEM),
            pl.BlockSpec(memory_space=pltpu.VMEM),
        ],
        out_specs=(pl.BlockSpec(memory_space=pltpu.VMEM),) * 2,
        scratch_shapes=[pltpu.VMEM((half, width + EXTRA), F32)],
        compiler_params=pltpu.CompilerParams(vmem_limit_bytes=VMEM),
        name="moments",
    )(core, x)


def diag_factor(g, w):
    lane = iota((PANEL, BLOCK), 1)
    sub = iota((PANEL, BLOCK), 0)
    for o in range(0, BLOCK, PANEL):
        r = g[o : o + PANEL, :]
        cols = [jnp.broadcast_to(r[:, o + s : o + s + 1], r.shape) for s in range(PANEL)]
        inside = (lane >= o) & (lane < o + PANEL)
        e = jnp.where(inside, jnp.where(lane - o == sub, 1.0, 0.0), r)
        y = jnp.zeros_like(r)
        for s in range(PANEL):
            d = jnp.broadcast_to(cols[s][s : s + 1, :], r.shape)
            inv = 1.0 / d
            m = cols[s] * inv
            pivot = jnp.broadcast_to(e[s : s + 1, :], r.shape)
            y = jnp.where(sub == s, pivot * lax.rsqrt(d), y)
            e = jnp.where(sub != s, e - m * pivot, pivot * inv)
            for t in range(s + 1, PANEL):
                c = jnp.broadcast_to(cols[t][s : s + 1, :], r.shape)
                cols[t] = jnp.where(sub != s, cols[t] - m * c, c * inv)
        w[o : o + PANEL, :] = jnp.where(lane <= sub + o, y, 0.0)
        after = o + PANEL
        if after < BLOCK:
            rest = g[after:, :]
            place = iota(rest.shape, 1)
            inside = (place >= o) & (place < after)
            parts = [e, jnp.zeros((BLOCK - after, BLOCK), F32)]
            if o:
                parts = [jnp.zeros((o, BLOCK), F32)] + parts
            z = jnp.concatenate(parts, 0)
            g[after:, :] = jnp.where(inside, 0.0, rest) - dot3(jnp.where(inside, rest, 0.0), z, NN)


def whiten_kernel(count, core_ref, mine_ref, other_ref, x_ref, white_ref, packed, m, w, g, wd):
    width = x_ref.shape[1]
    half = width // 2
    part = half // 2
    core = core_ref[0]
    scale = 1.0 / count
    packed[pl.ds(pl.multiple_of(core * part, part), part), :] = mine_ref[...] * scale
    packed[pl.ds(pl.multiple_of((1 - core) * part, part), part), :] = other_ref[...] * scale
    tail = packed[:, width:]
    tail_t = tail.T
    low_col, up_col, diag = tail[:, 0:1], tail[:, 1:2], tail[:, 2:3]
    low_row, up_row = tail_t[0:1, :], tail_t[1:2, :]
    m[half:, :half] = packed[:, :half] - low_col * up_row
    right = packed[:, half:width]
    low = right - low_col * low_row
    up = jnp.where(iota((half, half), 0) == iota((half, half), 1), diag, right) - up_col * up_row
    for i in range(0, half, BLOCK):
        keep = iota((BLOCK, BLOCK), 0) >= iota((BLOCK, BLOCK), 1)
        for j in range(0, i + BLOCK, BLOCK):
            block = up[j : j + BLOCK, i : i + BLOCK]
            turned = block.T
            if i == j:
                turned = jnp.where(keep, turned, block)
            m[i : i + BLOCK, j : j + BLOCK] = turned
            block = low[i : i + BLOCK, j : j + BLOCK]
            if i == j:
                block = jnp.where(keep, block, block.T)
            m[half + i : half + i + BLOCK, half + j : half + j + BLOCK] = block
    for b in range(0, width, BLOCK):
        after = b + BLOCK
        g[...] = m[b:after, b:after]
        diag_factor(g, wd)
        wk = wd[...]
        w[b:after, b:after] = wk
        if b:
            w[b:after, :b] = dot3(wk, m[b:after, :b], NN)
        if after < width:
            lk = dot3(m[after:, b:after], wk, NT)
            m[after:, b:after] = jnp.zeros((width - after, BLOCK), F32)
            m[after:, :after] = m[after:, :after] - dot3(lk, w[b:after, :after], NN)
            m[after:, after:] = m[after:, after:] - dot3(lk, lk, NT)
    mean = jnp.concatenate([up_row, low_row], 1)
    centred = x_ref[...] - mean
    step = 256
    for j in range(0, width, step):
        if j + step < width:
            w[j : j + BLOCK, j + BLOCK : j + step] = jnp.zeros((BLOCK, step - BLOCK), F32)
        else:
            w[j : j + BLOCK, j + BLOCK :] = jnp.zeros((BLOCK, width - j - BLOCK), F32)
        white_ref[:, j : j + step] = dot3(
            centred[:, : j + step], w[j : j + step, : j + step], NT
        ).astype(BF16)


def whiten(count, core, mine, other, x):
    width = x.shape[1]
    half = width // 2
    vmem = pl.BlockSpec(memory_space=pltpu.VMEM)
    return pl.pallas_call(
        functools.partial(whiten_kernel, count),
        out_shape=jax.ShapeDtypeStruct(x.shape, BF16),
        in_specs=[pl.BlockSpec(memory_space=pltpu.SMEM), vmem, vmem, vmem],
        out_specs=vmem,
        scratch_shapes=[
            pltpu.VMEM((half, width + EXTRA), F32),
            pltpu.VMEM((width, width), F32),
            pltpu.VMEM((width, width), F32),
            pltpu.VMEM((BLOCK, BLOCK), F32),
            pltpu.VMEM((BLOCK, BLOCK), F32),
        ],
        compiler_params=pltpu.CompilerParams(vmem_limit_bytes=VMEM),
        name="whiten",
    )(core, mine, other, x)


def terms_kernel(rows, row_ref, q_ref, *refs):
    key_refs, out_ref, keys, numer = refs[:-3], refs[-3], refs[-2], refs[-1]
    queries, width = q_ref.shape
    rate = SHARPNESS / width * math.log2(math.e)
    q = q_ref[...]
    qf = q.astype(F32)
    q_term = 2.0 * SHARPNESS * math.log2(math.e) - rate * jnp.sum(qf * qf, axis=1, keepdims=True)
    total = jnp.zeros((queries, 1), F32)
    chunk = keys.shape[0]
    place = 0
    done = 0
    total_rows = sum(ref.shape[0] for ref in key_refs)
    for ref in key_refs:
        size = ref.shape[0]
        keys[place : place + size, :] = ref[...]
        place += size
        if place < chunk and done + place < total_rows:
            continue
        k = keys[:place, :]
        kf = k.astype(F32)
        k_sq = jnp.sum(kf * kf, axis=1, keepdims=True)
        k_row = jnp.concatenate(
            [jnp.broadcast_to(k_sq[j : j + 128], (128, 128)).T[0:1, :] for j in range(0, place, 128)], 1
        )
        kern = jnp.exp2(q_term - rate * k_row + (2.0 * rate) * mul(q, k, NT))
        if done == 0:
            own = (iota(kern.shape, 0) - row_ref[0] * rows == iota(kern.shape, 1)) & (
                iota(kern.shape, 1) < rows
            )
            kern = jnp.where(own, 0.0, kern)
        total = total + jnp.sum(kern, axis=1, keepdims=True)
        term = mul(kern.astype(BF16), k, NN)
        if done == 0:
            numer[...] = term
        else:
            numer[...] += term
        done += place
        place = 0
    out_ref[:, :width] = numer[...].astype(BF16)
    hi, lo = split(total)
    lane = iota((queries, EXTRA), 1)
    wide = jnp.where(lane == 0, hi.astype(F32), jnp.where(lane == 1, lo.astype(F32), 0.0))
    out_ref[:, width:] = wide.astype(BF16)


def terms(row, rows, q, key_list, chunk):
    queries, width = q.shape
    vmem = pl.BlockSpec(memory_space=pltpu.VMEM)
    return pl.pallas_call(
        functools.partial(terms_kernel, rows),
        out_shape=jax.ShapeDtypeStruct((queries, width + EXTRA), BF16),
        in_specs=[pl.BlockSpec(memory_space=pltpu.SMEM)] + [vmem] * (1 + len(key_list)),
        out_specs=vmem,
        scratch_shapes=[pltpu.VMEM((chunk, width), BF16), pltpu.VMEM((queries, width), F32)],
        compiler_params=pltpu.CompilerParams(vmem_limit_bytes=VMEM),
        name="terms",
    )(row, q, *key_list)


def shift(sizes, dx=0, dz=0, dc=0):
    rows, his, zs = sizes
    pairs = []
    for r in range(rows):
        for h in range(his):
            for z in range(zs):
                for c in range(2):
                    src = ((r * his + h) * zs + z) * 2 + c
                    dst = ((r * his + (h + dx) % his) * zs + (z + dz) % zs) * 2 + (c ^ dc)
                    pairs.append((src, dst))
    return pairs


def shards(embeddings):
    rows, width = embeddings.shape
    row_count = lax.axis_size("row")
    col_count = lax.axis_size("col")
    count = rows * row_count * col_count
    row_pos = lax.axis_index("row")
    core = (lax.axis_index("col") % 2).astype(jnp.int32)[None]
    row = row_pos.astype(jnp.int32)[None]
    his, zs = 2, col_count // 4
    sizes = (row_count, his, zs)
    half = col_count // 2
    groups = [[2 * i + c for i in range(half)] for c in range(2)]
    send = functools.partial(lax.ppermute, axis_name=AXES)
    to_core = shift(sizes, dc=1)

    keep, give = moments(core, embeddings)
    mine = keep + send(give, perm=to_core)
    wide = mine.shape[1]
    mine = lax.all_to_all(mine.reshape(row_count, -1, wide), "row", 0, 0).sum(0)
    mine = lax.all_to_all(
        mine.reshape(half, -1, wide), "col", 0, 0, axis_index_groups=groups
    ).sum(0)
    mine = lax.all_to_all(
        jnp.broadcast_to(mine[None], (half,) + mine.shape), "col", 0, 0, axis_index_groups=groups
    ).reshape(-1, wide)
    mine = lax.all_to_all(
        jnp.broadcast_to(mine[None], (row_count,) + mine.shape), "row", 0, 0
    ).reshape(-1, wide)
    other = send(mine, perm=to_core)
    white = whiten(count, core, mine, other, embeddings)

    queries = lax.all_to_all(
        jnp.broadcast_to(white[None], (row_count, rows, width)), "row", 0, 0
    ).reshape(row_count * rows, width)
    far = send(white, perm=shift(sizes, dx=1))
    pair = jnp.concatenate([white, far], 0)
    held = [pair]
    right = left = pair
    up, down = shift(sizes, dz=1), shift(sizes, dz=-1)
    for _ in range((zs - 1) // 2):
        right = send(right, perm=up)
        left = send(left, perm=down)
        held += [right, left]
    if zs % 2 == 0:
        held += [send(right[:rows], perm=up), send(left[rows:], perm=down)]
    held += [send(block, perm=to_core) for block in held]
    partial = terms(row, rows, queries, held, 768)
    parts = lax.all_to_all(partial.reshape(row_count, rows, -1), "row", 0, 0)
    sums = jnp.sum(parts.astype(F32), axis=0)
    total = sums[:, width] + sums[:, width + 1]
    smoothed = sums[:, :width] / total[:, None]
    log_density = jnp.log(total / (count - 1))
    return (smoothed, log_density)


def solution(mesh):
    in_specs = (P(("col", "row"), None),)
    out_specs = (P(("col", "row"), None), P(("col", "row")))
    return jax.shard_map(shards, mesh=mesh, in_specs=in_specs, out_specs=out_specs, check_vma=False)
```

time: 844 us -> 239 us (0.28)
  waiting for transfers between devices: 354 us -> 36.6 us
  other arithmetic: 273 us -> 4.26 us
  Pallas kernels: 0 us -> 61.4 us
  matrix products: 55.8 us -> 0 us
  starting transfers between devices: 0.16 us -> 34 us
  local copies, waits for them, and re-layouts: 34.8 us -> 4.5 us
  between operations: 19.9 us -> 1.3 us
    another operation x33 -> x0, other arithmetic: 255 us -> none  [the longest x30 172 us: shards(): chol = jnp.linalg.cholesky(cov)]
    psum x1 -> x0, waiting for transfers between devices: 190 us -> none  [shards(): first_all, second_all = lax.psum((first, second), ('row', 'col'))]
    all_gather x2 -> x0, waiting for transfers between devices: 142 us -> none  [the longest x1 98.4 us: shards(): piece = lax.all_gather(white, 'col', axis=0, tiled=True)]
    all_to_all x0 -> x5, blocking collectives: none -> 93.6 us  [the longest x1 27.7 us: shards(): parts = lax.all_to_all(partial.reshape(row_count, rows, -1), 'row', 0, 0)]
    psum x1 -> x0, blocking collectives: 81.5 us -> none  [shards(): first_all, second_all = lax.psum((first, second), ('row', 'col'))]
    pallas_call x0 -> x3, Pallas kernels: none -> 61.4 us  [the longest x1 40.4 us: whiten(): pl.pallas_call(functools.partial(whiten_kernel, count), out_shape=jax.Sha...]
    ppermute x0 -> x20, waiting for transfers between devices: none -> 36.6 us  [the longest x3 10.4 us: shards(): right = send(right, perm=up)]
    another operation x29 -> x0, matrix products: 34.7 us -> none  [the longest x14 23.5 us: shards(): chol = jnp.linalg.cholesky(cov)]
  transfers between devices with their start and end apart: 4 -> 21, of which waited for: 4 -> 10; matrix products, arithmetic and copies ran while one was open for 0% -> 1% of each run, Pallas kernels for 0% -> 0%
where the time goes in v1:
time: 239 us; the launch traced here: 236 us
  blocking collectives  93.6 us (39%)
  Pallas kernels  61.4 us (26%)
  waiting for transfers between devices  36.6 us (15%)
  starting transfers between devices  34 us (14%)
  local copies, waits for them, and re-layouts  4.5 us (2%)
  other arithmetic  4.26 us (2%)
    pallas_call x1, Pallas kernels, whiten(): pl.pallas_call(functools.partial(whiten_kernel, count), out_shape=jax.Sha...  40.4 us
    all_to_all x1, blocking collectives, shards(): parts = lax.all_to_all(partial.reshape(row_count, rows, -1), 'row', 0, 0)  27.7 us
    all_to_all x1, blocking collectives, shards(): mine = lax.all_to_all(mine.reshape(row_count, -1, wide), 'row', 0, 0).sum(0)  19.5 us
    all_to_all x1, blocking collectives, shards(): lax.all_to_all(mine.reshape(half, -1, wide), 'col', 0, 0, axis_index_grou...  19.3 us
    pallas_call x1, Pallas kernels, terms(): pl.pallas_call(functools.partial(terms_kernel, rows), out_shape=jax.Shape...  16.8 us
    all_to_all x1, blocking collectives, shards(): lax.all_to_all(jnp.broadcast_to(mine[None], (row_count,) + mine.shape), '...  15.1 us
    all_to_all x1, blocking collectives, shards(): lax.all_to_all(jnp.broadcast_to(mine[None], (half,) + mine.shape), 'col',...  12.1 us
    ppermute x9, starting transfers between devices, shards(): held += [send(block, perm=to_core) for block in held]  10.7 us
  transfers between devices with their start and end apart: 21, of which 10 were waited for; matrix products, arithmetic and copies ran while one was open for 1% of the time, Pallas kernels for 0%

profile of v1, /device:TPU:1, one launch (start us, length us, event | category | flops | bytes accessed | tf_op | source)
XLA Modules:
  0.0 235.6 jit_solution(5131322876447361973)
XLA Ops:
  0.6 4.2 %moments.1 = (f32[256,1152]{1,0:T(8,128)}, f32[256,1152]{1,0:T(8,128)}) custom-call(s32[1]{0:T(128)} %bitcast.1.core_ref, f32[96,1024]{1,0:T(8,128)} %x_ref.3), custom_call_target="tpu_custom_call" | custom-call | tf_op jit(solution)/shard_map/moments/pallas_call | solution.py:76
  4.8 3.2 %collective-permute-start = (f32[256,1152]{1,0:T(8,128)}, f32[256,1152]{1,0:T(8,128)S(1)}, u32[]{:S(2)}, u32[]{:S(2)}) collective-permute-start(f32[256,1152]{1,0:T(8,128)} %get-tuple-element.5), channel_id=1, source_target_pairs={{0,1},{1,0},{2,3},{3,2},{4,5},{5,4},{6,7},{7,6},{8,9},{9,8},{10,11... | collective-permute-start | bytes 3538952 | tf_op jit(solution)/shard_map/ppermute | solution.py:285
  8.1 2.7 %collective-permute-done = f32[256,1152]{1,0:T(8,128)S(1)} collective-permute-done((f32[256,1152]{1,0:T(8,128)}, f32[256,1152]{1,0:T(8,128)S(1)}, u32[]{:S(2)}, u32[]{:S(2)}) %collective-permute-start) | collective-permute-done | bytes 1179680 | tf_op jit(solution)/shard_map/ppermute | solution.py:285
  10.8 1.4 add.13
  12.2 19.5 %all_to_all.30 = f32[8,32,1152]{2,1,0:T(8,128)S(1)} all-to-all(f32[8,32,1152]{2,1,0:T(8,128)S(1)} %bitcast.10), channel_id=1, replica_groups=mesh['row'=8,'col'=32] {'row'}, dimensions={0} | all-to-all | bytes 2359296 | tf_op jit(solution)/shard_map/all_to_all | solution.py:287
  31.6 0.1 reduce_sum.27
  31.7 0.1 reshape.27
  31.8 19.3 %all_to_all.31 = f32[16,2,1152]{2,1,0:T(2,128)S(1)} all-to-all(f32[16,2,1152]{2,1,0:T(2,128)S(1)} %reshape.27), channel_id=1, replica_groups={{0,2,4,6,8,10,12,14,16,18,20,22,24,26,28,30},{1,3,5,7,9,11,13,15,17,19,..., dimensions={0} | all-to-all | bytes 294912 | tf_op jit(solution)/shard_map/all_to_all | solution.py:288
  51.1 0.1 reduce_sum.28
  51.2 12.1 %all_to_all.32 = f32[16,2,1152]{2,1,0:T(2,128)S(1)} all-to-all(f32[16,2,1152]{2,1,0:T(2,128)S(1)} %broadcast_in_dim.28), channel_id=1, replica_groups={{0,2,4,6,8,10,12,14,16,18,20,22,24,26,28,30},{1,3,5,7,9,11,13,15,17,19,..., dimensions={0} | all-to-all | bytes 294912 | tf_op jit(solution)/shard_map/all_to_all | solution.py:291
  63.3 0.1 broadcast_in_dim.29
  63.4 0.1 broadcast_in_dim.30
  63.4 15.1 %all_to_all.33 = f32[8,32,1152]{2,1,0:T(8,128)S(1)} all-to-all(f32[8,32,1152]{2,1,0:T(8,128)S(1)} %broadcast_in_dim.30), channel_id=1, replica_groups=mesh['row'=8,'col'=32] {'row'}, dimensions={0} | all-to-all | bytes 2359296 | tf_op jit(solution)/shard_map/all_to_all | solution.py:294
  78.5 5.9 %collective-permute-start.1 = (f32[256,1152]{1,0:T(8,128)S(1)}, f32[256,1152]{1,0:T(8,128)S(1)}, u32[]{:S(2)}, u32[]{:S(2)}) collective-permute-start(f32[256,1152]{1,0:T(8,128)S(1)} %bitcast.8), channel_id=1, source_target_pairs={{0,1},{1,0},{2,3},{3,2},{4,5},{5,4},{6,7},{7,6},{8,9},{9,8},{10,11... | collective-permute-start | bytes 3538952 | tf_op jit(solution)/shard_map/ppermute | solution.py:297
  84.5 2.5 %collective-permute-done.1.other_ref = f32[256,1152]{1,0:T(8,128)S(1)} collective-permute-done((f32[256,1152]{1,0:T(8,128)S(1)}, f32[256,1152]{1,0:T(8,128)S(1)}, u32[]{:S(2)}, u32[]{:S(2)}) %collective-permute-start.1) | collective-permute-done | bytes 1179680 | tf_op jit(solution)/shard_map/ppermute | solution.py:297
  87.0 1.0 copy-done.3
  88.0 40.4 %whiten.1 = bf16[96,1024]{1,0:T(8,128)(2,1)} custom-call(s32[1]{0:T(128)} %bitcast.1.core_ref, f32[256,1152]{1,0:T(8,128)} %bitcast.9, f32[256,1152]{1,0:T(8,128)} %copy-done.3, f32[96,1024]{1,0:T(8,128)} %x_ref.3), custom_call_target="tpu_custom_call" | custom-call | tf_op jit(solution)/shard_map/whiten/pallas_call | solution.py:180
  128.3 1.4 collective-permute-start.2
  129.8 6.4 %collective-permute-done.2 = bf16[96,1024]{1,0:T(8,128)(2,1)S(1)} collective-permute-done((bf16[96,1024]{1,0:T(8,128)(2,1)}, bf16[96,1024]{1,0:T(8,128)(2,1)S(1)}, u32[]{:S(2)}, u32[]{:S(2)}) %collective-permute-start.2) | collective-permute-done | bytes 196640 | tf_op jit(solution)/shard_map/ppermute | solution.py:303
  136.2 1.0 pad_maximum_fusion.refs_0_
  137.1 0.0 copy-start.2
  137.1 1.3 collective-permute-start.4
  138.5 0.2 collective-permute-start.3
  138.7 7.9 %collective-permute-done.4.refs_2_ = bf16[192,1024]{1,0:T(8,128)(2,1)S(1)} collective-permute-done((bf16[192,1024]{1,0:T(8,128)(2,1)S(1)}, bf16[192,1024]{1,0:T(8,128)(2,1)S(1)}, u32[]{:S(2)}, u32[]{:S(2)}) %collective-permute-start.4) | collective-permute-done | bytes 393248 | tf_op jit(solution)/shard_map/ppermute | solution.py:310
  146.6 2.5 %collective-permute-start.6 = (bf16[192,1024]{1,0:T(8,128)(2,1)S(1)}, bf16[192,1024]{1,0:T(8,128)(2,1)}, u32[]{:S(2)}, u32[]{:S(2)}) collective-permute-start(bf16[192,1024]{1,0:T(8,128)(2,1)S(1)} %collective-permute-done.4.refs_2_), channel_id=1, source_target_pairs={{0,14},{1,15},{2,0},{3,1},{4,2},{5,3},{6,4},{7,5},{8,6},{9,7},{10,... | collective-permute-start | bytes 1179656 | tf_op jit(solution)/shard_map/ppermute | solution.py:310
  149.1 2.3 broadcast_in_dim.31
  151.4 3.6 %all-to-all-start.4 = ((bf16[8,96,1024]{2,1,0:T(8,128)(2,1)}), bf16[8,96,1024]{2,1,0:T(8,128)(2,1)S(1)}, u32[]{:S(2)}, u32[]{:S(2)}) async-start(bf16[8,96,1024]{2,1,0:T(8,128)(2,1)} %broadcast_in_dim.31), calls=%async_computation.4 | async-start | bytes 3145728 | tf_op jit(solution)/shard_map/all_to_all | solution.py:300
  155.0 0.0 collective-permute-done.3.refs_1_
  155.0 0.1 collective-permute-start.5
  155.1 0.3 collective-permute-done.6.refs_4_
  155.4 3.5 %collective-permute-start.8 = (bf16[192,1024]{1,0:T(8,128)(2,1)}, bf16[192,1024]{1,0:T(8,128)(2,1)S(1)}, u32[]{:S(2)}, u32[]{:S(2)}) collective-permute-start(bf16[192,1024]{1,0:T(8,128)(2,1)} %collective-permute-done.6.refs_4_), channel_id=1, source_target_pairs={{0,14},{1,15},{2,0},{3,1},{4,2},{5,3},{6,4},{7,5},{8,6},{9,7},{10,... | collective-permute-start | bytes 1179656 | tf_op jit(solution)/shard_map/ppermute | solution.py:310
  158.9 5.7 %collective-permute-done.5.refs_3_ = bf16[192,1024]{1,0:T(8,128)(2,1)} collective-permute-done((bf16[192,1024]{1,0:T(8,128)(2,1)S(1)}, bf16[192,1024]{1,0:T(8,128)(2,1)}, u32[]{:S(2)}, u32[]{:S(2)}) %collective-permute-start.5) | collective-permute-done | bytes 393248 | tf_op jit(solution)/shard_map/ppermute | solution.py:309
  164.6 0.0 collective-permute-start.7
  164.6 3.3 %collective-permute-start.11 = (bf16[192,1024]{1,0:T(8,128)(2,1)S(1)}, bf16[192,1024]{1,0:T(8,128)(2,1)S(1)}, u32[]{:S(2)}, u32[]{:S(2)}) collective-permute-start(bf16[192,1024]{1,0:T(8,128)(2,1)S(1)} %pad_maximum_fusion.refs_0_), channel_id=1, source_target_pairs={{0,1},{1,0},{2,3},{3,2},{4,5},{5,4},{6,7},{7,6},{8,9},{9,8},{10,11... | collective-permute-start | bytes 1179656 | tf_op jit(solution)/shard_map/ppermute | solution.py:314
  167.9 0.1 collective-permute-start.13
  168.0 0.4 collective-permute-start.12
  168.4 0.0 collective-permute-done.8.refs_6_
  168.4 0.1 collective-permute-start.15
  168.6 4.7 %collective-permute-done.7.refs_5_ = bf16[192,1024]{1,0:T(8,128)(2,1)S(1)} collective-permute-done((bf16[192,1024]{1,0:T(8,128)(2,1)}, bf16[192,1024]{1,0:T(8,128)(2,1)S(1)}, u32[]{:S(2)}, u32[]{:S(2)}) %collective-permute-start.7) | collective-permute-done | bytes 393248 | tf_op jit(solution)/shard_map/ppermute | solution.py:309
  173.3 4.2 %collective-permute-start.14 = (bf16[192,1024]{1,0:T(8,128)(2,1)}, bf16[192,1024]{1,0:T(8,128)(2,1)}, u32[]{:S(2)}, u32[]{:S(2)}) collective-permute-start(bf16[192,1024]{1,0:T(8,128)(2,1)} %collective-permute-done.5.refs_3_), channel_id=1, source_target_pairs={{0,1},{1,0},{2,3},{3,2},{4,5},{5,4},{6,7},{7,6},{8,9},{9,8},{10,11... | collective-permute-start | bytes 1179656 | tf_op jit(solution)/shard_map/ppermute | solution.py:314
  177.6 0.0 collective-permute-done.11.refs_9_
  177.6 0.1 collective-permute-start.10
  177.7 0.0 collective-permute-done.13.refs_11_
  177.7 1.4 collective-permute-start.9
  179.1 0.0 collective-permute-done.12.refs_10_
  179.1 0.6 collective-permute-start.17
  179.7 0.0 collective-permute-done.15.refs_13_
  179.7 0.1 collective-permute-start.16
  179.8 0.1 copy-done.10
  179.9 4.4 %collective-permute-done.10.refs_8_ = bf16[96,1024]{1,0:T(8,128)(2,1)} collective-permute-done((bf16[96,1024]{1,0:T(8,128)(2,1)S(1)}, bf16[96,1024]{1,0:T(8,128)(2,1)}, u32[]{:S(2)}, u32[]{:S(2)}) %collective-permute-start.10) | collective-permute-done | bytes 196640 | tf_op jit(solution)/shard_map/ppermute | solution.py:313
  184.3 0.8 collective-permute-start.19
  185.1 0.5 collective-permute-done.9.refs_7_
  185.6 1.0 collective-permute-start.18
  186.6 0.0 all-to-all-done.4
  186.7 0.0 collective-permute-done.19.refs_17_
  186.7 0.0 collective-permute-done.17.refs_15_
  186.7 1.4 collective-permute-done.18.refs_16_
  188.1 0.0 collective-permute-done.16.refs_14_
  188.1 0.8 copy-done.13
  188.9 16.8 %terms.1 = bf16[768,1152]{1,0:T(8,128)(2,1)} custom-call(s32[1]{0:T(128)} %bitcast.row_ref, bf16[768,1024]{1,0:T(8,128)(2,1)} %bitcast.7, bf16[192,1024]{1,0:T(8,128)(2,1)} %copy-done.2, bf16[192,1024]{1,0:T(8,128)(2,1)} %copy-done.7, bf16[192,1024]{1,0:T(8,128)(2,1)} %copy-done.6, bf16[192,1024]{1,0:T(8,128)(2,1)} %collective-permute-done.5.refs_3_, ...), custom_call_target="tpu_custom_call" | custom-call | tf_op jit(solution)/shard_map/terms/pallas_call | solution.py:245
  205.7 27.7 %all_to_all.34 = bf16[8,96,1152]{2,1,0:T(8,128)(2,1)S(1)} all-to-all(bf16[8,96,1152]{2,1,0:T(8,128)(2,1)} %bitcast.6), channel_id=1, replica_groups=mesh['row'=8,'col'=32] {'row'}, dimensions={0} | all-to-all | bytes 3538944 | tf_op jit(solution)/shard_map/all_to_all | solution.py:316
  233.4 0.2 convert_reduce_fusion
  233.6 0.7 log_reduce_fusion
  234.3 0.8 slice_divide_fusion
  (28 shorter events, 0.1 us)
Async XLA Ops:
  4.8 5.9 %collective-permute-start = (f32[256,1152]{1,0:T(8,128)}, f32[256,1152]{1,0:T(8,128)S(1)}, u32[]{:S(2)}, u32[]{:S(2)}) collective-permute-start(f32[256,1152]{1,0:T(8,128)} %get-tuple-element.5), channel_id=1, source_target_pairs={{0,1},{1,0},{2,3},{3,2},{4,5},{5,4},{6,7},{7,6},{8,9},{9,8},{10,11... | collective-permute-start | bytes 3538952 | tf_op jit(solution)/shard_map/ppermute | solution.py:285
  78.5 8.4 %copy-start.1 = (f32[8,32,1152]{2,1,0:T(8,128)}, f32[8,32,1152]{2,1,0:T(8,128)S(1)}, u32[]{:S(2)}) copy-start(f32[8,32,1152]{2,1,0:T(8,128)S(1)} %all_to_all.33) | copy-start | bytes 3538948
  78.5 8.4 %collective-permute-start.1 = (f32[256,1152]{1,0:T(8,128)S(1)}, f32[256,1152]{1,0:T(8,128)S(1)}, u32[]{:S(2)}, u32[]{:S(2)}) collective-permute-start(f32[256,1152]{1,0:T(8,128)S(1)} %bitcast.8), channel_id=1, source_target_pairs={{0,1},{1,0},{2,3},{3,2},{4,5},{5,4},{6,7},{7,6},{8,9},{9,8},{10,11... | collective-permute-start | bytes 3538952 | tf_op jit(solution)/shard_map/ppermute | solution.py:297
  87.0 1.0 copy-start.3
  128.3 7.8 %collective-permute-start.2 = (bf16[96,1024]{1,0:T(8,128)(2,1)}, bf16[96,1024]{1,0:T(8,128)(2,1)S(1)}, u32[]{:S(2)}, u32[]{:S(2)}) collective-permute-start(bf16[96,1024]{1,0:T(8,128)(2,1)} %whiten.1), channel_id=1, source_target_pairs={{0,16},{1,17},{2,18},{3,19},{4,20},{5,21},{6,22},{7,23},{8,24},{9,... | collective-permute-start | bytes 589832 | tf_op jit(solution)/shard_map/ppermute | solution.py:303
  137.1 27.5 %copy-start.2 = (bf16[192,1024]{1,0:T(8,128)(2,1)}, bf16[192,1024]{1,0:T(8,128)(2,1)S(1)}, u32[]{:S(2)}) copy-start(bf16[192,1024]{1,0:T(8,128)(2,1)S(1)} %pad_maximum_fusion.refs_0_) | copy-start | bytes 1179652
  137.1 9.5 %collective-permute-start.4 = (bf16[192,1024]{1,0:T(8,128)(2,1)S(1)}, bf16[192,1024]{1,0:T(8,128)(2,1)S(1)}, u32[]{:S(2)}, u32[]{:S(2)}) collective-permute-start(bf16[192,1024]{1,0:T(8,128)(2,1)S(1)} %pad_maximum_fusion.refs_0_), channel_id=1, source_target_pairs={{0,14},{1,15},{2,0},{3,1},{4,2},{5,3},{6,4},{7,5},{8,6},{9,7},{10,... | collective-permute-start | bytes 1179656 | tf_op jit(solution)/shard_map/ppermute | solution.py:310
  138.5 16.5 %collective-permute-start.3 = (bf16[192,1024]{1,0:T(8,128)(2,1)S(1)}, bf16[192,1024]{1,0:T(8,128)(2,1)S(1)}, u32[]{:S(2)}, u32[]{:S(2)}) collective-permute-start(bf16[192,1024]{1,0:T(8,128)(2,1)S(1)} %pad_maximum_fusion.refs_0_), channel_id=1, source_target_pairs={{0,2},{1,3},{2,4},{3,5},{4,6},{5,7},{6,8},{7,9},{8,10},{9,11},{10,... | collective-permute-start | bytes 1179656 | tf_op jit(solution)/shard_map/ppermute | solution.py:309
  146.6 21.3 %copy-start.6 = (bf16[192,1024]{1,0:T(8,128)(2,1)}, bf16[192,1024]{1,0:T(8,128)(2,1)S(1)}, u32[]{:S(2)}) copy-start(bf16[192,1024]{1,0:T(8,128)(2,1)S(1)} %collective-permute-done.4.refs_2_) | copy-start | bytes 1179652
  146.6 8.8 %collective-permute-start.6 = (bf16[192,1024]{1,0:T(8,128)(2,1)S(1)}, bf16[192,1024]{1,0:T(8,128)(2,1)}, u32[]{:S(2)}, u32[]{:S(2)}) collective-permute-start(bf16[192,1024]{1,0:T(8,128)(2,1)S(1)} %collective-permute-done.4.refs_2_), channel_id=1, source_target_pairs={{0,14},{1,15},{2,0},{3,1},{4,2},{5,3},{6,4},{7,5},{8,6},{9,7},{10,... | collective-permute-start | bytes 1179656 | tf_op jit(solution)/shard_map/ppermute | solution.py:310
  151.4 35.3 %all-to-all-start.4 = ((bf16[8,96,1024]{2,1,0:T(8,128)(2,1)}), bf16[8,96,1024]{2,1,0:T(8,128)(2,1)S(1)}, u32[]{:S(2)}, u32[]{:S(2)}) async-start(bf16[8,96,1024]{2,1,0:T(8,128)(2,1)} %broadcast_in_dim.31), calls=%async_computation.4 | async-start | bytes 3145728 | tf_op jit(solution)/shard_map/all_to_all | solution.py:300
  155.0 33.1 %copy-start.7 = (bf16[192,1024]{1,0:T(8,128)(2,1)}, bf16[192,1024]{1,0:T(8,128)(2,1)S(1)}, u32[]{:S(2)}) copy-start(bf16[192,1024]{1,0:T(8,128)(2,1)S(1)} %collective-permute-done.3.refs_1_) | copy-start | bytes 1179652
  155.0 9.6 %collective-permute-start.5 = (bf16[192,1024]{1,0:T(8,128)(2,1)S(1)}, bf16[192,1024]{1,0:T(8,128)(2,1)}, u32[]{:S(2)}, u32[]{:S(2)}) collective-permute-start(bf16[192,1024]{1,0:T(8,128)(2,1)S(1)} %collective-permute-done.3.refs_1_), channel_id=1, source_target_pairs={{0,2},{1,3},{2,4},{3,5},{4,6},{5,7},{6,8},{7,9},{8,10},{9,11},{10,... | collective-permute-start | bytes 1179656 | tf_op jit(solution)/shard_map/ppermute | solution.py:309
  155.4 13.1 %collective-permute-start.8 = (bf16[192,1024]{1,0:T(8,128)(2,1)}, bf16[192,1024]{1,0:T(8,128)(2,1)S(1)}, u32[]{:S(2)}, u32[]{:S(2)}) collective-permute-start(bf16[192,1024]{1,0:T(8,128)(2,1)} %collective-permute-done.6.refs_4_), channel_id=1, source_target_pairs={{0,14},{1,15},{2,0},{3,1},{4,2},{5,3},{6,4},{7,5},{8,6},{9,7},{10,... | collective-permute-start | bytes 1179656 | tf_op jit(solution)/shard_map/ppermute | solution.py:310
  164.6 8.7 %collective-permute-start.7 = (bf16[192,1024]{1,0:T(8,128)(2,1)}, bf16[192,1024]{1,0:T(8,128)(2,1)S(1)}, u32[]{:S(2)}, u32[]{:S(2)}) collective-permute-start(bf16[192,1024]{1,0:T(8,128)(2,1)} %collective-permute-done.5.refs_3_), channel_id=1, source_target_pairs={{0,2},{1,3},{2,4},{3,5},{4,6},{5,7},{6,8},{7,9},{8,10},{9,11},{10,... | collective-permute-start | bytes 1179656 | tf_op jit(solution)/shard_map/ppermute | solution.py:309
  164.6 13.0 %collective-permute-start.11 = (bf16[192,1024]{1,0:T(8,128)(2,1)S(1)}, bf16[192,1024]{1,0:T(8,128)(2,1)S(1)}, u32[]{:S(2)}, u32[]{:S(2)}) collective-permute-start(bf16[192,1024]{1,0:T(8,128)(2,1)S(1)} %pad_maximum_fusion.refs_0_), channel_id=1, source_target_pairs={{0,1},{1,0},{2,3},{3,2},{4,5},{5,4},{6,7},{7,6},{8,9},{9,8},{10,11... | collective-permute-start | bytes 1179656 | tf_op jit(solution)/shard_map/ppermute | solution.py:314
  167.9 9.8 %collective-permute-start.13 = (bf16[192,1024]{1,0:T(8,128)(2,1)S(1)}, bf16[192,1024]{1,0:T(8,128)(2,1)S(1)}, u32[]{:S(2)}, u32[]{:S(2)}) collective-permute-start(bf16[192,1024]{1,0:T(8,128)(2,1)S(1)} %collective-permute-done.4.refs_2_), channel_id=1, source_target_pairs={{0,1},{1,0},{2,3},{3,2},{4,5},{5,4},{6,7},{7,6},{8,9},{9,8},{10,11... | collective-permute-start | bytes 1179656 | tf_op jit(solution)/shard_map/ppermute | solution.py:314
  168.0 11.1 %collective-permute-start.12 = (bf16[192,1024]{1,0:T(8,128)(2,1)S(1)}, bf16[192,1024]{1,0:T(8,128)(2,1)S(1)}, u32[]{:S(2)}, u32[]{:S(2)}) collective-permute-start(bf16[192,1024]{1,0:T(8,128)(2,1)S(1)} %collective-permute-done.3.refs_1_), channel_id=1, source_target_pairs={{0,1},{1,0},{2,3},{3,2},{4,5},{5,4},{6,7},{7,6},{8,9},{9,8},{10,11... | collective-permute-start | bytes 1179656 | tf_op jit(solution)/shard_map/ppermute | solution.py:314
  168.4 19.6 %copy-start.4 = (bf16[192,1024]{1,0:T(8,128)(2,1)}, bf16[192,1024]{1,0:T(8,128)(2,1)S(1)}, u32[]{:S(2)}) copy-start(bf16[192,1024]{1,0:T(8,128)(2,1)S(1)} %collective-permute-done.8.refs_6_) | copy-start | bytes 1179652
  168.4 11.3 %collective-permute-start.15 = (bf16[192,1024]{1,0:T(8,128)(2,1)}, bf16[192,1024]{1,0:T(8,128)(2,1)S(1)}, u32[]{:S(2)}, u32[]{:S(2)}) collective-permute-start(bf16[192,1024]{1,0:T(8,128)(2,1)} %collective-permute-done.6.refs_4_), channel_id=1, source_target_pairs={{0,1},{1,0},{2,3},{3,2},{4,5},{5,4},{6,7},{7,6},{8,9},{9,8},{10,11... | collective-permute-start | bytes 1179656 | tf_op jit(solution)/shard_map/ppermute | solution.py:314
  173.3 14.8 %copy-start.5 = (bf16[192,1024]{1,0:T(8,128)(2,1)}, bf16[192,1024]{1,0:T(8,128)(2,1)S(1)}, u32[]{:S(2)}) copy-start(bf16[192,1024]{1,0:T(8,128)(2,1)S(1)} %collective-permute-done.7.refs_5_) | copy-start | bytes 1179652
  173.3 13.4 %collective-permute-start.14 = (bf16[192,1024]{1,0:T(8,128)(2,1)}, bf16[192,1024]{1,0:T(8,128)(2,1)}, u32[]{:S(2)}, u32[]{:S(2)}) collective-permute-start(bf16[192,1024]{1,0:T(8,128)(2,1)} %collective-permute-done.5.refs_3_), channel_id=1, source_target_pairs={{0,1},{1,0},{2,3},{3,2},{4,5},{5,4},{6,7},{7,6},{8,9},{9,8},{10,11... | collective-permute-start | bytes 1179656 | tf_op jit(solution)/shard_map/ppermute | solution.py:314
  177.6 2.1 copy-start.8
  177.6 6.7 %collective-permute-start.10 = (bf16[96,1024]{1,0:T(8,128)(2,1)S(1)}, bf16[96,1024]{1,0:T(8,128)(2,1)}, u32[]{:S(2)}, u32[]{:S(2)}) collective-permute-start(bf16[96,1024]{1,0:T(8,128)(2,1)S(1)} %slice.21), channel_id=1, source_target_pairs={{0,14},{1,15},{2,0},{3,1},{4,2},{5,3},{6,4},{7,5},{8,6},{9,7},{10,... | collective-permute-start | bytes 589832 | tf_op jit(solution)/shard_map/ppermute | solution.py:313
  177.7 2.0 copy-start.9
  177.7 7.9 %collective-permute-start.9 = (bf16[96,1024]{1,0:T(8,128)(2,1)S(1)}, bf16[96,1024]{1,0:T(8,128)(2,1)}, u32[]{:S(2)}, u32[]{:S(2)}) collective-permute-start(bf16[96,1024]{1,0:T(8,128)(2,1)S(1)} %slice.20), channel_id=1, source_target_pairs={{0,2},{1,3},{2,4},{3,5},{4,6},{5,7},{6,8},{7,9},{8,10},{9,11},{10,... | collective-permute-start | bytes 589832 | tf_op jit(solution)/shard_map/ppermute | solution.py:313
  179.1 0.8 copy-start.10
  179.1 7.5 %collective-permute-start.17 = (bf16[192,1024]{1,0:T(8,128)(2,1)S(1)}, bf16[192,1024]{1,0:T(8,128)(2,1)S(1)}, u32[]{:S(2)}, u32[]{:S(2)}) collective-permute-start(bf16[192,1024]{1,0:T(8,128)(2,1)S(1)} %collective-permute-done.8.refs_6_), channel_id=1, source_target_pairs={{0,1},{1,0},{2,3},{3,2},{4,5},{5,4},{6,7},{7,6},{8,9},{9,8},{10,11... | collective-permute-start | bytes 1179656 | tf_op jit(solution)/shard_map/ppermute | solution.py:314
  179.7 4.6 %copy-start.11 = (bf16[192,1024]{1,0:T(8,128)(2,1)}, bf16[192,1024]{1,0:T(8,128)(2,1)S(1)}, u32[]{:S(2)}) copy-start(bf16[192,1024]{1,0:T(8,128)(2,1)S(1)} %collective-permute-done.15.refs_13_) | copy-start | bytes 1179652
  179.7 8.3 %collective-permute-start.16 = (bf16[192,1024]{1,0:T(8,128)(2,1)S(1)}, bf16[192,1024]{1,0:T(8,128)(2,1)S(1)}, u32[]{:S(2)}, u32[]{:S(2)}) collective-permute-start(bf16[192,1024]{1,0:T(8,128)(2,1)S(1)} %collective-permute-done.7.refs_5_), channel_id=1, source_target_pairs={{0,1},{1,0},{2,3},{3,2},{4,5},{5,4},{6,7},{7,6},{8,9},{9,8},{10,11... | collective-permute-start | bytes 1179656 | tf_op jit(solution)/shard_map/ppermute | solution.py:314
  184.3 2.4 collective-permute-start.19
  185.6 2.4 %collective-permute-start.18 = (bf16[96,1024]{1,0:T(8,128)(2,1)}, bf16[96,1024]{1,0:T(8,128)(2,1)}, u32[]{:S(2)}, u32[]{:S(2)}) collective-permute-start(bf16[96,1024]{1,0:T(8,128)(2,1)} %collective-permute-done.9.refs_7_), channel_id=1, source_target_pairs={{0,1},{1,0},{2,3},{3,2},{4,5},{5,4},{6,7},{7,6},{8,9},{9,8},{10,11... | collective-permute-start | bytes 589832 | tf_op jit(solution)/shard_map/ppermute | solution.py:314
  186.7 1.4 copy-start
  186.7 1.4 copy-start.12
  188.1 0.8 copy-start.13

commit v2 on v1

v2 whole, which is shorter than its diff:
```python
import functools
import math
import jax
import jax.numpy as jnp
from jax import lax
from jax.experimental import pallas as pl
from jax.experimental.pallas import tpu as pltpu
from jax.sharding import PartitionSpec as P

SHARPNESS = 24.0
BLOCK = 128
PANEL = 16
EXTRA = 128
VMEM = 56 * 2**20
TERMS_VMEM = 40 * 2**20
AXES = ("row", "col")
NN = ((1,), (0,))
NT = ((1,), (1,))
BF16 = jnp.bfloat16
F32 = jnp.float32


def split(a):
    hi = a.astype(BF16)
    return hi, (a - hi.astype(F32)).astype(BF16)


def mul(a, b, dims):
    return lax.dot_general(a, b, (dims, ((), ())), preferred_element_type=F32)


def dot3(a, b, dims):
    a_hi, a_lo = split(a)
    b_hi, b_lo = split(b)
    return mul(a_hi, b_hi, dims) + (mul(a_hi, b_lo, dims) + mul(a_lo, b_hi, dims))


def iota(shape, dim):
    return lax.broadcasted_iota(jnp.int32, shape, dim)


def moments_kernel(core_ref, x_ref, y_ref, out_ref, turned_hi, turned_lo):
    rows, width = x_ref.shape
    half = width // 2
    part = half // 2
    pad = jnp.zeros((BLOCK - rows, width), F32)
    x = jnp.concatenate([x_ref[...], pad, y_ref[...], pad], 0)
    hi, lo = split(x)
    for c in range(0, width, BLOCK):
        t_hi, t_lo = split(x[:, c : c + BLOCK].T)
        turned_hi[c : c + BLOCK, :] = t_hi
        turned_lo[c : c + BLOCK, :] = t_lo
    core = core_ref[0]

    def product(start, right_hi, right_lo):
        place = pl.ds(pl.multiple_of(start + core * part, part), part)
        left_hi, left_lo = turned_hi[place, :], turned_lo[place, :]
        small = mul(left_lo, right_lo, NN)
        small = small + (mul(left_hi, right_lo, NN) + mul(left_lo, right_hi, NN))
        return mul(left_hi, right_hi, NN) + small

    low = product(half, hi, lo)
    up = product(0, hi[:, :half], lo[:, :half])
    ones = jnp.where(iota((2 * BLOCK, EXTRA), 1) == 0, 1.0, 0.0).astype(BF16)
    none = jnp.zeros((2 * BLOCK, EXTRA), BF16)
    low_sum = product(half, ones, none)
    up_sum = product(0, ones, none)
    r, c = iota((part, half), 0) + core * part, iota((part, half), 1)
    diag = jnp.sum(jnp.where(r == c, up, 0.0), axis=1, keepdims=True)
    lane = iota((part, EXTRA), 1)
    out_ref[:, :half] = low[:, :half]
    out_ref[:, half:width] = jnp.where(r >= c, low[:, half:], up)
    out_ref[:, width:] = jnp.where(
        lane == 0,
        low_sum,
        jnp.where(lane == 1, up_sum[:, :1], jnp.where(lane == 2, diag, 0.0)),
    )


def moments(core, x, y):
    width = x.shape[1]
    vmem = pl.BlockSpec(memory_space=pltpu.VMEM)
    return pl.pallas_call(
        moments_kernel,
        out_shape=jax.ShapeDtypeStruct((width // 4, width + EXTRA), F32),
        in_specs=[pl.BlockSpec(memory_space=pltpu.SMEM), vmem, vmem],
        out_specs=vmem,
        scratch_shapes=[pltpu.VMEM((width, 2 * BLOCK), BF16)] * 2,
        compiler_params=pltpu.CompilerParams(vmem_limit_bytes=VMEM),
        name="moments",
    )(core, x, y)


def row_of(v, s):
    return jnp.broadcast_to(v[s : s + 1, :], (PANEL, BLOCK))


def columns_of(v, o):
    return [jnp.broadcast_to(v[:, o + s : o + s + 1], (PANEL, BLOCK)) for s in range(PANEL)]


def diag_factor(g, w):
    lane = iota((PANEL, BLOCK), 1)
    sub = iota((PANEL, BLOCK), 0)
    r = g[:PANEL, :]
    for o in range(0, BLOCK, PANEL):
        after = o + PANEL
        if after < BLOCK:
            ahead = g[after : after + PANEL, :]
            factors = columns_of(ahead, o)
        cols = columns_of(r, o)
        inside = (lane >= o) & (lane < after)
        e = jnp.where(inside, jnp.where(lane - o == sub, 1.0, 0.0), r)
        y = jnp.zeros_like(r)
        for s in range(PANEL):
            d = row_of(cols[s], s)
            inv = 1.0 / d
            pivot = row_of(e, s)
            y = jnp.where(sub == s, pivot * lax.rsqrt(d), y)
            m = jnp.where(sub != s, cols[s] * inv, 1.0 - inv)
            e = e - m * pivot
            for t in range(s + 1, PANEL):
                cols[t] = cols[t] - m * row_of(cols[t], s)
        w[o:after, :] = jnp.where(lane <= sub + o, y, 0.0)
        if after < BLOCK:
            sums = [jnp.zeros_like(r)] * 4
            for s in range(PANEL):
                sums[s % 4] = sums[s % 4] + factors[s] * row_of(e, s)
            r = jnp.where(inside, 0.0, ahead) - ((sums[0] + sums[1]) + (sums[2] + sums[3]))
        far = after + PANEL
        if far < BLOCK:
            rest = g[far:, :]
            place = iota(rest.shape, 1)
            inside = (place >= o) & (place < after)
            parts = [e, jnp.zeros((BLOCK - after, BLOCK), F32)]
            if o:
                parts = [jnp.zeros((o, BLOCK), F32)] + parts
            z = jnp.concatenate(parts, 0)
            g[far:, :] = jnp.where(inside, 0.0, rest) - dot3(jnp.where(inside, rest, 0.0), z, NN)


def whiten_kernel(
    count, core_ref, mine_ref, other_ref, x_ref, white_ref, packed, m, w, g, wd
):
    width = x_ref.shape[1]
    half = width // 2
    part = half // 2
    core = core_ref[0]
    scale = 1.0 / count
    packed[pl.ds(pl.multiple_of(core * part, part), part), :] = mine_ref[...] * scale
    packed[pl.ds(pl.multiple_of((1 - core) * part, part), part), :] = other_ref[...] * scale
    tail = packed[:, width:]
    tail_t = tail.T
    low_col, up_col, diag = tail[:, 0:1], tail[:, 1:2], tail[:, 2:3]
    low_row, up_row = tail_t[0:1, :], tail_t[1:2, :]
    m[half:, :half] = packed[:, :half] - low_col * up_row
    right = packed[:, half:width]
    low = right - low_col * low_row
    up = jnp.where(iota((half, half), 0) == iota((half, half), 1), diag, right) - up_col * up_row
    for i in range(0, half, BLOCK):
        keep = iota((BLOCK, BLOCK), 0) >= iota((BLOCK, BLOCK), 1)
        for j in range(0, i + BLOCK, BLOCK):
            block = up[j : j + BLOCK, i : i + BLOCK]
            turned = block.T
            if i == j:
                turned = jnp.where(keep, turned, block)
            m[i : i + BLOCK, j : j + BLOCK] = turned
            block = low[i : i + BLOCK, j : j + BLOCK]
            if i == j:
                block = jnp.where(keep, block, block.T)
            m[half + i : half + i + BLOCK, half + j : half + j + BLOCK] = block
    for b in range(0, width, BLOCK):
        after = b + BLOCK
        g[...] = m[b:after, b:after]
        diag_factor(g, wd)
        wk = wd[...]
        w[b:after, b:after] = wk
        if b:
            w[b:after, :b] = dot3(wk, m[b:after, :b], NN)
        if after < width:
            lk = dot3(m[after:, b:after], wk, NT)
            m[after:, b:after] = jnp.zeros((width - after, BLOCK), F32)
            m[after:, :after] = m[after:, :after] - dot3(lk, w[b:after, :after], NN)
            m[after:, after:] = m[after:, after:] - dot3(lk, lk, NT)
    mean = jnp.concatenate([up_row, low_row], 1)
    centred = x_ref[...] - mean
    step = 256
    for j in range(0, width, step):
        if j + step < width:
            w[j : j + BLOCK, j + BLOCK : j + step] = jnp.zeros((BLOCK, step - BLOCK), F32)
        else:
            w[j : j + BLOCK, j + BLOCK :] = jnp.zeros((BLOCK, width - j - BLOCK), F32)
        white_ref[:, j : j + step] = dot3(
            centred[:, : j + step], w[j : j + step, : j + step], NT
        ).astype(BF16)


def whiten(count, core, mine, other, x):
    width = x.shape[1]
    half = width // 2
    vmem = pl.BlockSpec(memory_space=pltpu.VMEM)
    return pl.pallas_call(
        functools.partial(whiten_kernel, count),
        out_shape=jax.ShapeDtypeStruct(x.shape, BF16),
        in_specs=[pl.BlockSpec(memory_space=pltpu.SMEM), vmem, vmem, vmem],
        out_specs=vmem,
        scratch_shapes=[
            pltpu.VMEM((half, width + EXTRA), F32),
            pltpu.VMEM((width, width), F32),
            pltpu.VMEM((width, width), F32),
            pltpu.VMEM((BLOCK, BLOCK), F32),
            pltpu.VMEM((BLOCK, BLOCK), F32),
        ],
        compiler_params=pltpu.CompilerParams(vmem_limit_bytes=VMEM),
        name="whiten",
    )(core, mine, other, x)


def terms_kernel(rows, first, last, n_queries, n_keys, *refs):
    q_refs, refs = refs[:n_queries], refs[n_queries:]
    key_refs, refs = refs[:n_keys], refs[n_keys:]
    if first:
        numer_in = stat_in = None
    else:
        numer_in, stat_in, refs = refs[0], refs[1], refs[2:]
    if last:
        outs, refs = refs[:-1], refs[-1:]
        keys = refs[0]
    else:
        numer_out, stat_out, keys = refs
    q = jnp.concatenate([ref[...] for ref in q_refs], 0)
    queries, width = q.shape
    rate = SHARPNESS / width * math.log2(math.e)
    if first:
        qf = q.astype(F32)
        q_term = 2.0 * SHARPNESS * math.log2(math.e) - rate * jnp.sum(qf * qf, axis=1, keepdims=True)
        total = jnp.zeros((queries, 1), F32)
    else:
        q_term, total = stat_in[:, 0:1], stat_in[:, 1:2]
    place = 0
    for ref in key_refs:
        size = ref.shape[0]
        keys[place : place + size, :] = ref[...]
        place += size
    k = keys[...]
    kf = k.astype(F32)
    k_sq = jnp.sum(kf * kf, axis=1, keepdims=True)
    k_row = jnp.concatenate(
        [jnp.broadcast_to(k_sq[j : j + 128], (128, 128)).T[0:1, :] for j in range(0, place, 128)], 1
    )
    step = 384
    terms = []
    for j in range(0, place, step):
        kern = jnp.exp2(
            q_term - rate * k_row[:, j : j + step] + (2.0 * rate) * mul(q, k[j : j + step], NT)
        )
        if first and j == 0:
            own = (iota(kern.shape, 0) == iota(kern.shape, 1)) & (
                iota(kern.shape, 1) < rows
            )
            kern = jnp.where(own, 0.0, kern)
        total = total + jnp.sum(kern, axis=1, keepdims=True)
        terms.append(kern.astype(BF16))
    numer = mul(jnp.concatenate(terms, 1), k, NN)
    if not first:
        numer = numer_in[...] + numer
    if not last:
        numer_out[...] = numer
        lane = iota((queries, EXTRA), 1)
        stat_out[...] = jnp.where(lane == 0, q_term, total)
        return
    lane = iota((queries, EXTRA), 1)
    hi, lo = split(total)
    wide = jnp.where(lane == 0, hi.astype(F32), jnp.where(lane == 1, lo.astype(F32), 0.0))
    for i, out in enumerate(outs):
        out[:, :width] = numer[i * rows : (i + 1) * rows].astype(BF16)
        out[:, width:] = wide[i * rows : (i + 1) * rows].astype(BF16)


def moves(row_count):
    return [(dy, dx) for dy in range(row_count // 2) for dx in range(2)]


def turn(row, dy, dx, row_count):
    y, x = row // 2, row % 2
    return (y + dy) % (row_count // 2) * 2 + (x + dx) % 2


def terms(rows, query_list, key_list, state, last):
    width = query_list[0].shape[1]
    queries = sum(q.shape[0] for q in query_list)
    n_keys = len(key_list)
    keys = sum(k.shape[0] for k in key_list)
    vmem = pl.BlockSpec(memory_space=pltpu.VMEM)
    if last:
        out_shape = (jax.ShapeDtypeStruct((rows, width + EXTRA), BF16),) * (queries // rows)
    else:
        out_shape = (
            jax.ShapeDtypeStruct((queries, width), F32),
            jax.ShapeDtypeStruct((queries, EXTRA), F32),
        )
    return pl.pallas_call(
        functools.partial(terms_kernel, rows, not state, last, len(query_list), n_keys),
        out_shape=out_shape,
        in_specs=[vmem] * (len(query_list) + n_keys + len(state)),
        out_specs=(vmem,) * len(out_shape),
        scratch_shapes=[pltpu.VMEM((keys, width), BF16)],
        compiler_params=pltpu.CompilerParams(vmem_limit_bytes=TERMS_VMEM),
        cost_estimate=pl.CostEstimate(
            flops=4 * queries * keys * width,
            bytes_accessed=8 * queries * width,
            transcendentals=queries * keys,
        ),
        name="terms",
    )(*query_list, *key_list, *state)


def shift(sizes, dx=0, dz=0, dc=0):
    rows, his, zs = sizes
    pairs = []
    for r in range(rows):
        for h in range(his):
            for z in range(zs):
                for c in range(2):
                    src = ((r * his + h) * zs + z) * 2 + c
                    dst = ((r * his + (h + dx) % his) * zs + (z + dz) % zs) * 2 + (c ^ dc)
                    pairs.append((src, dst))
    return pairs


def shards(embeddings):
    rows, width = embeddings.shape
    row_count = lax.axis_size("row")
    col_count = lax.axis_size("col")
    count = rows * row_count * col_count
    core = (lax.axis_index("col") % 2).astype(jnp.int32)[None]
    his, zs = 2, col_count // 4
    sizes = (row_count, his, zs)
    half = col_count // 2
    groups = [[2 * i + c for i in range(half)] for c in range(2)]
    send = functools.partial(lax.ppermute, axis_name=AXES)
    to_core = shift(sizes, dc=1)

    mine = moments(core, embeddings, send(embeddings, perm=to_core))
    wide = mine.shape[1]
    mine = lax.all_to_all(mine.reshape(row_count, -1, wide), "row", 0, 0).sum(0)
    mine = lax.all_to_all(
        mine.reshape(half, -1, wide), "col", 0, 0, axis_index_groups=groups
    ).sum(0)
    mine = lax.all_to_all(
        jnp.broadcast_to(mine[None], (half,) + mine.shape), "col", 0, 0, axis_index_groups=groups
    ).reshape(-1, wide)
    mine = lax.all_to_all(
        jnp.broadcast_to(mine[None], (row_count,) + mine.shape), "row", 0, 0
    ).reshape(-1, wide)
    other = send(mine, perm=to_core)
    white = whiten(count, core, mine, other, embeddings)

    def row_shift(dy, dx, back):
        pairs = []
        for r in range(row_count):
            for c in range(col_count):
                ends = (r * col_count + c, turn(r, dy, dx, row_count) * col_count + c)
                pairs.append(ends[::-1] if back else ends)
        return pairs

    far = send(white, perm=shift(sizes, dx=1))
    near = send(white, perm=row_shift(0, 1, True))
    pair = jnp.concatenate([white, far], 0)
    asked = jnp.concatenate([white, near], 0)
    queries = [asked] + [
        send(asked, perm=row_shift(dy, 0, True)) for dy in range(1, row_count // 2)
    ]
    right = left = pair
    up, down = shift(sizes, dz=1), shift(sizes, dz=-1)
    arrived = []
    for _ in range((zs - 1) // 2):
        right = send(right, perm=up)
        left = send(left, perm=down)
        arrived.append([right, left])
    if zs % 2 == 0:
        arrived[-1] += [send(right[:rows], perm=up), send(left[rows:], perm=down)]
    arrived[0] = [pair] + arrived[0]
    state = ()
    for i, blocks in enumerate(arrived):
        blocks = blocks + [send(block, perm=to_core) for block in blocks]
        state = terms(rows, queries, blocks, state, i == len(arrived) - 1)
    sums = state[0].astype(F32)
    for (dy, dx), part in list(zip(moves(row_count), state))[1:]:
        sums = sums + send(part, perm=row_shift(dy, dx, False)).astype(F32)
    total = sums[:, width] + sums[:, width + 1]
    smoothed = sums[:, :width] / total[:, None]
    log_density = jnp.log(total / (count - 1))
    return (smoothed, log_density)


def solution(mesh):
    in_specs = (P(("col", "row"), None),)
    out_specs = (P(("col", "row"), None), P(("col", "row")))
    return jax.shard_map(shards, mesh=mesh, in_specs=in_specs, out_specs=out_specs, check_vma=False)
```

time: 239 us -> 222 us (0.929)
  the two profiles are of different devices: /device:TPU:1 before, /device:TPU:2 now
where the time goes in v2:
time: 222 us; the launch traced here: 219 us
  blocking collectives  72.2 us (33%)
  waiting for transfers between devices  60.3 us (27%)
  Pallas kernels  50.6 us (23%)
  starting transfers between devices  29.4 us (13%)
  other arithmetic  2.91 us (1%)
    pallas_call x1, Pallas kernels, whiten(): pl.pallas_call(functools.partial(whiten_kernel, count), out_shape=jax.Sha...  34 us
    ppermute x7, waiting for transfers between devices, shards(): sums = sums + send(part, perm=row_shift(dy, dx, False)).astype(F32)  22.5 us
    all_to_all x1, blocking collectives, shards(): mine = lax.all_to_all(mine.reshape(row_count, -1, wide), 'row', 0, 0).sum(0)  22.2 us
    all_to_all x1, blocking collectives, shards(): lax.all_to_all(mine.reshape(half, -1, wide), 'col', 0, 0, axis_index_grou...  19.9 us
    all_to_all x1, blocking collectives, shards(): lax.all_to_all(jnp.broadcast_to(mine[None], (row_count,) + mine.shape), '...  16.6 us
    ppermute x3, waiting for transfers between devices, shards(): right = send(right, perm=up)  15.7 us
    all_to_all x1, blocking collectives, shards(): lax.all_to_all(jnp.broadcast_to(mine[None], (half,) + mine.shape), 'col',...  13.4 us
    pallas_call x3, Pallas kernels, terms(): pl.pallas_call(functools.partial(terms_kernel, rows, not state, last, len...  12.7 us
  transfers between devices with their start and end apart: 31, of which 13 were waited for; matrix products, arithmetic and copies ran while one was open for 0% of the time, Pallas kernels for 4%

profile of v2, /device:TPU:2, one launch (start us, length us, event | category | flops | bytes accessed | tf_op | source)
XLA Modules:
  0.0 218.6 jit_solution(17033892092076133896)
XLA Ops:
  0.6 0.1 collective-permute-start
  0.7 1.9 collective-permute-done.y_ref
  2.7 0.7 copy-done.2
  3.4 3.9 %moments.1 = f32[256,1152]{1,0:T(8,128)} custom-call(s32[1]{0:T(128)} %bitcast.core_ref, f32[96,1024]{1,0:T(8,128)} %x_ref.3, f32[96,1024]{1,0:T(8,128)} %copy-done.2), custom_call_target="tpu_custom_call" | custom-call | tf_op jit(solution)/shard_map/moments/pallas_call | solution.py:83
  7.3 22.2 %all_to_all.20 = f32[8,32,1152]{2,1,0:T(8,128)S(1)} all-to-all(f32[8,32,1152]{2,1,0:T(8,128)} %bitcast.5), channel_id=1, replica_groups=mesh['row'=8,'col'=32] {'row'}, dimensions={0} | all-to-all | bytes 2359296 | tf_op jit(solution)/shard_map/all_to_all | solution.py:346
  29.5 0.1 reduce_sum.18
  29.6 0.1 reshape.20
  29.7 19.9 %all_to_all.21 = f32[16,2,1152]{2,1,0:T(2,128)S(1)} all-to-all(f32[16,2,1152]{2,1,0:T(2,128)S(1)} %reshape.20), channel_id=1, replica_groups={{0,2,4,6,8,10,12,14,16,18,20,22,24,26,28,30},{1,3,5,7,9,11,13,15,17,19,..., dimensions={0} | all-to-all | bytes 294912 | tf_op jit(solution)/shard_map/all_to_all | solution.py:347
  49.6 0.1 reduce_sum.19
  49.7 13.4 %all_to_all.22 = f32[16,2,1152]{2,1,0:T(2,128)S(1)} all-to-all(f32[16,2,1152]{2,1,0:T(2,128)S(1)} %broadcast_in_dim.18), channel_id=1, replica_groups={{0,2,4,6,8,10,12,14,16,18,20,22,24,26,28,30},{1,3,5,7,9,11,13,15,17,19,..., dimensions={0} | all-to-all | bytes 294912 | tf_op jit(solution)/shard_map/all_to_all | solution.py:350
  63.1 0.1 broadcast_in_dim.19
  63.2 0.1 broadcast_in_dim.20
  63.3 16.6 %all_to_all.23 = f32[8,32,1152]{2,1,0:T(8,128)S(1)} all-to-all(f32[8,32,1152]{2,1,0:T(8,128)S(1)} %broadcast_in_dim.20), channel_id=1, replica_groups=mesh['row'=8,'col'=32] {'row'}, dimensions={0} | all-to-all | bytes 2359296 | tf_op jit(solution)/shard_map/all_to_all | solution.py:353
  79.9 0.2 collective-permute-start.1
  80.1 2.8 %collective-permute-done.1.other_ref = f32[256,1152]{1,0:T(8,128)S(1)} collective-permute-done((f32[256,1152]{1,0:T(8,128)S(1)}, f32[256,1152]{1,0:T(8,128)S(1)}, u32[]{:S(2)}, u32[]{:S(2)}) %collective-permute-start.1) | collective-permute-done | bytes 1179680 | tf_op jit(solution)/shard_map/ppermute | solution.py:356
  82.9 1.0 copy-done.1
  83.9 34.0 %whiten.1 = bf16[96,1024]{1,0:T(8,128)(2,1)} custom-call(s32[1]{0:T(128)} %bitcast.core_ref, f32[256,1152]{1,0:T(8,128)} %bitcast.4, f32[256,1152]{1,0:T(8,128)} %copy-done.1, f32[96,1024]{1,0:T(8,128)} %x_ref.3), custom_call_target="tpu_custom_call" | custom-call | tf_op jit(solution)/shard_map/whiten/pallas_call | solution.py:202
  118.0 1.4 collective-permute-start.2
  119.4 1.1 collective-permute-start.6
  120.5 5.6 %collective-permute-done.2 = bf16[96,1024]{1,0:T(8,128)(2,1)S(1)} collective-permute-done((bf16[96,1024]{1,0:T(8,128)(2,1)}, bf16[96,1024]{1,0:T(8,128)(2,1)S(1)}, u32[]{:S(2)}, u32[]{:S(2)}) %collective-permute-start.2) | collective-permute-done | bytes 196640 | tf_op jit(solution)/shard_map/ppermute | solution.py:368
  126.1 3.8 %collective-permute-done.6 = bf16[96,1024]{1,0:T(8,128)(2,1)S(1)} collective-permute-done((bf16[96,1024]{1,0:T(8,128)(2,1)}, bf16[96,1024]{1,0:T(8,128)(2,1)S(1)}, u32[]{:S(2)}, u32[]{:S(2)}) %collective-permute-start.6) | collective-permute-done | bytes 196640 | tf_op jit(solution)/shard_map/ppermute | solution.py:367
  129.9 1.0 pad_maximum_fusion
  130.9 1.4 collective-permute-start.7
  132.3 1.9 collective-permute-start.10
  134.2 8.3 %collective-permute-done.7.refs_5_ = bf16[192,1024]{1,0:T(8,128)(2,1)S(1)} collective-permute-done((bf16[192,1024]{1,0:T(8,128)(2,1)S(1)}, bf16[192,1024]{1,0:T(8,128)(2,1)S(1)}, u32[]{:S(2)}, u32[]{:S(2)}) %collective-permute-start.7) | collective-permute-done | bytes 393248 | tf_op jit(solution)/shard_map/ppermute | solution.py:378
  142.5 0.1 collective-permute-start.8
  142.7 3.1 %collective-permute-start.11 = (bf16[192,1024]{1,0:T(8,128)(2,1)S(1)}, bf16[192,1024]{1,0:T(8,128)(2,1)S(1)}, u32[]{:S(2)}, u32[]{:S(2)}) collective-permute-start(bf16[192,1024]{1,0:T(8,128)(2,1)S(1)} %collective-permute-done.10.refs_6_), channel_id=1, source_target_pairs={{0,14},{1,15},{2,0},{3,1},{4,2},{5,3},{6,4},{7,5},{8,6},{9,7},{10,... | collective-permute-start | bytes 1179656 | tf_op jit(solution)/shard_map/ppermute | solution.py:379
  145.8 1.0 collective-permute-start.3
  146.8 1.5 collective-permute-start.4
  148.3 4.9 %collective-permute-done.8.refs_4_ = bf16[192,1024]{1,0:T(8,128)(2,1)S(1)} collective-permute-done((bf16[192,1024]{1,0:T(8,128)(2,1)S(1)}, bf16[192,1024]{1,0:T(8,128)(2,1)S(1)}, u32[]{:S(2)}, u32[]{:S(2)}) %collective-permute-start.8) | collective-permute-done | bytes 393248 | tf_op jit(solution)/shard_map/ppermute | solution.py:378
  153.1 0.0 collective-permute-start.9
  153.1 0.0 collective-permute-done.11.refs_5_
  153.1 3.2 %collective-permute-start.12 = (bf16[192,1024]{1,0:T(8,128)(2,1)S(1)}, bf16[192,1024]{1,0:T(8,128)(2,1)S(1)}, u32[]{:S(2)}, u32[]{:S(2)}) collective-permute-start(bf16[192,1024]{1,0:T(8,128)(2,1)S(1)} %collective-permute-done.11.refs_5_), channel_id=1, source_target_pairs={{0,14},{1,15},{2,0},{3,1},{4,2},{5,3},{6,4},{7,5},{8,6},{9,7},{10,... | collective-permute-start | bytes 1179656 | tf_op jit(solution)/shard_map/ppermute | solution.py:379
  156.4 0.4 collective-permute-start.5
  156.8 0.9 collective-permute-done.3.refs_1_
  157.7 2.6 %collective-permute-done.4.refs_2_ = bf16[192,1024]{1,0:T(8,128)(2,1)S(1)} collective-permute-done((bf16[192,1024]{1,0:T(8,128)(2,1)S(1)}, bf16[192,1024]{1,0:T(8,128)(2,1)S(1)}, u32[]{:S(2)}, u32[]{:S(2)}) %collective-permute-start.4) | collective-permute-done | bytes 393248 | tf_op jit(solution)/shard_map/ppermute | solution.py:372
  160.3 0.0 collective-permute-start.23
  160.3 2.6 %collective-permute-done.9.refs_4_ = bf16[192,1024]{1,0:T(8,128)(2,1)S(1)} collective-permute-done((bf16[192,1024]{1,0:T(8,128)(2,1)S(1)}, bf16[192,1024]{1,0:T(8,128)(2,1)S(1)}, u32[]{:S(2)}, u32[]{:S(2)}) %collective-permute-start.9) | collective-permute-done | bytes 393248 | tf_op jit(solution)/shard_map/ppermute | solution.py:378
  162.8 0.0 collective-permute-start.19
  162.8 0.5 collective-permute-start.20
  163.4 4.6 %collective-permute-done.5.refs_3_ = bf16[192,1024]{1,0:T(8,128)(2,1)S(1)} collective-permute-done((bf16[192,1024]{1,0:T(8,128)(2,1)S(1)}, bf16[192,1024]{1,0:T(8,128)(2,1)S(1)}, u32[]{:S(2)}, u32[]{:S(2)}) %collective-permute-start.5) | collective-permute-done | bytes 393248 | tf_op jit(solution)/shard_map/ppermute | solution.py:372
  168.0 0.0 collective-permute-done.22.refs_8_
  168.0 3.2 %collective-permute-start.14 = (bf16[96,1024]{1,0:T(8,128)(2,1)S(1)}, bf16[96,1024]{1,0:T(8,128)(2,1)S(1)}, u32[]{:S(2)}, u32[]{:S(2)}) collective-permute-start(bf16[96,1024]{1,0:T(8,128)(2,1)S(1)} %slice.21), channel_id=1, source_target_pairs={{0,14},{1,15},{2,0},{3,1},{4,2},{5,3},{6,4},{7,5},{8,6},{9,7},{10,... | collective-permute-start | bytes 589832 | tf_op jit(solution)/shard_map/ppermute | solution.py:382
  171.2 0.0 collective-permute-done.23.refs_9_
  171.2 0.0 collective-permute-start.15
  171.2 0.0 collective-permute-done.19.refs_6_
  171.2 0.7 collective-permute-start.16
  171.9 4.7 %terms.3 = (f32[768,1024]{1,0:T(8,128)S(1)}, f32[768,128]{1,0:T(8,128)S(1)}) custom-call(bf16[192,1024]{1,0:T(8,128)(2,1)S(1)} %get-tuple-element.29.refs_0_, bf16[192,1024]{1,0:T(8,128)(2,1)S(1)} %collective-permute-done.3.refs_1_, bf16[192,1024]{1,0:T(8,128)(2,1)S(1)} %collective-permute-done.4.refs_2_, ...), custom_call_target="tpu_custom_call" | custom-call | flops 3623878656 | bytes 6291456 | tf_op jit(solution)/shard_map/terms/pallas_call | solution.py:302
  176.6 0.0 collective-permute-done.13.refs_6_
  176.6 0.2 collective-permute-start.17
  176.8 0.4 collective-permute-start.18
  177.3 3.1 %terms.4 = (f32[768,1024]{1,0:T(8,128)S(1)}, f32[768,128]{1,0:T(8,128)S(1)}) custom-call(bf16[192,1024]{1,0:T(8,128)(2,1)S(1)} %get-tuple-element.29.refs_0_, bf16[192,1024]{1,0:T(8,128)(2,1)S(1)} %collective-permute-done.3.refs_1_, bf16[192,1024]{1,0:T(8,128)(2,1)S(1)} %collective-permute-done.4.refs_2_, ...), custom_call_target="tpu_custom_call" | custom-call | flops 2415919104 | bytes 6291456 | tf_op jit(solution)/shard_map/terms/pallas_call | solution.py:302
  180.4 4.8 %terms.5 = (bf16[96,1152]{1,0:T(8,128)(2,1)S(1)}, bf16[96,1152]{1,0:T(8,128)(2,1)S(1)}, bf16[96,1152]{1,0:T(8,128)(2,1)S(1)}, bf16[96,1152]{1,0:T(8,128)(2,1)S(1...) custom-call(bf16[192,1024]{1,0:T(8,128)(2,1)S(1)} %get-tuple-element, ...), custom_call_target="tpu_custom_call" | custom-call | flops 3623878656 | bytes 6291456 | tf_op jit(solution)/shard_map/terms/pallas_call | solution.py:302
  185.3 1.9 collective-permute-start.24
  187.1 1.4 collective-permute-start.26
  188.5 3.3 %collective-permute-start.27 = (bf16[96,1152]{1,0:T(8,128)(2,1)S(1)}, bf16[96,1152]{1,0:T(8,128)(2,1)S(1)}, u32[]{:S(2)}, u32[]{:S(2)}) collective-permute-start(bf16[96,1152]{1,0:T(8,128)(2,1)S(1)} %get-tuple-element.22), channel_id=1, source_target_pairs={{0,128},{1,129},{2,130},{3,131},{4,132},{5,133},{6,134},{7,135},{8... | collective-permute-start | bytes 663560 | tf_op jit(solution)/shard_map/ppermute | solution.py:390
  191.8 1.2 collective-permute-start.28
  192.9 1.0 collective-permute-done.24
  193.9 1.2 collective-permute-start.29
  195.0 14.7 %collective-permute-done.25 = bf16[96,1152]{1,0:T(8,128)(2,1)S(1)} collective-permute-done((bf16[96,1152]{1,0:T(8,128)(2,1)S(1)}, bf16[96,1152]{1,0:T(8,128)(2,1)S(1)}, u32[]{:S(2)}, u32[]{:S(2)}) %collective-permute-start.25) | collective-permute-done | bytes 221216 | tf_op jit(solution)/shard_map/ppermute | solution.py:390
  209.8 6.8 %collective-permute-done.30 = bf16[96,1152]{1,0:T(8,128)(2,1)S(1)} collective-permute-done((bf16[96,1152]{1,0:T(8,128)(2,1)S(1)}, bf16[96,1152]{1,0:T(8,128)(2,1)S(1)}, u32[]{:S(2)}, u32[]{:S(2)}) %collective-permute-start.30) | collective-permute-done | bytes 221216 | tf_op jit(solution)/shard_map/ppermute | solution.py:390
  216.6 0.2 convert_add_fusion
  216.8 0.7 log_reduce_fusion
  217.5 0.8 slice_divide_fusion
  (25 shorter events, 0.1 us)
Async XLA Ops:
  0.6 2.0 collective-permute-start
  2.6 0.7 copy-start.2
  79.9 3.0 %copy-start = (f32[8,32,1152]{2,1,0:T(8,128)}, f32[8,32,1152]{2,1,0:T(8,128)S(1)}, u32[]{:S(2)}) copy-start(f32[8,32,1152]{2,1,0:T(8,128)S(1)} %all_to_all.23) | copy-start | bytes 3538948
  79.9 3.0 %collective-permute-start.1 = (f32[256,1152]{1,0:T(8,128)S(1)}, f32[256,1152]{1,0:T(8,128)S(1)}, u32[]{:S(2)}, u32[]{:S(2)}) collective-permute-start(f32[256,1152]{1,0:T(8,128)S(1)} %bitcast.3), channel_id=1, source_target_pairs={{0,1},{1,0},{2,3},{3,2},{4,5},{5,4},{6,7},{7,6},{8,9},{9,8},{10,11... | collective-permute-start | bytes 3538952 | tf_op jit(solution)/shard_map/ppermute | solution.py:356
  82.9 1.0 copy-start.1
  118.0 8.1 %collective-permute-start.2 = (bf16[96,1024]{1,0:T(8,128)(2,1)}, bf16[96,1024]{1,0:T(8,128)(2,1)S(1)}, u32[]{:S(2)}, u32[]{:S(2)}) collective-permute-start(bf16[96,1024]{1,0:T(8,128)(2,1)} %whiten.1), channel_id=1, source_target_pairs={{32,0},{33,1},{34,2},{35,3},{36,4},{37,5},{38,6},{39,7},{40,8},{41... | collective-permute-start | bytes 589832 | tf_op jit(solution)/shard_map/ppermute | solution.py:368
  119.4 10.4 %collective-permute-start.6 = (bf16[96,1024]{1,0:T(8,128)(2,1)}, bf16[96,1024]{1,0:T(8,128)(2,1)S(1)}, u32[]{:S(2)}, u32[]{:S(2)}) collective-permute-start(bf16[96,1024]{1,0:T(8,128)(2,1)} %whiten.1), channel_id=1, source_target_pairs={{0,16},{1,17},{2,18},{3,19},{4,20},{5,21},{6,22},{7,23},{8,24},{9,... | collective-permute-start | bytes 589832 | tf_op jit(solution)/shard_map/ppermute | solution.py:367
  130.9 11.6 %collective-permute-start.7 = (bf16[192,1024]{1,0:T(8,128)(2,1)S(1)}, bf16[192,1024]{1,0:T(8,128)(2,1)S(1)}, u32[]{:S(2)}, u32[]{:S(2)}) collective-permute-start(bf16[192,1024]{1,0:T(8,128)(2,1)S(1)} %get-tuple-element.28.refs_4_), channel_id=1, source_target_pairs={{0,2},{1,3},{2,4},{3,5},{4,6},{5,7},{6,8},{7,9},{8,10},{9,11},{10,... | collective-permute-start | bytes 1179656 | tf_op jit(solution)/shard_map/ppermute | solution.py:378
  132.3 10.3 %collective-permute-start.10 = (bf16[192,1024]{1,0:T(8,128)(2,1)S(1)}, bf16[192,1024]{1,0:T(8,128)(2,1)S(1)}, u32[]{:S(2)}, u32[]{:S(2)}) collective-permute-start(bf16[192,1024]{1,0:T(8,128)(2,1)S(1)} %get-tuple-element.28.refs_4_), channel_id=1, source_target_pairs={{0,14},{1,15},{2,0},{3,1},{4,2},{5,3},{6,4},{7,5},{8,6},{9,7},{10,... | collective-permute-start | bytes 1179656 | tf_op jit(solution)/shard_map/ppermute | solution.py:379
  142.5 10.6 %collective-permute-start.8 = (bf16[192,1024]{1,0:T(8,128)(2,1)S(1)}, bf16[192,1024]{1,0:T(8,128)(2,1)S(1)}, u32[]{:S(2)}, u32[]{:S(2)}) collective-permute-start(bf16[192,1024]{1,0:T(8,128)(2,1)S(1)} %collective-permute-done.7.refs_5_), channel_id=1, source_target_pairs={{0,2},{1,3},{2,4},{3,5},{4,6},{5,7},{6,8},{7,9},{8,10},{9,11},{10,... | collective-permute-start | bytes 1179656 | tf_op jit(solution)/shard_map/ppermute | solution.py:378
  142.7 10.5 %collective-permute-start.11 = (bf16[192,1024]{1,0:T(8,128)(2,1)S(1)}, bf16[192,1024]{1,0:T(8,128)(2,1)S(1)}, u32[]{:S(2)}, u32[]{:S(2)}) collective-permute-start(bf16[192,1024]{1,0:T(8,128)(2,1)S(1)} %collective-permute-done.10.refs_6_), channel_id=1, source_target_pairs={{0,14},{1,15},{2,0},{3,1},{4,2},{5,3},{6,4},{7,5},{8,6},{9,7},{10,... | collective-permute-start | bytes 1179656 | tf_op jit(solution)/shard_map/ppermute | solution.py:379
  145.7 10.6 %collective-permute-start.21 = (bf16[192,1024]{1,0:T(8,128)(2,1)S(1)}, bf16[192,1024]{1,0:T(8,128)(2,1)S(1)}, u32[]{:S(2)}, u32[]{:S(2)}) collective-permute-start(bf16[192,1024]{1,0:T(8,128)(2,1)S(1)} %get-tuple-element.28.refs_4_), channel_id=1, source_target_pairs={{0,1},{1,0},{2,3},{3,2},{4,5},{5,4},{6,7},{7,6},{8,9},{9,8},{10,11... | collective-permute-start | bytes 1179656 | tf_op jit(solution)/shard_map/ppermute | solution.py:386
  145.8 11.9 %collective-permute-start.3 = (bf16[192,1024]{1,0:T(8,128)(2,1)S(1)}, bf16[192,1024]{1,0:T(8,128)(2,1)S(1)}, u32[]{:S(2)}, u32[]{:S(2)}) collective-permute-start(bf16[192,1024]{1,0:T(8,128)(2,1)S(1)} %get-tuple-element.29.refs_0_), channel_id=1, source_target_pairs={{64,0},{65,1},{66,2},{67,3},{68,4},{69,5},{70,6},{71,7},{72,8},{73... | collective-permute-start | bytes 1179656 | tf_op jit(solution)/shard_map/ppermute | solution.py:372
  146.8 13.5 %collective-permute-start.4 = (bf16[192,1024]{1,0:T(8,128)(2,1)S(1)}, bf16[192,1024]{1,0:T(8,128)(2,1)S(1)}, u32[]{:S(2)}, u32[]{:S(2)}) collective-permute-start(bf16[192,1024]{1,0:T(8,128)(2,1)S(1)} %get-tuple-element.29.refs_0_), channel_id=1, source_target_pairs={{128,0},{129,1},{130,2},{131,3},{132,4},{133,5},{134,6},{135,7},{1... | collective-permute-start | bytes 1179656 | tf_op jit(solution)/shard_map/ppermute | solution.py:372
  153.1 9.7 %collective-permute-start.9 = (bf16[192,1024]{1,0:T(8,128)(2,1)S(1)}, bf16[192,1024]{1,0:T(8,128)(2,1)S(1)}, u32[]{:S(2)}, u32[]{:S(2)}) collective-permute-start(bf16[192,1024]{1,0:T(8,128)(2,1)S(1)} %collective-permute-done.8.refs_4_), channel_id=1, source_target_pairs={{0,2},{1,3},{2,4},{3,5},{4,6},{5,7},{6,8},{7,9},{8,10},{9,11},{10,... | collective-permute-start | bytes 1179656 | tf_op jit(solution)/shard_map/ppermute | solution.py:378
  153.1 9.7 %collective-permute-start.12 = (bf16[192,1024]{1,0:T(8,128)(2,1)S(1)}, bf16[192,1024]{1,0:T(8,128)(2,1)S(1)}, u32[]{:S(2)}, u32[]{:S(2)}) collective-permute-start(bf16[192,1024]{1,0:T(8,128)(2,1)S(1)} %collective-permute-done.11.refs_5_), channel_id=1, source_target_pairs={{0,14},{1,15},{2,0},{3,1},{4,2},{5,3},{6,4},{7,5},{8,6},{9,7},{10,... | collective-permute-start | bytes 1179656 | tf_op jit(solution)/shard_map/ppermute | solution.py:379
  156.4 11.6 %collective-permute-start.5 = (bf16[192,1024]{1,0:T(8,128)(2,1)S(1)}, bf16[192,1024]{1,0:T(8,128)(2,1)S(1)}, u32[]{:S(2)}, u32[]{:S(2)}) collective-permute-start(bf16[192,1024]{1,0:T(8,128)(2,1)S(1)} %get-tuple-element.29.refs_0_), channel_id=1, source_target_pairs={{192,0},{193,1},{194,2},{195,3},{196,4},{197,5},{198,6},{199,7},{2... | collective-permute-start | bytes 1179656 | tf_op jit(solution)/shard_map/ppermute | solution.py:372
  157.7 10.3 %collective-permute-start.22 = (bf16[192,1024]{1,0:T(8,128)(2,1)S(1)}, bf16[192,1024]{1,0:T(8,128)(2,1)S(1)}, u32[]{:S(2)}, u32[]{:S(2)}) collective-permute-start(bf16[192,1024]{1,0:T(8,128)(2,1)S(1)} %collective-permute-done.7.refs_5_), channel_id=1, source_target_pairs={{0,1},{1,0},{2,3},{3,2},{4,5},{5,4},{6,7},{7,6},{8,9},{9,8},{10,11... | collective-permute-start | bytes 1179656 | tf_op jit(solution)/shard_map/ppermute | solution.py:386
  160.3 10.9 %collective-permute-start.23 = (bf16[192,1024]{1,0:T(8,128)(2,1)S(1)}, bf16[192,1024]{1,0:T(8,128)(2,1)S(1)}, u32[]{:S(2)}, u32[]{:S(2)}) collective-permute-start(bf16[192,1024]{1,0:T(8,128)(2,1)S(1)} %collective-permute-done.10.refs_6_), channel_id=1, source_target_pairs={{0,1},{1,0},{2,3},{3,2},{4,5},{5,4},{6,7},{7,6},{8,9},{9,8},{10,11... | collective-permute-start | bytes 1179656 | tf_op jit(solution)/shard_map/ppermute | solution.py:386
  162.8 8.4 %collective-permute-start.19 = (bf16[192,1024]{1,0:T(8,128)(2,1)S(1)}, bf16[192,1024]{1,0:T(8,128)(2,1)S(1)}, u32[]{:S(2)}, u32[]{:S(2)}) collective-permute-start(bf16[192,1024]{1,0:T(8,128)(2,1)S(1)} %collective-permute-done.8.refs_4_), channel_id=1, source_target_pairs={{0,1},{1,0},{2,3},{3,2},{4,5},{5,4},{6,7},{7,6},{8,9},{9,8},{10,11... | collective-permute-start | bytes 1179656 | tf_op jit(solution)/shard_map/ppermute | solution.py:386
  162.8 14.4 %collective-permute-start.20 = (bf16[192,1024]{1,0:T(8,128)(2,1)S(1)}, bf16[192,1024]{1,0:T(8,128)(2,1)S(1)}, u32[]{:S(2)}, u32[]{:S(2)}) collective-permute-start(bf16[192,1024]{1,0:T(8,128)(2,1)S(1)} %collective-permute-done.11.refs_5_), channel_id=1, source_target_pairs={{0,1},{1,0},{2,3},{3,2},{4,5},{5,4},{6,7},{7,6},{8,9},{9,8},{10,11... | collective-permute-start | bytes 1179656 | tf_op jit(solution)/shard_map/ppermute | solution.py:386
  168.0 8.7 %collective-permute-start.13 = (bf16[96,1024]{1,0:T(8,128)(2,1)S(1)}, bf16[96,1024]{1,0:T(8,128)(2,1)S(1)}, u32[]{:S(2)}, u32[]{:S(2)}) collective-permute-start(bf16[96,1024]{1,0:T(8,128)(2,1)S(1)} %slice.20), channel_id=1, source_target_pairs={{0,2},{1,3},{2,4},{3,5},{4,6},{5,7},{6,8},{7,9},{8,10},{9,11},{10,... | collective-permute-start | bytes 589832 | tf_op jit(solution)/shard_map/ppermute | solution.py:382
  168.0 8.9 %collective-permute-start.14 = (bf16[96,1024]{1,0:T(8,128)(2,1)S(1)}, bf16[96,1024]{1,0:T(8,128)(2,1)S(1)}, u32[]{:S(2)}, u32[]{:S(2)}) collective-permute-start(bf16[96,1024]{1,0:T(8,128)(2,1)S(1)} %slice.21), channel_id=1, source_target_pairs={{0,14},{1,15},{2,0},{3,1},{4,2},{5,3},{6,4},{7,5},{8,6},{9,7},{10,... | collective-permute-start | bytes 589832 | tf_op jit(solution)/shard_map/ppermute | solution.py:382
  171.2 9.2 %collective-permute-start.15 = (bf16[192,1024]{1,0:T(8,128)(2,1)S(1)}, bf16[192,1024]{1,0:T(8,128)(2,1)S(1)}, u32[]{:S(2)}, u32[]{:S(2)}) collective-permute-start(bf16[192,1024]{1,0:T(8,128)(2,1)S(1)} %collective-permute-done.9.refs_4_), channel_id=1, source_target_pairs={{0,1},{1,0},{2,3},{3,2},{4,5},{5,4},{6,7},{7,6},{8,9},{9,8},{10,11... | collective-permute-start | bytes 1179656 | tf_op jit(solution)/shard_map/ppermute | solution.py:386
  171.2 9.2 %collective-permute-start.16 = (bf16[192,1024]{1,0:T(8,128)(2,1)S(1)}, bf16[192,1024]{1,0:T(8,128)(2,1)S(1)}, u32[]{:S(2)}, u32[]{:S(2)}) collective-permute-start(bf16[192,1024]{1,0:T(8,128)(2,1)S(1)} %collective-permute-done.12.refs_5_), channel_id=1, source_target_pairs={{0,1},{1,0},{2,3},{3,2},{4,5},{5,4},{6,7},{7,6},{8,9},{9,8},{10,11... | collective-permute-start | bytes 1179656 | tf_op jit(solution)/shard_map/ppermute | solution.py:386
  176.6 3.8 %collective-permute-start.17 = (bf16[96,1024]{1,0:T(8,128)(2,1)S(1)}, bf16[96,1024]{1,0:T(8,128)(2,1)S(1)}, u32[]{:S(2)}, u32[]{:S(2)}) collective-permute-start(bf16[96,1024]{1,0:T(8,128)(2,1)S(1)} %collective-permute-done.13.refs_6_), channel_id=1, source_target_pairs={{0,1},{1,0},{2,3},{3,2},{4,5},{5,4},{6,7},{7,6},{8,9},{9,8},{10,11... | collective-permute-start | bytes 589832 | tf_op jit(solution)/shard_map/ppermute | solution.py:386
  176.8 3.6 %collective-permute-start.18 = (bf16[96,1024]{1,0:T(8,128)(2,1)S(1)}, bf16[96,1024]{1,0:T(8,128)(2,1)S(1)}, u32[]{:S(2)}, u32[]{:S(2)}) collective-permute-start(bf16[96,1024]{1,0:T(8,128)(2,1)S(1)} %collective-permute-done.14.refs_7_), channel_id=1, source_target_pairs={{0,1},{1,0},{2,3},{3,2},{4,5},{5,4},{6,7},{7,6},{8,9},{9,8},{10,11... | collective-permute-start | bytes 589832 | tf_op jit(solution)/shard_map/ppermute | solution.py:386
  185.3 8.6 %collective-permute-start.24 = (bf16[96,1152]{1,0:T(8,128)(2,1)S(1)}, bf16[96,1152]{1,0:T(8,128)(2,1)S(1)}, u32[]{:S(2)}, u32[]{:S(2)}) collective-permute-start(bf16[96,1152]{1,0:T(8,128)(2,1)S(1)} %get-tuple-element.19), channel_id=1, source_target_pairs={{0,32},{1,33},{2,34},{3,35},{4,36},{5,37},{6,38},{7,39},{8,40},{9,... | collective-permute-start | bytes 663560 | tf_op jit(solution)/shard_map/ppermute | solution.py:390
  187.1 22.6 %collective-permute-start.25 = (bf16[96,1152]{1,0:T(8,128)(2,1)S(1)}, bf16[96,1152]{1,0:T(8,128)(2,1)S(1)}, u32[]{:S(2)}, u32[]{:S(2)}) collective-permute-start(bf16[96,1152]{1,0:T(8,128)(2,1)S(1)} %get-tuple-element.20), channel_id=1, source_target_pairs={{0,64},{1,65},{2,66},{3,67},{4,68},{5,69},{6,70},{7,71},{8,72},{9,... | collective-permute-start | bytes 663560 | tf_op jit(solution)/shard_map/ppermute | solution.py:390
  187.1 22.6 %collective-permute-start.26 = (bf16[96,1152]{1,0:T(8,128)(2,1)S(1)}, bf16[96,1152]{1,0:T(8,128)(2,1)S(1)}, u32[]{:S(2)}, u32[]{:S(2)}) collective-permute-start(bf16[96,1152]{1,0:T(8,128)(2,1)S(1)} %get-tuple-element.21), channel_id=1, source_target_pairs={{0,96},{1,97},{2,98},{3,99},{4,100},{5,101},{6,102},{7,103},{8,104... | collective-permute-start | bytes 663560 | tf_op jit(solution)/shard_map/ppermute | solution.py:390
  188.5 21.2 %collective-permute-start.27 = (bf16[96,1152]{1,0:T(8,128)(2,1)S(1)}, bf16[96,1152]{1,0:T(8,128)(2,1)S(1)}, u32[]{:S(2)}, u32[]{:S(2)}) collective-permute-start(bf16[96,1152]{1,0:T(8,128)(2,1)S(1)} %get-tuple-element.22), channel_id=1, source_target_pairs={{0,128},{1,129},{2,130},{3,131},{4,132},{5,133},{6,134},{7,135},{8... | collective-permute-start | bytes 663560 | tf_op jit(solution)/shard_map/ppermute | solution.py:390
  191.8 18.0 %collective-permute-start.28 = (bf16[96,1152]{1,0:T(8,128)(2,1)S(1)}, bf16[96,1152]{1,0:T(8,128)(2,1)S(1)}, u32[]{:S(2)}, u32[]{:S(2)}) collective-permute-start(bf16[96,1152]{1,0:T(8,128)(2,1)S(1)} %get-tuple-element.23), channel_id=1, source_target_pairs={{0,160},{1,161},{2,162},{3,163},{4,164},{5,165},{6,166},{7,167},{8... | collective-permute-start | bytes 663560 | tf_op jit(solution)/shard_map/ppermute | solution.py:390
  193.9 15.9 %collective-permute-start.29 = (bf16[96,1152]{1,0:T(8,128)(2,1)S(1)}, bf16[96,1152]{1,0:T(8,128)(2,1)S(1)}, u32[]{:S(2)}, u32[]{:S(2)}) collective-permute-start(bf16[96,1152]{1,0:T(8,128)(2,1)S(1)} %get-tuple-element.24), channel_id=1, source_target_pairs={{0,192},{1,193},{2,194},{3,195},{4,196},{5,197},{6,198},{7,199},{8... | collective-permute-start | bytes 663560 | tf_op jit(solution)/shard_map/ppermute | solution.py:390
  209.7 6.8 %collective-permute-start.30 = (bf16[96,1152]{1,0:T(8,128)(2,1)S(1)}, bf16[96,1152]{1,0:T(8,128)(2,1)S(1)}, u32[]{:S(2)}, u32[]{:S(2)}) collective-permute-start(bf16[96,1152]{1,0:T(8,128)(2,1)S(1)} %get-tuple-element.25), channel_id=1, source_target_pairs={{0,224},{1,225},{2,226},{3,227},{4,228},{5,229},{6,230},{7,231},{8... | collective-permute-start | bytes 663560 | tf_op jit(solution)/shard_map/ppermute | solution.py:390

commit v3 on v2

--- a/solution.py
+++ b/solution.py
@@ -11,8 +11,9 @@
 BLOCK = 128
 PANEL = 16
 EXTRA = 128
+STRIP = 256
 VMEM = 56 * 2**20
-TERMS_VMEM = 40 * 2**20
+SOME_VMEM = 40 * 2**20
 AXES = ("row", "col")
 NN = ((1,), (0,))
 NT = ((1,), (1,))
@@ -179,9 +180,19 @@
             w[b:after, :b] = dot3(wk, m[b:after, :b], NN)
         if after < width:
             lk = dot3(m[after:, b:after], wk, NT)
-            m[after:, b:after] = jnp.zeros((width - after, BLOCK), F32)
-            m[after:, :after] = m[after:, :after] - dot3(lk, w[b:after, :after], NN)
-            m[after:, after:] = m[after:, after:] - dot3(lk, lk, NT)
+            lk_hi, lk_lo = split(lk)
+            both = jnp.concatenate([lk_hi, lk_lo], 1)
+            twice = jnp.concatenate([lk_hi, lk_hi], 1)
+            w_hi, w_lo = split(w[b:after, :after])
+            left = mul(both, jnp.concatenate([w_hi, w_hi], 0), NN) + mul(lk_hi, w_lo, NN)
+            if b:
+                m[after:, :b] = m[after:, :b] - left[:, :b]
+            m[after:, b:after] = -left[:, b:]
+            for j in range(after, width, STRIP):
+                end = min(j + STRIP, width)
+                i, n = j - after, end - after
+                term = mul(both[i:], twice[i:n], NT) + mul(lk_hi[i:], lk_lo[i:n], NT)
+                m[j:, j:end] = m[j:, j:end] - term
     mean = jnp.concatenate([up_row, low_row], 1)
     centred = x_ref[...] - mean
     step = 256
@@ -211,7 +222,7 @@
             pltpu.VMEM((BLOCK, BLOCK), F32),
             pltpu.VMEM((BLOCK, BLOCK), F32),
         ],
-        compiler_params=pltpu.CompilerParams(vmem_limit_bytes=VMEM),
+        compiler_params=pltpu.CompilerParams(vmem_limit_bytes=SOME_VMEM),
         name="whiten",
     )(core, mine, other, x)
 
@@ -305,7 +316,7 @@
         in_specs=[vmem] * (len(query_list) + n_keys + len(state)),
         out_specs=(vmem,) * len(out_shape),
         scratch_shapes=[pltpu.VMEM((keys, width), BF16)],
-        compiler_params=pltpu.CompilerParams(vmem_limit_bytes=TERMS_VMEM),
+        compiler_params=pltpu.CompilerParams(vmem_limit_bytes=SOME_VMEM),
         cost_estimate=pl.CostEstimate(
             flops=4 * queries * keys * width,
             bytes_accessed=8 * queries * width,
@@ -365,8 +376,9 @@
         return pairs
 
     far = send(white, perm=shift(sizes, dx=1))
-    near = send(white, perm=row_shift(0, 1, True))
     pair = jnp.concatenate([white, far], 0)
+    pair, later = lax.optimization_barrier((pair, white))
+    near = send(later, perm=row_shift(0, 1, True))
     asked = jnp.concatenate([white, near], 0)
     queries = [asked] + [
         send(asked, perm=row_shift(dy, 0, True)) for dy in range(1, row_count // 2)
@@ -386,7 +398,8 @@
         blocks = blocks + [send(block, perm=to_core) for block in blocks]
         state = terms(rows, queries, blocks, state, i == len(arrived) - 1)
     sums = state[0].astype(F32)
-    for (dy, dx), part in list(zip(moves(row_count), state))[1:]:
+    tail = list(zip(moves(row_count), state))[1:]
+    for (dy, dx), part in sorted(tail, key=lambda item: -item[0][1]):
         sums = sums + send(part, perm=row_shift(dy, dx, False)).astype(F32)
     total = sums[:, width] + sums[:, width + 1]
     smoothed = sums[:, :width] / total[:, None]

time: 222 us -> 213 us (0.959)
  the two profiles are of different devices: /device:TPU:2 before, /device:TPU:1 now
where the time goes in v3:
time: 213 us; the launch traced here: 209 us
  blocking collectives  66.2 us (31%)
  waiting for transfers between devices  50.1 us (24%)
  Pallas kernels  44.8 us (21%)
  starting transfers between devices  43.9 us (21%)
    pallas_call x1, Pallas kernels, whiten(): pl.pallas_call(functools.partial(whiten_kernel, count), out_shape=jax.Sha...  28.3 us
    ppermute x7, waiting for transfers between devices, shards(): sums = sums + send(part, perm=row_shift(dy, dx, False)).astype(F32)  21.1 us
    all_to_all x1, blocking collectives, shards(): mine = lax.all_to_all(mine.reshape(row_count, -1, wide), 'row', 0, 0).sum(0)  20.1 us
    all_to_all x1, blocking collectives, shards(): lax.all_to_all(mine.reshape(half, -1, wide), 'col', 0, 0, axis_index_grou...  18.8 us
    all_to_all x1, blocking collectives, shards(): lax.all_to_all(jnp.broadcast_to(mine[None], (row_count,) + mine.shape), '...  15.2 us
    pallas_call x3, Pallas kernels, terms(): pl.pallas_call(functools.partial(terms_kernel, rows, not state, last, len...  12.6 us
    ppermute x9, starting transfers between devices, shards(): blocks = blocks + [send(block, perm=to_core) for block in blocks]  12.3 us
    all_to_all x1, blocking collectives, shards(): lax.all_to_all(jnp.broadcast_to(mine[None], (half,) + mine.shape), 'col',...  12.1 us
  transfers between devices with their start and end apart: 31, of which 14 were waited for; matrix products, arithmetic and copies ran while one was open for 0% of the time, Pallas kernels for 4%

profile of v3, /device:TPU:1, one launch (start us, length us, event | category | flops | bytes accessed | tf_op | source)
XLA Modules:
  0.0 208.9 jit_solution(5957844736819033757)
XLA Ops:
  0.6 3.3 %collective-permute-start = (f32[96,1024]{1,0:T(8,128)}, f32[96,1024]{1,0:T(8,128)S(1)}, u32[]{:S(2)}, u32[]{:S(2)}) collective-permute-start(f32[96,1024]{1,0:T(8,128)} %x_ref.3), channel_id=1, source_target_pairs={{0,1},{1,0},{2,3},{3,2},{4,5},{5,4},{6,7},{7,6},{8,9},{9,8},{10,11... | collective-permute-start | bytes 1179656 | tf_op jit(solution)/shard_map/ppermute | solution.py:355
  4.0 1.6 collective-permute-done.y_ref
  5.5 0.7 copy-done.1
  6.3 3.8 %moments.1 = f32[256,1152]{1,0:T(8,128)} custom-call(s32[1]{0:T(128)} %bitcast.core_ref, f32[96,1024]{1,0:T(8,128)} %x_ref.3, f32[96,1024]{1,0:T(8,128)} %copy-done.1), custom_call_target="tpu_custom_call" | custom-call | tf_op jit(solution)/shard_map/moments/pallas_call | solution.py:84
  10.1 20.1 %all_to_all.20 = f32[8,32,1152]{2,1,0:T(8,128)S(1)} all-to-all(f32[8,32,1152]{2,1,0:T(8,128)} %bitcast.5), channel_id=1, replica_groups=mesh['row'=8,'col'=32] {'row'}, dimensions={0} | all-to-all | bytes 2359296 | tf_op jit(solution)/shard_map/all_to_all | solution.py:357
  30.2 0.1 reduce_sum.18
  30.3 0.1 reshape.20
  30.4 18.8 %all_to_all.21 = f32[16,2,1152]{2,1,0:T(2,128)S(1)} all-to-all(f32[16,2,1152]{2,1,0:T(2,128)S(1)} %reshape.20), channel_id=1, replica_groups={{0,2,4,6,8,10,12,14,16,18,20,22,24,26,28,30},{1,3,5,7,9,11,13,15,17,19,..., dimensions={0} | all-to-all | bytes 294912 | tf_op jit(solution)/shard_map/all_to_all | solution.py:358
  49.2 0.1 reduce_sum.19
  49.3 12.1 %all_to_all.22 = f32[16,2,1152]{2,1,0:T(2,128)S(1)} all-to-all(f32[16,2,1152]{2,1,0:T(2,128)S(1)} %broadcast_in_dim.18), channel_id=1, replica_groups={{0,2,4,6,8,10,12,14,16,18,20,22,24,26,28,30},{1,3,5,7,9,11,13,15,17,19,..., dimensions={0} | all-to-all | bytes 294912 | tf_op jit(solution)/shard_map/all_to_all | solution.py:361
  61.4 0.1 broadcast_in_dim.19
  61.5 0.1 broadcast_in_dim.20
  61.6 0.0 copy-start
  61.6 15.2 %all_to_all.23 = f32[8,32,1152]{2,1,0:T(8,128)S(1)} all-to-all(f32[8,32,1152]{2,1,0:T(8,128)S(1)} %broadcast_in_dim.20), channel_id=1, replica_groups=mesh['row'=8,'col'=32] {'row'}, dimensions={0} | all-to-all | bytes 2359296 | tf_op jit(solution)/shard_map/all_to_all | solution.py:364
  76.8 6.0 %collective-permute-start.1 = (f32[256,1152]{1,0:T(8,128)S(1)}, f32[256,1152]{1,0:T(8,128)S(1)}, u32[]{:S(2)}, u32[]{:S(2)}) collective-permute-start(f32[256,1152]{1,0:T(8,128)S(1)} %bitcast.3), channel_id=1, source_target_pairs={{0,1},{1,0},{2,3},{3,2},{4,5},{5,4},{6,7},{7,6},{8,9},{9,8},{10,11... | collective-permute-start | bytes 3538952 | tf_op jit(solution)/shard_map/ppermute | solution.py:367
  82.8 2.5 %collective-permute-done.1.other_ref = f32[256,1152]{1,0:T(8,128)S(1)} collective-permute-done((f32[256,1152]{1,0:T(8,128)S(1)}, f32[256,1152]{1,0:T(8,128)S(1)}, u32[]{:S(2)}, u32[]{:S(2)}) %collective-permute-start.1) | collective-permute-done | bytes 1179680 | tf_op jit(solution)/shard_map/ppermute | solution.py:367
  85.3 28.3 %whiten.1 = bf16[96,1024]{1,0:T(8,128)(2,1)S(1)} custom-call(s32[1]{0:T(128)} %bitcast.core_ref, f32[256,1152]{1,0:T(8,128)S(1)} %bitcast.4, f32[256,1152]{1,0:T(8,128)S(1)} %collective-permute-done.1.other_ref, f32[96,1024]{1,0:T(8,128)S(1)} %copy-done), custom_call_target="tpu_custom_call" | custom-call | tf_op jit(solution)/shard_map/whiten/pallas_call | solution.py:213
  113.6 1.5 collective-permute-start.2
  115.1 6.2 %collective-permute-done.2 = bf16[96,1024]{1,0:T(8,128)(2,1)S(1)} collective-permute-done((bf16[96,1024]{1,0:T(8,128)(2,1)S(1)}, bf16[96,1024]{1,0:T(8,128)(2,1)S(1)}, u32[]{:S(2)}, u32[]{:S(2)}) %collective-permute-start.2) | collective-permute-done | bytes 196640 | tf_op jit(solution)/shard_map/ppermute | solution.py:378
  121.3 1.3 collective-permute-start.7
  122.7 1.4 collective-permute-start.10
  124.1 7.9 %collective-permute-done.7.refs_5_ = bf16[192,1024]{1,0:T(8,128)(2,1)S(1)} collective-permute-done((bf16[192,1024]{1,0:T(8,128)(2,1)S(1)}, bf16[192,1024]{1,0:T(8,128)(2,1)S(1)}, u32[]{:S(2)}, u32[]{:S(2)}) %collective-permute-start.7) | collective-permute-done | bytes 393248 | tf_op jit(solution)/shard_map/ppermute | solution.py:390
  132.0 0.2 collective-permute-start.8
  132.3 0.5 collective-permute-start.3
  132.8 2.6 %collective-permute-start.21 = (bf16[192,1024]{1,0:T(8,128)(2,1)S(1)}, bf16[192,1024]{1,0:T(8,128)(2,1)S(1)}, u32[]{:S(2)}, u32[]{:S(2)}) collective-permute-start(bf16[192,1024]{1,0:T(8,128)(2,1)S(1)} %pad_maximum_fusion.refs_4_), channel_id=1, source_target_pairs={{0,1},{1,0},{2,3},{3,2},{4,5},{5,4},{6,7},{7,6},{8,9},{9,8},{10,11... | collective-permute-start | bytes 1179656 | tf_op jit(solution)/shard_map/ppermute | solution.py:398
  135.4 0.0 collective-permute-done.10.refs_6_
  135.4 2.6 %collective-permute-start.11 = (bf16[192,1024]{1,0:T(8,128)(2,1)S(1)}, bf16[192,1024]{1,0:T(8,128)(2,1)S(1)}, u32[]{:S(2)}, u32[]{:S(2)}) collective-permute-start(bf16[192,1024]{1,0:T(8,128)(2,1)S(1)} %collective-permute-done.10.refs_6_), channel_id=1, source_target_pairs={{0,14},{1,15},{2,0},{3,1},{4,2},{5,3},{6,4},{7,5},{8,6},{9,7},{10,... | collective-permute-start | bytes 1179656 | tf_op jit(solution)/shard_map/ppermute | solution.py:391
  138.1 1.0 collective-permute-start.4
  139.0 1.2 collective-permute-start.5
  140.2 1.7 collective-permute-done.8.refs_4_
  141.9 0.0 collective-permute-start.9
  141.9 4.7 %collective-permute-done.11.refs_5_ = bf16[192,1024]{1,0:T(8,128)(2,1)S(1)} collective-permute-done((bf16[192,1024]{1,0:T(8,128)(2,1)S(1)}, bf16[192,1024]{1,0:T(8,128)(2,1)S(1)}, u32[]{:S(2)}, u32[]{:S(2)}) %collective-permute-start.11) | collective-permute-done | bytes 393248 | tf_op jit(solution)/shard_map/ppermute | solution.py:391
  146.6 3.4 %collective-permute-start.12 = (bf16[192,1024]{1,0:T(8,128)(2,1)S(1)}, bf16[192,1024]{1,0:T(8,128)(2,1)S(1)}, u32[]{:S(2)}, u32[]{:S(2)}) collective-permute-start(bf16[192,1024]{1,0:T(8,128)(2,1)S(1)} %collective-permute-done.11.refs_5_), channel_id=1, source_target_pairs={{0,14},{1,15},{2,0},{3,1},{4,2},{5,3},{6,4},{7,5},{8,6},{9,7},{10,... | collective-permute-start | bytes 1179656 | tf_op jit(solution)/shard_map/ppermute | solution.py:391
  150.0 0.3 collective-permute-start.6
  150.3 2.2 %collective-permute-start.22 = (bf16[192,1024]{1,0:T(8,128)(2,1)S(1)}, bf16[192,1024]{1,0:T(8,128)(2,1)S(1)}, u32[]{:S(2)}, u32[]{:S(2)}) collective-permute-start(bf16[192,1024]{1,0:T(8,128)(2,1)S(1)} %collective-permute-done.7.refs_5_), channel_id=1, source_target_pairs={{0,1},{1,0},{2,3},{3,2},{4,5},{5,4},{6,7},{7,6},{8,9},{9,8},{10,11... | collective-permute-start | bytes 1179656 | tf_op jit(solution)/shard_map/ppermute | solution.py:398
  152.5 0.0 collective-permute-start.23
  152.5 2.1 %collective-permute-start.19 = (bf16[192,1024]{1,0:T(8,128)(2,1)S(1)}, bf16[192,1024]{1,0:T(8,128)(2,1)S(1)}, u32[]{:S(2)}, u32[]{:S(2)}) collective-permute-start(bf16[192,1024]{1,0:T(8,128)(2,1)S(1)} %collective-permute-done.8.refs_4_), channel_id=1, source_target_pairs={{0,1},{1,0},{2,3},{3,2},{4,5},{5,4},{6,7},{7,6},{8,9},{9,8},{10,11... | collective-permute-start | bytes 1179656 | tf_op jit(solution)/shard_map/ppermute | solution.py:398
  154.6 3.0 %collective-permute-done.12.refs_5_ = bf16[192,1024]{1,0:T(8,128)(2,1)S(1)} collective-permute-done((bf16[192,1024]{1,0:T(8,128)(2,1)S(1)}, bf16[192,1024]{1,0:T(8,128)(2,1)S(1)}, u32[]{:S(2)}, u32[]{:S(2)}) %collective-permute-start.12) | collective-permute-done | bytes 393248 | tf_op jit(solution)/shard_map/ppermute | solution.py:391
  157.6 1.7 collective-permute-start.20
  159.4 1.4 collective-permute-done.6.refs_3_
  160.8 2.7 %collective-permute-start.14 = (bf16[96,1024]{1,0:T(8,128)(2,1)S(1)}, bf16[96,1024]{1,0:T(8,128)(2,1)S(1)}, u32[]{:S(2)}, u32[]{:S(2)}) collective-permute-start(bf16[96,1024]{1,0:T(8,128)(2,1)S(1)} %slice.21), channel_id=1, source_target_pairs={{0,14},{1,15},{2,0},{3,1},{4,2},{5,3},{6,4},{7,5},{8,6},{9,7},{10,... | collective-permute-start | bytes 589832 | tf_op jit(solution)/shard_map/ppermute | solution.py:394
  163.4 2.5 %collective-permute-start.15 = (bf16[192,1024]{1,0:T(8,128)(2,1)S(1)}, bf16[192,1024]{1,0:T(8,128)(2,1)S(1)}, u32[]{:S(2)}, u32[]{:S(2)}) collective-permute-start(bf16[192,1024]{1,0:T(8,128)(2,1)S(1)} %collective-permute-done.9.refs_4_), channel_id=1, source_target_pairs={{0,1},{1,0},{2,3},{3,2},{4,5},{5,4},{6,7},{7,6},{8,9},{9,8},{10,11... | collective-permute-start | bytes 1179656 | tf_op jit(solution)/shard_map/ppermute | solution.py:398
  166.0 0.5 collective-permute-start.16
  166.5 4.7 %terms.3 = (f32[768,1024]{1,0:T(8,128)S(1)}, f32[768,128]{1,0:T(8,128)S(1)}) custom-call(bf16[192,1024]{1,0:T(8,128)(2,1)S(1)} %pad_maximum_fusion.1.refs_0_, bf16[192,1024]{1,0:T(8,128)(2,1)S(1)} %collective-permute-done.4.refs_1_, bf16[192,1024]{1,0:T(8,128)(2,1)S(1)} %collective-permute-done.5.refs_2_, ...), custom_call_target="tpu_custom_call" | custom-call | flops 3623878656 | bytes 6291456 | tf_op jit(solution)/shard_map/terms/pallas_call | solution.py:313
  171.2 0.5 collective-permute-start.17
  171.7 0.1 collective-permute-start.18
  171.8 3.1 %terms.4 = (f32[768,1024]{1,0:T(8,128)S(1)}, f32[768,128]{1,0:T(8,128)S(1)}) custom-call(bf16[192,1024]{1,0:T(8,128)(2,1)S(1)} %pad_maximum_fusion.1.refs_0_, bf16[192,1024]{1,0:T(8,128)(2,1)S(1)} %collective-permute-done.4.refs_1_, bf16[192,1024]{1,0:T(8,128)(2,1)S(1)} %collective-permute-done.5.refs_2_, ...), custom_call_target="tpu_custom_call" | custom-call | flops 2415919104 | bytes 6291456 | tf_op jit(solution)/shard_map/terms/pallas_call | solution.py:313
  175.0 4.8 %terms.5 = (bf16[96,1152]{1,0:T(8,128)(2,1)S(1)}, bf16[96,1152]{1,0:T(8,128)(2,1)S(1)}, bf16[96,1152]{1,0:T(8,128)(2,1)S(1)}, bf16[96,1152]{1,0:T(8,128)(2,1)S(1...) custom-call(bf16[192,1024]{1,0:T(8,128)(2,1)S(1)} %pad_maximum_fusio, ...), custom_call_target="tpu_custom_call" | custom-call | flops 3623878656 | bytes 6291456 | tf_op jit(solution)/shard_map/terms/pallas_call | solution.py:313
  179.8 1.1 collective-permute-start.24
  180.9 0.2 collective-permute-start.25
  181.1 1.6 collective-permute-start.26
  182.6 2.0 collective-permute-start.27
  184.6 0.6 collective-permute-start.28
  185.2 1.3 collective-permute-done.24
  186.5 0.7 collective-permute-start.29
  187.2 3.5 %collective-permute-done.25 = bf16[96,1152]{1,0:T(8,128)(2,1)S(1)} collective-permute-done((bf16[96,1152]{1,0:T(8,128)(2,1)S(1)}, bf16[96,1152]{1,0:T(8,128)(2,1)S(1)}, u32[]{:S(2)}, u32[]{:S(2)}) %collective-permute-start.25) | collective-permute-done | bytes 221216 | tf_op jit(solution)/shard_map/ppermute | solution.py:403
  190.7 0.0 collective-permute-start.30
  190.7 4.7 %collective-permute-done.26 = bf16[96,1152]{1,0:T(8,128)(2,1)S(1)} collective-permute-done((bf16[96,1152]{1,0:T(8,128)(2,1)S(1)}, bf16[96,1152]{1,0:T(8,128)(2,1)S(1)}, u32[]{:S(2)}, u32[]{:S(2)}) %collective-permute-start.26) | collective-permute-done | bytes 221216 | tf_op jit(solution)/shard_map/ppermute | solution.py:403
  195.3 4.3 %collective-permute-done.27 = bf16[96,1152]{1,0:T(8,128)(2,1)S(1)} collective-permute-done((bf16[96,1152]{1,0:T(8,128)(2,1)S(1)}, bf16[96,1152]{1,0:T(8,128)(2,1)S(1)}, u32[]{:S(2)}, u32[]{:S(2)}) %collective-permute-start.27) | collective-permute-done | bytes 221216 | tf_op jit(solution)/shard_map/ppermute | solution.py:403
  199.7 5.9 %collective-permute-done.28 = bf16[96,1152]{1,0:T(8,128)(2,1)S(1)} collective-permute-done((bf16[96,1152]{1,0:T(8,128)(2,1)S(1)}, bf16[96,1152]{1,0:T(8,128)(2,1)S(1)}, u32[]{:S(2)}, u32[]{:S(2)}) %collective-permute-start.28) | collective-permute-done | bytes 221216 | tf_op jit(solution)/shard_map/ppermute | solution.py:403
  205.6 1.4 collective-permute-done.30
  207.0 0.2 convert_add_fusion
  207.2 0.7 log_reduce_fusion
  207.9 0.8 slice_divide_fusion
  (24 shorter events, 0.2 us)
Async XLA Ops:
  0.6 4.9 %collective-permute-start = (f32[96,1024]{1,0:T(8,128)}, f32[96,1024]{1,0:T(8,128)S(1)}, u32[]{:S(2)}, u32[]{:S(2)}) collective-permute-start(f32[96,1024]{1,0:T(8,128)} %x_ref.3), channel_id=1, source_target_pairs={{0,1},{1,0},{2,3},{3,2},{4,5},{5,4},{6,7},{7,6},{8,9},{9,8},{10,11... | collective-permute-start | bytes 1179656 | tf_op jit(solution)/shard_map/ppermute | solution.py:355
  5.5 0.7 copy-start.1
  61.6 23.7 %copy-start = (f32[96,1024]{1,0:T(8,128)S(1)}, f32[96,1024]{1,0:T(8,128)}, u32[]{:S(2)}) copy-start(f32[96,1024]{1,0:T(8,128)} %x_ref.3) | copy-start | bytes 1179652
  76.8 8.5 %collective-permute-start.1 = (f32[256,1152]{1,0:T(8,128)S(1)}, f32[256,1152]{1,0:T(8,128)S(1)}, u32[]{:S(2)}, u32[]{:S(2)}) collective-permute-start(f32[256,1152]{1,0:T(8,128)S(1)} %bitcast.3), channel_id=1, source_target_pairs={{0,1},{1,0},{2,3},{3,2},{4,5},{5,4},{6,7},{7,6},{8,9},{9,8},{10,11... | collective-permute-start | bytes 3538952 | tf_op jit(solution)/shard_map/ppermute | solution.py:367
  113.6 7.7 %collective-permute-start.2 = (bf16[96,1024]{1,0:T(8,128)(2,1)S(1)}, bf16[96,1024]{1,0:T(8,128)(2,1)S(1)}, u32[]{:S(2)}, u32[]{:S(2)}) collective-permute-start(bf16[96,1024]{1,0:T(8,128)(2,1)S(1)} %whiten.1), channel_id=1, source_target_pairs={{0,16},{1,17},{2,18},{3,19},{4,20},{5,21},{6,22},{7,23},{8,24},{9,... | collective-permute-start | bytes 589832 | tf_op jit(solution)/shard_map/ppermute | solution.py:378
  121.3 10.7 %collective-permute-start.7 = (bf16[192,1024]{1,0:T(8,128)(2,1)S(1)}, bf16[192,1024]{1,0:T(8,128)(2,1)S(1)}, u32[]{:S(2)}, u32[]{:S(2)}) collective-permute-start(bf16[192,1024]{1,0:T(8,128)(2,1)S(1)} %pad_maximum_fusion.refs_4_), channel_id=1, source_target_pairs={{0,2},{1,3},{2,4},{3,5},{4,6},{5,7},{6,8},{7,9},{8,10},{9,11},{10,... | collective-permute-start | bytes 1179656 | tf_op jit(solution)/shard_map/ppermute | solution.py:390
  122.7 12.7 %collective-permute-start.10 = (bf16[192,1024]{1,0:T(8,128)(2,1)S(1)}, bf16[192,1024]{1,0:T(8,128)(2,1)S(1)}, u32[]{:S(2)}, u32[]{:S(2)}) collective-permute-start(bf16[192,1024]{1,0:T(8,128)(2,1)S(1)} %pad_maximum_fusion.refs_4_), channel_id=1, source_target_pairs={{0,14},{1,15},{2,0},{3,1},{4,2},{5,3},{6,4},{7,5},{8,6},{9,7},{10,... | collective-permute-start | bytes 1179656 | tf_op jit(solution)/shard_map/ppermute | solution.py:391
  132.0 9.9 %collective-permute-start.8 = (bf16[192,1024]{1,0:T(8,128)(2,1)S(1)}, bf16[192,1024]{1,0:T(8,128)(2,1)S(1)}, u32[]{:S(2)}, u32[]{:S(2)}) collective-permute-start(bf16[192,1024]{1,0:T(8,128)(2,1)S(1)} %collective-permute-done.7.refs_5_), channel_id=1, source_target_pairs={{0,2},{1,3},{2,4},{3,5},{4,6},{5,7},{6,8},{7,9},{8,10},{9,11},{10,... | collective-permute-start | bytes 1179656 | tf_op jit(solution)/shard_map/ppermute | solution.py:390
  132.3 5.8 %collective-permute-start.3 = (bf16[96,1024]{1,0:T(8,128)(2,1)S(1)}, bf16[96,1024]{1,0:T(8,128)(2,1)S(1)}, u32[]{:S(2)}, u32[]{:S(2)}) collective-permute-start(bf16[96,1024]{1,0:T(8,128)(2,1)S(1)} %whiten.1), channel_id=1, source_target_pairs={{32,0},{33,1},{34,2},{35,3},{36,4},{37,5},{38,6},{39,7},{40,8},{41... | collective-permute-start | bytes 589832 | tf_op jit(solution)/shard_map/ppermute | solution.py:381
  132.8 17.2 %collective-permute-start.21 = (bf16[192,1024]{1,0:T(8,128)(2,1)S(1)}, bf16[192,1024]{1,0:T(8,128)(2,1)S(1)}, u32[]{:S(2)}, u32[]{:S(2)}) collective-permute-start(bf16[192,1024]{1,0:T(8,128)(2,1)S(1)} %pad_maximum_fusion.refs_4_), channel_id=1, source_target_pairs={{0,1},{1,0},{2,3},{3,2},{4,5},{5,4},{6,7},{7,6},{8,9},{9,8},{10,11... | collective-permute-start | bytes 1179656 | tf_op jit(solution)/shard_map/ppermute | solution.py:398
  135.4 11.2 %collective-permute-start.11 = (bf16[192,1024]{1,0:T(8,128)(2,1)S(1)}, bf16[192,1024]{1,0:T(8,128)(2,1)S(1)}, u32[]{:S(2)}, u32[]{:S(2)}) collective-permute-start(bf16[192,1024]{1,0:T(8,128)(2,1)S(1)} %collective-permute-done.10.refs_6_), channel_id=1, source_target_pairs={{0,14},{1,15},{2,0},{3,1},{4,2},{5,3},{6,4},{7,5},{8,6},{9,7},{10,... | collective-permute-start | bytes 1179656 | tf_op jit(solution)/shard_map/ppermute | solution.py:391
  138.1 12.2 %collective-permute-start.4 = (bf16[192,1024]{1,0:T(8,128)(2,1)S(1)}, bf16[192,1024]{1,0:T(8,128)(2,1)S(1)}, u32[]{:S(2)}, u32[]{:S(2)}) collective-permute-start(bf16[192,1024]{1,0:T(8,128)(2,1)S(1)} %pad_maximum_fusion.1.refs_0_), channel_id=1, source_target_pairs={{64,0},{65,1},{66,2},{67,3},{68,4},{69,5},{70,6},{71,7},{72,8},{73... | collective-permute-start | bytes 1179656 | tf_op jit(solution)/shard_map/ppermute | solution.py:384
  139.0 13.5 %collective-permute-start.5 = (bf16[192,1024]{1,0:T(8,128)(2,1)S(1)}, bf16[192,1024]{1,0:T(8,128)(2,1)S(1)}, u32[]{:S(2)}, u32[]{:S(2)}) collective-permute-start(bf16[192,1024]{1,0:T(8,128)(2,1)S(1)} %pad_maximum_fusion.1.refs_0_), channel_id=1, source_target_pairs={{128,0},{129,1},{130,2},{131,3},{132,4},{133,5},{134,6},{135,7},{1... | collective-permute-start | bytes 1179656 | tf_op jit(solution)/shard_map/ppermute | solution.py:384
  141.9 10.6 %collective-permute-start.9 = (bf16[192,1024]{1,0:T(8,128)(2,1)S(1)}, bf16[192,1024]{1,0:T(8,128)(2,1)S(1)}, u32[]{:S(2)}, u32[]{:S(2)}) collective-permute-start(bf16[192,1024]{1,0:T(8,128)(2,1)S(1)} %collective-permute-done.8.refs_4_), channel_id=1, source_target_pairs={{0,2},{1,3},{2,4},{3,5},{4,6},{5,7},{6,8},{7,9},{8,10},{9,11},{10,... | collective-permute-start | bytes 1179656 | tf_op jit(solution)/shard_map/ppermute | solution.py:390
  146.6 11.1 %collective-permute-start.12 = (bf16[192,1024]{1,0:T(8,128)(2,1)S(1)}, bf16[192,1024]{1,0:T(8,128)(2,1)S(1)}, u32[]{:S(2)}, u32[]{:S(2)}) collective-permute-start(bf16[192,1024]{1,0:T(8,128)(2,1)S(1)} %collective-permute-done.11.refs_5_), channel_id=1, source_target_pairs={{0,14},{1,15},{2,0},{3,1},{4,2},{5,3},{6,4},{7,5},{8,6},{9,7},{10,... | collective-permute-start | bytes 1179656 | tf_op jit(solution)/shard_map/ppermute | solution.py:391
  150.0 10.8 %collective-permute-start.6 = (bf16[192,1024]{1,0:T(8,128)(2,1)S(1)}, bf16[192,1024]{1,0:T(8,128)(2,1)S(1)}, u32[]{:S(2)}, u32[]{:S(2)}) collective-permute-start(bf16[192,1024]{1,0:T(8,128)(2,1)S(1)} %pad_maximum_fusion.1.refs_0_), channel_id=1, source_target_pairs={{192,0},{193,1},{194,2},{195,3},{196,4},{197,5},{198,6},{199,7},{2... | collective-permute-start | bytes 1179656 | tf_op jit(solution)/shard_map/ppermute | solution.py:384
  150.3 10.5 %collective-permute-start.22 = (bf16[192,1024]{1,0:T(8,128)(2,1)S(1)}, bf16[192,1024]{1,0:T(8,128)(2,1)S(1)}, u32[]{:S(2)}, u32[]{:S(2)}) collective-permute-start(bf16[192,1024]{1,0:T(8,128)(2,1)S(1)} %collective-permute-done.7.refs_5_), channel_id=1, source_target_pairs={{0,1},{1,0},{2,3},{3,2},{4,5},{5,4},{6,7},{7,6},{8,9},{9,8},{10,11... | collective-permute-start | bytes 1179656 | tf_op jit(solution)/shard_map/ppermute | solution.py:398
  152.5 10.9 %collective-permute-start.23 = (bf16[192,1024]{1,0:T(8,128)(2,1)S(1)}, bf16[192,1024]{1,0:T(8,128)(2,1)S(1)}, u32[]{:S(2)}, u32[]{:S(2)}) collective-permute-start(bf16[192,1024]{1,0:T(8,128)(2,1)S(1)} %collective-permute-done.10.refs_6_), channel_id=1, source_target_pairs={{0,1},{1,0},{2,3},{3,2},{4,5},{5,4},{6,7},{7,6},{8,9},{9,8},{10,11... | collective-permute-start | bytes 1179656 | tf_op jit(solution)/shard_map/ppermute | solution.py:398
  152.5 13.5 %collective-permute-start.19 = (bf16[192,1024]{1,0:T(8,128)(2,1)S(1)}, bf16[192,1024]{1,0:T(8,128)(2,1)S(1)}, u32[]{:S(2)}, u32[]{:S(2)}) collective-permute-start(bf16[192,1024]{1,0:T(8,128)(2,1)S(1)} %collective-permute-done.8.refs_4_), channel_id=1, source_target_pairs={{0,1},{1,0},{2,3},{3,2},{4,5},{5,4},{6,7},{7,6},{8,9},{9,8},{10,11... | collective-permute-start | bytes 1179656 | tf_op jit(solution)/shard_map/ppermute | solution.py:398
  157.6 14.2 %collective-permute-start.20 = (bf16[192,1024]{1,0:T(8,128)(2,1)S(1)}, bf16[192,1024]{1,0:T(8,128)(2,1)S(1)}, u32[]{:S(2)}, u32[]{:S(2)}) collective-permute-start(bf16[192,1024]{1,0:T(8,128)(2,1)S(1)} %collective-permute-done.11.refs_5_), channel_id=1, source_target_pairs={{0,1},{1,0},{2,3},{3,2},{4,5},{5,4},{6,7},{7,6},{8,9},{9,8},{10,11... | collective-permute-start | bytes 1179656 | tf_op jit(solution)/shard_map/ppermute | solution.py:398
  160.7 10.5 %collective-permute-start.13 = (bf16[96,1024]{1,0:T(8,128)(2,1)S(1)}, bf16[96,1024]{1,0:T(8,128)(2,1)S(1)}, u32[]{:S(2)}, u32[]{:S(2)}) collective-permute-start(bf16[96,1024]{1,0:T(8,128)(2,1)S(1)} %slice.20), channel_id=1, source_target_pairs={{0,2},{1,3},{2,4},{3,5},{4,6},{5,7},{6,8},{7,9},{8,10},{9,11},{10,... | collective-permute-start | bytes 589832 | tf_op jit(solution)/shard_map/ppermute | solution.py:394
  160.8 11.0 %collective-permute-start.14 = (bf16[96,1024]{1,0:T(8,128)(2,1)S(1)}, bf16[96,1024]{1,0:T(8,128)(2,1)S(1)}, u32[]{:S(2)}, u32[]{:S(2)}) collective-permute-start(bf16[96,1024]{1,0:T(8,128)(2,1)S(1)} %slice.21), channel_id=1, source_target_pairs={{0,14},{1,15},{2,0},{3,1},{4,2},{5,3},{6,4},{7,5},{8,6},{9,7},{10,... | collective-permute-start | bytes 589832 | tf_op jit(solution)/shard_map/ppermute | solution.py:394
  163.4 11.6 %collective-permute-start.15 = (bf16[192,1024]{1,0:T(8,128)(2,1)S(1)}, bf16[192,1024]{1,0:T(8,128)(2,1)S(1)}, u32[]{:S(2)}, u32[]{:S(2)}) collective-permute-start(bf16[192,1024]{1,0:T(8,128)(2,1)S(1)} %collective-permute-done.9.refs_4_), channel_id=1, source_target_pairs={{0,1},{1,0},{2,3},{3,2},{4,5},{5,4},{6,7},{7,6},{8,9},{9,8},{10,11... | collective-permute-start | bytes 1179656 | tf_op jit(solution)/shard_map/ppermute | solution.py:398
  166.0 9.0 %collective-permute-start.16 = (bf16[192,1024]{1,0:T(8,128)(2,1)S(1)}, bf16[192,1024]{1,0:T(8,128)(2,1)S(1)}, u32[]{:S(2)}, u32[]{:S(2)}) collective-permute-start(bf16[192,1024]{1,0:T(8,128)(2,1)S(1)} %collective-permute-done.12.refs_5_), channel_id=1, source_target_pairs={{0,1},{1,0},{2,3},{3,2},{4,5},{5,4},{6,7},{7,6},{8,9},{9,8},{10,11... | collective-permute-start | bytes 1179656 | tf_op jit(solution)/shard_map/ppermute | solution.py:398
  171.2 3.7 %collective-permute-start.17 = (bf16[96,1024]{1,0:T(8,128)(2,1)S(1)}, bf16[96,1024]{1,0:T(8,128)(2,1)S(1)}, u32[]{:S(2)}, u32[]{:S(2)}) collective-permute-start(bf16[96,1024]{1,0:T(8,128)(2,1)S(1)} %collective-permute-done.13.refs_6_), channel_id=1, source_target_pairs={{0,1},{1,0},{2,3},{3,2},{4,5},{5,4},{6,7},{7,6},{8,9},{9,8},{10,11... | collective-permute-start | bytes 589832 | tf_op jit(solution)/shard_map/ppermute | solution.py:398
  171.7 3.3 %collective-permute-start.18 = (bf16[96,1024]{1,0:T(8,128)(2,1)S(1)}, bf16[96,1024]{1,0:T(8,128)(2,1)S(1)}, u32[]{:S(2)}, u32[]{:S(2)}) collective-permute-start(bf16[96,1024]{1,0:T(8,128)(2,1)S(1)} %collective-permute-done.14.refs_7_), channel_id=1, source_target_pairs={{0,1},{1,0},{2,3},{3,2},{4,5},{5,4},{6,7},{7,6},{8,9},{9,8},{10,11... | collective-permute-start | bytes 589832 | tf_op jit(solution)/shard_map/ppermute | solution.py:398
  179.8 6.7 %collective-permute-start.24 = (bf16[96,1152]{1,0:T(8,128)(2,1)S(1)}, bf16[96,1152]{1,0:T(8,128)(2,1)S(1)}, u32[]{:S(2)}, u32[]{:S(2)}) collective-permute-start(bf16[96,1152]{1,0:T(8,128)(2,1)S(1)} %get-tuple-element.23), channel_id=1, source_target_pairs={{0,32},{1,33},{2,34},{3,35},{4,36},{5,37},{6,38},{7,39},{8,40},{9,... | collective-permute-start | bytes 663560 | tf_op jit(solution)/shard_map/ppermute | solution.py:403
  180.9 9.8 %collective-permute-start.25 = (bf16[96,1152]{1,0:T(8,128)(2,1)S(1)}, bf16[96,1152]{1,0:T(8,128)(2,1)S(1)}, u32[]{:S(2)}, u32[]{:S(2)}) collective-permute-start(bf16[96,1152]{1,0:T(8,128)(2,1)S(1)} %get-tuple-element.24), channel_id=1, source_target_pairs={{0,96},{1,97},{2,98},{3,99},{4,100},{5,101},{6,102},{7,103},{8,104... | collective-permute-start | bytes 663560 | tf_op jit(solution)/shard_map/ppermute | solution.py:403
  181.1 14.3 %collective-permute-start.26 = (bf16[96,1152]{1,0:T(8,128)(2,1)S(1)}, bf16[96,1152]{1,0:T(8,128)(2,1)S(1)}, u32[]{:S(2)}, u32[]{:S(2)}) collective-permute-start(bf16[96,1152]{1,0:T(8,128)(2,1)S(1)} %get-tuple-element.25), channel_id=1, source_target_pairs={{0,160},{1,161},{2,162},{3,163},{4,164},{5,165},{6,166},{7,167},{8... | collective-permute-start | bytes 663560 | tf_op jit(solution)/shard_map/ppermute | solution.py:403
  182.6 17.0 %collective-permute-start.27 = (bf16[96,1152]{1,0:T(8,128)(2,1)S(1)}, bf16[96,1152]{1,0:T(8,128)(2,1)S(1)}, u32[]{:S(2)}, u32[]{:S(2)}) collective-permute-start(bf16[96,1152]{1,0:T(8,128)(2,1)S(1)} %get-tuple-element.26), channel_id=1, source_target_pairs={{0,224},{1,225},{2,226},{3,227},{4,228},{5,229},{6,230},{7,231},{8... | collective-permute-start | bytes 663560 | tf_op jit(solution)/shard_map/ppermute | solution.py:403
  184.6 20.9 %collective-permute-start.28 = (bf16[96,1152]{1,0:T(8,128)(2,1)S(1)}, bf16[96,1152]{1,0:T(8,128)(2,1)S(1)}, u32[]{:S(2)}, u32[]{:S(2)}) collective-permute-start(bf16[96,1152]{1,0:T(8,128)(2,1)S(1)} %get-tuple-element.27), channel_id=1, source_target_pairs={{0,64},{1,65},{2,66},{3,67},{4,68},{5,69},{6,70},{7,71},{8,72},{9,... | collective-permute-start | bytes 663560 | tf_op jit(solution)/shard_map/ppermute | solution.py:403
  186.5 19.1 %collective-permute-start.29 = (bf16[96,1152]{1,0:T(8,128)(2,1)S(1)}, bf16[96,1152]{1,0:T(8,128)(2,1)S(1)}, u32[]{:S(2)}, u32[]{:S(2)}) collective-permute-start(bf16[96,1152]{1,0:T(8,128)(2,1)S(1)} %get-tuple-element.28), channel_id=1, source_target_pairs={{0,128},{1,129},{2,130},{3,131},{4,132},{5,133},{6,134},{7,135},{8... | collective-permute-start | bytes 663560 | tf_op jit(solution)/shard_map/ppermute | solution.py:403
  190.7 16.3 %collective-permute-start.30 = (bf16[96,1152]{1,0:T(8,128)(2,1)S(1)}, bf16[96,1152]{1,0:T(8,128)(2,1)S(1)}, u32[]{:S(2)}, u32[]{:S(2)}) collective-permute-start(bf16[96,1152]{1,0:T(8,128)(2,1)S(1)} %get-tuple-element.29), channel_id=1, source_target_pairs={{0,192},{1,193},{2,194},{3,195},{4,196},{5,197},{6,198},{7,199},{8... | collective-permute-start | bytes 663560 | tf_op jit(solution)/shard_map/ppermute | solution.py:403

commit v4 on v3

--- a/solution.py
+++ b/solution.py
@@ -376,13 +376,16 @@
         return pairs
 
     far = send(white, perm=shift(sizes, dx=1))
+    ys = row_count // 2
+    along = {dy: send(white, perm=row_shift(dy, 0, True)) for dy in {1, ys - 1}}
     pair = jnp.concatenate([white, far], 0)
-    pair, later = lax.optimization_barrier((pair, white))
+    pair, later, along = lax.optimization_barrier((pair, white, along))
     near = send(later, perm=row_shift(0, 1, True))
-    asked = jnp.concatenate([white, near], 0)
-    queries = [asked] + [
-        send(asked, perm=row_shift(dy, 0, True)) for dy in range(1, row_count // 2)
-    ]
+    queries = [white, near]
+    for dy in range(1, ys):
+        if dy not in along:
+            along[dy] = send(later, perm=row_shift(dy, 0, True))
+        queries += [along[dy], send(near, perm=row_shift(dy, 0, True))]
     right = left = pair
     up, down = shift(sizes, dz=1), shift(sizes, dz=-1)
     arrived = []

time: 213 us -> 210 us (0.986)
  waiting for transfers between devices: 50.1 us -> 42.5 us
  starting transfers between devices: 43.9 us -> 48.4 us
    ppermute x3, waiting for transfers between devices: 7.67 us -> 0.01 us  [shards(): left = send(left, perm=down)]
    ppermute x7, starting transfers between devices: 6.09 us -> 12.1 us  [shards(): sums = sums + send(part, perm=row_shift(dy, dx, False)).astype(F32)]
    ppermute x3, waiting for transfers between devices: 9.63 us -> 13.7 us  [shards(): right = send(right, perm=up)]
    ppermute x7, waiting for transfers between devices: 21.1 us -> 18.6 us  [shards(): sums = sums + send(part, perm=row_shift(dy, dx, False)).astype(F32)]
  transfers between devices with their start and end apart: 31 -> 34, of which waited for: 14 -> 13; matrix products, arithmetic and copies ran while one was open for 0% -> 0% of each run, Pallas kernels for 4% -> 4%
where the time goes in v4:
time: 210 us; the launch traced here: 206 us
  blocking collectives  66.2 us (32%)
  starting transfers between devices  48.4 us (23%)
  Pallas kernels  45 us (21%)
  waiting for transfers between devices  42.5 us (20%)
    pallas_call x1, Pallas kernels, whiten(): pl.pallas_call(functools.partial(whiten_kernel, count), out_shape=jax.Sha...  28.5 us
    all_to_all x1, blocking collectives, shards(): mine = lax.all_to_all(mine.reshape(row_count, -1, wide), 'row', 0, 0).sum(0)  20.1 us
    all_to_all x1, blocking collectives, shards(): lax.all_to_all(mine.reshape(half, -1, wide), 'col', 0, 0, axis_index_grou...  18.8 us
    ppermute x7, waiting for transfers between devices, shards(): sums = sums + send(part, perm=row_shift(dy, dx, False)).astype(F32)  18.6 us
    all_to_all x1, blocking collectives, shards(): lax.all_to_all(jnp.broadcast_to(mine[None], (row_count,) + mine.shape), '...  15.2 us
    ppermute x3, waiting for transfers between devices, shards(): right = send(right, perm=up)  13.7 us
    pallas_call x3, Pallas kernels, terms(): pl.pallas_call(functools.partial(terms_kernel, rows, not state, last, len...  12.7 us
    all_to_all x1, blocking collectives, shards(): lax.all_to_all(jnp.broadcast_to(mine[None], (half,) + mine.shape), 'col',...  12.1 us
  transfers between devices with their start and end apart: 34, of which 13 were waited for; matrix products, arithmetic and copies ran while one was open for 0% of the time, Pallas kernels for 4%

profile of v4, /device:TPU:1, one launch (start us, length us, event | category | flops | bytes accessed | tf_op | source)
XLA Modules:
  0.0 206.3 jit_solution(2389517790056391308)
XLA Ops:
  0.6 3.3 %collective-permute-start = (f32[96,1024]{1,0:T(8,128)}, f32[96,1024]{1,0:T(8,128)S(1)}, u32[]{:S(2)}, u32[]{:S(2)}) collective-permute-start(f32[96,1024]{1,0:T(8,128)} %x_ref.3), channel_id=1, source_target_pairs={{0,1},{1,0},{2,3},{3,2},{4,5},{5,4},{6,7},{7,6},{8,9},{9,8},{10,11... | collective-permute-start | bytes 1179656 | tf_op jit(solution)/shard_map/ppermute | solution.py:355
  4.0 1.6 collective-permute-done.y_ref
  5.5 0.7 copy-done.1
  6.3 3.9 %moments.1 = f32[256,1152]{1,0:T(8,128)} custom-call(s32[1]{0:T(128)} %bitcast.core_ref, f32[96,1024]{1,0:T(8,128)} %x_ref.3, f32[96,1024]{1,0:T(8,128)} %copy-done.1), custom_call_target="tpu_custom_call" | custom-call | tf_op jit(solution)/shard_map/moments/pallas_call | solution.py:84
  10.1 20.1 %all_to_all.20 = f32[8,32,1152]{2,1,0:T(8,128)S(1)} all-to-all(f32[8,32,1152]{2,1,0:T(8,128)} %bitcast.5), channel_id=1, replica_groups=mesh['row'=8,'col'=32] {'row'}, dimensions={0} | all-to-all | bytes 2359296 | tf_op jit(solution)/shard_map/all_to_all | solution.py:357
  30.2 0.1 reduce_sum.18
  30.3 0.1 reshape.20
  30.4 18.8 %all_to_all.21 = f32[16,2,1152]{2,1,0:T(2,128)S(1)} all-to-all(f32[16,2,1152]{2,1,0:T(2,128)S(1)} %reshape.20), channel_id=1, replica_groups={{0,2,4,6,8,10,12,14,16,18,20,22,24,26,28,30},{1,3,5,7,9,11,13,15,17,19,..., dimensions={0} | all-to-all | bytes 294912 | tf_op jit(solution)/shard_map/all_to_all | solution.py:358
  49.2 0.1 reduce_sum.19
  49.3 12.1 %all_to_all.22 = f32[16,2,1152]{2,1,0:T(2,128)S(1)} all-to-all(f32[16,2,1152]{2,1,0:T(2,128)S(1)} %broadcast_in_dim.18), channel_id=1, replica_groups={{0,2,4,6,8,10,12,14,16,18,20,22,24,26,28,30},{1,3,5,7,9,11,13,15,17,19,..., dimensions={0} | all-to-all | bytes 294912 | tf_op jit(solution)/shard_map/all_to_all | solution.py:361
  61.4 0.1 broadcast_in_dim.19
  61.5 0.1 broadcast_in_dim.20
  61.6 0.0 copy-start
  61.6 15.2 %all_to_all.23 = f32[8,32,1152]{2,1,0:T(8,128)S(1)} all-to-all(f32[8,32,1152]{2,1,0:T(8,128)S(1)} %broadcast_in_dim.20), channel_id=1, replica_groups=mesh['row'=8,'col'=32] {'row'}, dimensions={0} | all-to-all | bytes 2359296 | tf_op jit(solution)/shard_map/all_to_all | solution.py:364
  76.8 5.7 %collective-permute-start.1 = (f32[256,1152]{1,0:T(8,128)S(1)}, f32[256,1152]{1,0:T(8,128)S(1)}, u32[]{:S(2)}, u32[]{:S(2)}) collective-permute-start(f32[256,1152]{1,0:T(8,128)S(1)} %bitcast.3), channel_id=1, source_target_pairs={{0,1},{1,0},{2,3},{3,2},{4,5},{5,4},{6,7},{7,6},{8,9},{9,8},{10,11... | collective-permute-start | bytes 3538952 | tf_op jit(solution)/shard_map/ppermute | solution.py:367
  82.5 2.5 %collective-permute-done.1.other_ref = f32[256,1152]{1,0:T(8,128)S(1)} collective-permute-done((f32[256,1152]{1,0:T(8,128)S(1)}, f32[256,1152]{1,0:T(8,128)S(1)}, u32[]{:S(2)}, u32[]{:S(2)}) %collective-permute-start.1) | collective-permute-done | bytes 1179680 | tf_op jit(solution)/shard_map/ppermute | solution.py:367
  84.9 28.5 %whiten.1.refs_0_ = bf16[96,1024]{1,0:T(8,128)(2,1)S(1)} custom-call(s32[1]{0:T(128)} %bitcast.core_ref, f32[256,1152]{1,0:T(8,128)S(1)} %bitcast.4, f32[256,1152]{1,0:T(8,128)S(1)} %collective-permute-done.1.other_ref, f32[96,1024]{1,0:T(8,128)S(1)} %copy-done), custom_call_target="tpu_custom_call" | custom-call | tf_op jit(solution)/shard_map/whiten/pallas_call | solution.py:213
  113.5 1.5 collective-permute-start.2
  115.0 0.8 collective-permute-start.3
  115.7 0.7 collective-permute-start.4
  116.5 4.7 %collective-permute-done.2 = bf16[96,1024]{1,0:T(8,128)(2,1)S(1)} collective-permute-done((bf16[96,1024]{1,0:T(8,128)(2,1)S(1)}, bf16[96,1024]{1,0:T(8,128)(2,1)S(1)}, u32[]{:S(2)}, u32[]{:S(2)}) %collective-permute-start.2) | collective-permute-done | bytes 196640 | tf_op jit(solution)/shard_map/ppermute | solution.py:378
  121.2 0.0 collective-permute-done.3.refs_2_
  121.2 1.2 collective-permute-done.4.refs_6_
  122.4 1.2 collective-permute-start.10
  123.6 1.6 collective-permute-start.13
  125.3 7.3 %collective-permute-done.10.refs_9_ = bf16[192,1024]{1,0:T(8,128)(2,1)S(1)} collective-permute-done((bf16[192,1024]{1,0:T(8,128)(2,1)S(1)}, bf16[192,1024]{1,0:T(8,128)(2,1)S(1)}, u32[]{:S(2)}, u32[]{:S(2)}) %collective-permute-start.10) | collective-permute-done | bytes 393248 | tf_op jit(solution)/shard_map/ppermute | solution.py:393
  132.6 0.0 collective-permute-start.11
  132.6 2.7 %collective-permute-start.14 = (bf16[192,1024]{1,0:T(8,128)(2,1)S(1)}, bf16[192,1024]{1,0:T(8,128)(2,1)S(1)}, u32[]{:S(2)}, u32[]{:S(2)}) collective-permute-start(bf16[192,1024]{1,0:T(8,128)(2,1)S(1)} %collective-permute-done.13.refs_10_), channel_id=1, source_target_pairs={{0,14},{1,15},{2,0},{3,1},{4,2},{5,3},{6,4},{7,5},{8,6},{9,7},{10,... | collective-permute-start | bytes 1179656 | tf_op jit(solution)/shard_map/ppermute | solution.py:394
  135.2 0.0 collective-permute-start.5
  135.3 6.4 %collective-permute-done.11.refs_8_ = bf16[192,1024]{1,0:T(8,128)(2,1)S(1)} collective-permute-done((bf16[192,1024]{1,0:T(8,128)(2,1)S(1)}, bf16[192,1024]{1,0:T(8,128)(2,1)S(1)}, u32[]{:S(2)}, u32[]{:S(2)}) %collective-permute-start.11) | collective-permute-done | bytes 393248 | tf_op jit(solution)/shard_map/ppermute | solution.py:393
  141.6 1.0 collective-permute-start.6
  142.6 0.3 collective-permute-start.8
  142.9 0.4 collective-permute-start.9
  143.3 2.6 %collective-permute-start.15 = (bf16[192,1024]{1,0:T(8,128)(2,1)S(1)}, bf16[192,1024]{1,0:T(8,128)(2,1)S(1)}, u32[]{:S(2)}, u32[]{:S(2)}) collective-permute-start(bf16[192,1024]{1,0:T(8,128)(2,1)S(1)} %collective-permute-done.14.refs_9_), channel_id=1, source_target_pairs={{0,14},{1,15},{2,0},{3,1},{4,2},{5,3},{6,4},{7,5},{8,6},{9,7},{10,... | collective-permute-start | bytes 1179656 | tf_op jit(solution)/shard_map/ppermute | solution.py:394
  145.9 0.3 collective-permute-done.6.refs_3_
  146.1 4.9 %collective-permute-start.24 = (bf16[192,1024]{1,0:T(8,128)(2,1)S(1)}, bf16[192,1024]{1,0:T(8,128)(2,1)S(1)}, u32[]{:S(2)}, u32[]{:S(2)}) collective-permute-start(bf16[192,1024]{1,0:T(8,128)(2,1)S(1)} %pad_maximum_fusion.refs_8_), channel_id=1, source_target_pairs={{0,1},{1,0},{2,3},{3,2},{4,5},{5,4},{6,7},{7,6},{8,9},{9,8},{10,11... | collective-permute-start | bytes 1179656 | tf_op jit(solution)/shard_map/ppermute | solution.py:401
  151.0 2.6 %collective-permute-start.25 = (bf16[192,1024]{1,0:T(8,128)(2,1)S(1)}, bf16[192,1024]{1,0:T(8,128)(2,1)S(1)}, u32[]{:S(2)}, u32[]{:S(2)}) collective-permute-start(bf16[192,1024]{1,0:T(8,128)(2,1)S(1)} %collective-permute-done.10.refs_9_), channel_id=1, source_target_pairs={{0,1},{1,0},{2,3},{3,2},{4,5},{5,4},{6,7},{7,6},{8,9},{9,8},{10,11... | collective-permute-start | bytes 1179656 | tf_op jit(solution)/shard_map/ppermute | solution.py:401
  153.7 2.0 collective-permute-start.26
  155.7 0.0 collective-permute-start.22
  155.7 0.5 collective-permute-start.23
  156.2 0.1 collective-permute-start.16
  156.3 3.2 %collective-permute-start.17 = (bf16[96,1024]{1,0:T(8,128)(2,1)S(1)}, bf16[96,1024]{1,0:T(8,128)(2,1)S(1)}, u32[]{:S(2)}, u32[]{:S(2)}) collective-permute-start(bf16[96,1024]{1,0:T(8,128)(2,1)S(1)} %slice.21), channel_id=1, source_target_pairs={{0,14},{1,15},{2,0},{3,1},{4,2},{5,3},{6,4},{7,5},{8,6},{9,7},{10,... | collective-permute-start | bytes 589832 | tf_op jit(solution)/shard_map/ppermute | solution.py:397
  159.5 0.3 collective-permute-start.18
  159.8 0.4 collective-permute-start.19
  160.2 4.7 %terms.3 = (f32[768,1024]{1,0:T(8,128)S(1)}, f32[768,128]{1,0:T(8,128)S(1)}) custom-call(bf16[96,1024]{1,0:T(8,128)(2,1)S(1)} %whiten.1.refs_0_, bf16[96,1024]{1,0:T(8,128)(2,1)S(1)} %collective-permute-done.5.refs_1_, bf16[96,1024]{1,0:T(8,128)(2,1)S(1)} %collective-permute-done.3.refs_2_, bf16[96,1024]{1,0:T(8,128)(2,1)S(1)} %collective-permute-done.6.refs_3_, ...), custom_call_target="tpu_custom_call" | custom-call | flops 3623878656 | bytes 6291456 | tf_op jit(solution)/shard_map/terms/pallas_call | solution.py:313
  165.0 0.4 collective-permute-start.20
  165.3 0.2 collective-permute-start.21
  165.6 3.1 %terms.4 = (f32[768,1024]{1,0:T(8,128)S(1)}, f32[768,128]{1,0:T(8,128)S(1)}) custom-call(bf16[96,1024]{1,0:T(8,128)(2,1)S(1)} %whiten.1.refs_0_, bf16[96,1024]{1,0:T(8,128)(2,1)S(1)} %collective-permute-done.5.refs_1_, bf16[96,1024]{1,0:T(8,128)(2,1)S(1)} %collective-permute-done.3.refs_2_, bf16[96,1024]{1,0:T(8,128)(2,1)S(1)} %collective-permute-done.6.refs_3_, ...), custom_call_target="tpu_custom_call" | custom-call | flops 2415919104 | bytes 6291456 | tf_op jit(solution)/shard_map/terms/pallas_call | solution.py:313
  168.8 4.8 %terms.5 = (bf16[96,1152]{1,0:T(8,128)(2,1)S(1)}, bf16[96,1152]{1,0:T(8,128)(2,1)S(1)}, bf16[96,1152]{1,0:T(8,128)(2,1)S(1)}, bf16[96,1152]{1,0:T(8,128)(2,1)S(1...) custom-call(bf16[96,1024]{1,0:T(8,128)(2,1)S(1)} %whiten.1.refs_0_, ...), custom_call_target="tpu_custom_call" | custom-call | flops 3623878656 | bytes 6291456 | tf_op jit(solution)/shard_map/terms/pallas_call | solution.py:313
  173.6 0.8 collective-permute-start.27
  174.4 2.8 %collective-permute-start.28 = (bf16[96,1152]{1,0:T(8,128)(2,1)S(1)}, bf16[96,1152]{1,0:T(8,128)(2,1)S(1)}, u32[]{:S(2)}, u32[]{:S(2)}) collective-permute-start(bf16[96,1152]{1,0:T(8,128)(2,1)S(1)} %get-tuple-element.28), channel_id=1, source_target_pairs={{0,96},{1,97},{2,98},{3,99},{4,100},{5,101},{6,102},{7,103},{8,104... | collective-permute-start | bytes 663560 | tf_op jit(solution)/shard_map/ppermute | solution.py:406
  177.2 2.0 collective-permute-start.29
  179.2 2.7 %collective-permute-start.30 = (bf16[96,1152]{1,0:T(8,128)(2,1)S(1)}, bf16[96,1152]{1,0:T(8,128)(2,1)S(1)}, u32[]{:S(2)}, u32[]{:S(2)}) collective-permute-start(bf16[96,1152]{1,0:T(8,128)(2,1)S(1)} %get-tuple-element.30), channel_id=1, source_target_pairs={{0,224},{1,225},{2,226},{3,227},{4,228},{5,229},{6,230},{7,231},{8... | collective-permute-start | bytes 663560 | tf_op jit(solution)/shard_map/ppermute | solution.py:406
  181.9 2.3 %collective-permute-start.32 = (bf16[96,1152]{1,0:T(8,128)(2,1)S(1)}, bf16[96,1152]{1,0:T(8,128)(2,1)S(1)}, u32[]{:S(2)}, u32[]{:S(2)}) collective-permute-start(bf16[96,1152]{1,0:T(8,128)(2,1)S(1)} %get-tuple-element.32), channel_id=1, source_target_pairs={{0,128},{1,129},{2,130},{3,131},{4,132},{5,133},{6,134},{7,135},{8... | collective-permute-start | bytes 663560 | tf_op jit(solution)/shard_map/ppermute | solution.py:406
  184.2 3.4 %collective-permute-done.28 = bf16[96,1152]{1,0:T(8,128)(2,1)S(1)} collective-permute-done((bf16[96,1152]{1,0:T(8,128)(2,1)S(1)}, bf16[96,1152]{1,0:T(8,128)(2,1)S(1)}, u32[]{:S(2)}, u32[]{:S(2)}) %collective-permute-start.28) | collective-permute-done | bytes 221216 | tf_op jit(solution)/shard_map/ppermute | solution.py:406
  187.6 1.4 collective-permute-start.33
  189.0 4.5 %collective-permute-done.29 = bf16[96,1152]{1,0:T(8,128)(2,1)S(1)} collective-permute-done((bf16[96,1152]{1,0:T(8,128)(2,1)S(1)}, bf16[96,1152]{1,0:T(8,128)(2,1)S(1)}, u32[]{:S(2)}, u32[]{:S(2)}) %collective-permute-start.29) | collective-permute-done | bytes 221216 | tf_op jit(solution)/shard_map/ppermute | solution.py:406
  193.5 3.1 %collective-permute-done.30 = bf16[96,1152]{1,0:T(8,128)(2,1)S(1)} collective-permute-done((bf16[96,1152]{1,0:T(8,128)(2,1)S(1)}, bf16[96,1152]{1,0:T(8,128)(2,1)S(1)}, u32[]{:S(2)}, u32[]{:S(2)}) %collective-permute-start.30) | collective-permute-done | bytes 221216 | tf_op jit(solution)/shard_map/ppermute | solution.py:406
  196.6 1.9 collective-permute-done.31
  198.5 3.2 %collective-permute-done.32 = bf16[96,1152]{1,0:T(8,128)(2,1)S(1)} collective-permute-done((bf16[96,1152]{1,0:T(8,128)(2,1)S(1)}, bf16[96,1152]{1,0:T(8,128)(2,1)S(1)}, u32[]{:S(2)}, u32[]{:S(2)}) %collective-permute-start.32) | collective-permute-done | bytes 221216 | tf_op jit(solution)/shard_map/ppermute | solution.py:406
  201.6 2.6 %collective-permute-done.33 = bf16[96,1152]{1,0:T(8,128)(2,1)S(1)} collective-permute-done((bf16[96,1152]{1,0:T(8,128)(2,1)S(1)}, bf16[96,1152]{1,0:T(8,128)(2,1)S(1)}, u32[]{:S(2)}, u32[]{:S(2)}) %collective-permute-start.33) | collective-permute-done | bytes 221216 | tf_op jit(solution)/shard_map/ppermute | solution.py:406
  204.2 0.2 convert_add_fusion
  204.5 0.7 log_reduce_fusion
  205.2 0.8 slice_divide_fusion
  (29 shorter events, 0.2 us)
Async XLA Ops:
  0.6 4.9 %collective-permute-start = (f32[96,1024]{1,0:T(8,128)}, f32[96,1024]{1,0:T(8,128)S(1)}, u32[]{:S(2)}, u32[]{:S(2)}) collective-permute-start(f32[96,1024]{1,0:T(8,128)} %x_ref.3), channel_id=1, source_target_pairs={{0,1},{1,0},{2,3},{3,2},{4,5},{5,4},{6,7},{7,6},{8,9},{9,8},{10,11... | collective-permute-start | bytes 1179656 | tf_op jit(solution)/shard_map/ppermute | solution.py:355
  5.5 0.7 copy-start.1
  61.6 23.4 %copy-start = (f32[96,1024]{1,0:T(8,128)S(1)}, f32[96,1024]{1,0:T(8,128)}, u32[]{:S(2)}) copy-start(f32[96,1024]{1,0:T(8,128)} %x_ref.3) | copy-start | bytes 1179652
  76.8 8.1 %collective-permute-start.1 = (f32[256,1152]{1,0:T(8,128)S(1)}, f32[256,1152]{1,0:T(8,128)S(1)}, u32[]{:S(2)}, u32[]{:S(2)}) collective-permute-start(f32[256,1152]{1,0:T(8,128)S(1)} %bitcast.3), channel_id=1, source_target_pairs={{0,1},{1,0},{2,3},{3,2},{4,5},{5,4},{6,7},{7,6},{8,9},{9,8},{10,11... | collective-permute-start | bytes 3538952 | tf_op jit(solution)/shard_map/ppermute | solution.py:367
  113.5 7.7 %collective-permute-start.2 = (bf16[96,1024]{1,0:T(8,128)(2,1)S(1)}, bf16[96,1024]{1,0:T(8,128)(2,1)S(1)}, u32[]{:S(2)}, u32[]{:S(2)}) collective-permute-start(bf16[96,1024]{1,0:T(8,128)(2,1)S(1)} %whiten.1.refs_0_), channel_id=1, source_target_pairs={{0,16},{1,17},{2,18},{3,19},{4,20},{5,21},{6,22},{7,23},{8,24},{9,... | collective-permute-start | bytes 589832 | tf_op jit(solution)/shard_map/ppermute | solution.py:378
  115.0 6.2 %collective-permute-start.3 = (bf16[96,1024]{1,0:T(8,128)(2,1)S(1)}, bf16[96,1024]{1,0:T(8,128)(2,1)S(1)}, u32[]{:S(2)}, u32[]{:S(2)}) collective-permute-start(bf16[96,1024]{1,0:T(8,128)(2,1)S(1)} %whiten.1.refs_0_), channel_id=1, source_target_pairs={{64,0},{65,1},{66,2},{67,3},{68,4},{69,5},{70,6},{71,7},{72,8},{73... | collective-permute-start | bytes 589832 | tf_op jit(solution)/shard_map/ppermute | solution.py:380
  115.7 6.7 %collective-permute-start.4 = (bf16[96,1024]{1,0:T(8,128)(2,1)S(1)}, bf16[96,1024]{1,0:T(8,128)(2,1)S(1)}, u32[]{:S(2)}, u32[]{:S(2)}) collective-permute-start(bf16[96,1024]{1,0:T(8,128)(2,1)S(1)} %whiten.1.refs_0_), channel_id=1, source_target_pairs={{192,0},{193,1},{194,2},{195,3},{196,4},{197,5},{198,6},{199,7},{2... | collective-permute-start | bytes 589832 | tf_op jit(solution)/shard_map/ppermute | solution.py:380
  122.4 10.1 %collective-permute-start.10 = (bf16[192,1024]{1,0:T(8,128)(2,1)S(1)}, bf16[192,1024]{1,0:T(8,128)(2,1)S(1)}, u32[]{:S(2)}, u32[]{:S(2)}) collective-permute-start(bf16[192,1024]{1,0:T(8,128)(2,1)S(1)} %pad_maximum_fusion.refs_8_), channel_id=1, source_target_pairs={{0,2},{1,3},{2,4},{3,5},{4,6},{5,7},{6,8},{7,9},{8,10},{9,11},{10,... | collective-permute-start | bytes 1179656 | tf_op jit(solution)/shard_map/ppermute | solution.py:393
  123.6 8.9 %collective-permute-start.13 = (bf16[192,1024]{1,0:T(8,128)(2,1)S(1)}, bf16[192,1024]{1,0:T(8,128)(2,1)S(1)}, u32[]{:S(2)}, u32[]{:S(2)}) collective-permute-start(bf16[192,1024]{1,0:T(8,128)(2,1)S(1)} %pad_maximum_fusion.refs_8_), channel_id=1, source_target_pairs={{0,14},{1,15},{2,0},{3,1},{4,2},{5,3},{6,4},{7,5},{8,6},{9,7},{10,... | collective-permute-start | bytes 1179656 | tf_op jit(solution)/shard_map/ppermute | solution.py:394
  132.6 9.1 %collective-permute-start.11 = (bf16[192,1024]{1,0:T(8,128)(2,1)S(1)}, bf16[192,1024]{1,0:T(8,128)(2,1)S(1)}, u32[]{:S(2)}, u32[]{:S(2)}) collective-permute-start(bf16[192,1024]{1,0:T(8,128)(2,1)S(1)} %collective-permute-done.10.refs_9_), channel_id=1, source_target_pairs={{0,2},{1,3},{2,4},{3,5},{4,6},{5,7},{6,8},{7,9},{8,10},{9,11},{10,... | collective-permute-start | bytes 1179656 | tf_op jit(solution)/shard_map/ppermute | solution.py:393
  132.6 10.7 %collective-permute-start.14 = (bf16[192,1024]{1,0:T(8,128)(2,1)S(1)}, bf16[192,1024]{1,0:T(8,128)(2,1)S(1)}, u32[]{:S(2)}, u32[]{:S(2)}) collective-permute-start(bf16[192,1024]{1,0:T(8,128)(2,1)S(1)} %collective-permute-done.13.refs_10_), channel_id=1, source_target_pairs={{0,14},{1,15},{2,0},{3,1},{4,2},{5,3},{6,4},{7,5},{8,6},{9,7},{10,... | collective-permute-start | bytes 1179656 | tf_op jit(solution)/shard_map/ppermute | solution.py:394
  135.2 6.4 %collective-permute-start.5 = (bf16[96,1024]{1,0:T(8,128)(2,1)S(1)}, bf16[96,1024]{1,0:T(8,128)(2,1)S(1)}, u32[]{:S(2)}, u32[]{:S(2)}) collective-permute-start(bf16[96,1024]{1,0:T(8,128)(2,1)S(1)} %whiten.1.refs_0_), channel_id=1, source_target_pairs={{32,0},{33,1},{34,2},{35,3},{36,4},{37,5},{38,6},{39,7},{40,8},{41... | collective-permute-start | bytes 589832 | tf_op jit(solution)/shard_map/ppermute | solution.py:383
  135.3 7.6 %collective-permute-start.7 = (bf16[96,1024]{1,0:T(8,128)(2,1)S(1)}, bf16[96,1024]{1,0:T(8,128)(2,1)S(1)}, u32[]{:S(2)}, u32[]{:S(2)}) collective-permute-start(bf16[96,1024]{1,0:T(8,128)(2,1)S(1)} %whiten.1.refs_0_), channel_id=1, source_target_pairs={{128,0},{129,1},{130,2},{131,3},{132,4},{133,5},{134,6},{135,7},{1... | collective-permute-start | bytes 589832 | tf_op jit(solution)/shard_map/ppermute | solution.py:387
  141.6 14.1 %collective-permute-start.12 = (bf16[192,1024]{1,0:T(8,128)(2,1)S(1)}, bf16[192,1024]{1,0:T(8,128)(2,1)S(1)}, u32[]{:S(2)}, u32[]{:S(2)}) collective-permute-start(bf16[192,1024]{1,0:T(8,128)(2,1)S(1)} %collective-permute-done.11.refs_8_), channel_id=1, source_target_pairs={{0,2},{1,3},{2,4},{3,5},{4,6},{5,7},{6,8},{7,9},{8,10},{9,11},{10,... | collective-permute-start | bytes 1179656 | tf_op jit(solution)/shard_map/ppermute | solution.py:393
  141.6 4.5 %collective-permute-start.6 = (bf16[96,1024]{1,0:T(8,128)(2,1)S(1)}, bf16[96,1024]{1,0:T(8,128)(2,1)S(1)}, u32[]{:S(2)}, u32[]{:S(2)}) collective-permute-start(bf16[96,1024]{1,0:T(8,128)(2,1)S(1)} %collective-permute-done.5.refs_1_), channel_id=1, source_target_pairs={{64,0},{65,1},{66,2},{67,3},{68,4},{69,5},{70,6},{71,7},{72,8},{73... | collective-permute-start | bytes 589832 | tf_op jit(solution)/shard_map/ppermute | solution.py:388
  142.6 8.5 %collective-permute-start.8 = (bf16[96,1024]{1,0:T(8,128)(2,1)S(1)}, bf16[96,1024]{1,0:T(8,128)(2,1)S(1)}, u32[]{:S(2)}, u32[]{:S(2)}) collective-permute-start(bf16[96,1024]{1,0:T(8,128)(2,1)S(1)} %collective-permute-done.5.refs_1_), channel_id=1, source_target_pairs={{128,0},{129,1},{130,2},{131,3},{132,4},{133,5},{134,6},{135,7},{1... | collective-permute-start | bytes 589832 | tf_op jit(solution)/shard_map/ppermute | solution.py:388
  142.9 10.8 %collective-permute-start.9 = (bf16[96,1024]{1,0:T(8,128)(2,1)S(1)}, bf16[96,1024]{1,0:T(8,128)(2,1)S(1)}, u32[]{:S(2)}, u32[]{:S(2)}) collective-permute-start(bf16[96,1024]{1,0:T(8,128)(2,1)S(1)} %collective-permute-done.5.refs_1_), channel_id=1, source_target_pairs={{192,0},{193,1},{194,2},{195,3},{196,4},{197,5},{198,6},{199,7},{2... | collective-permute-start | bytes 589832 | tf_op jit(solution)/shard_map/ppermute | solution.py:388
  143.3 12.4 %collective-permute-start.15 = (bf16[192,1024]{1,0:T(8,128)(2,1)S(1)}, bf16[192,1024]{1,0:T(8,128)(2,1)S(1)}, u32[]{:S(2)}, u32[]{:S(2)}) collective-permute-start(bf16[192,1024]{1,0:T(8,128)(2,1)S(1)} %collective-permute-done.14.refs_9_), channel_id=1, source_target_pairs={{0,14},{1,15},{2,0},{3,1},{4,2},{5,3},{6,4},{7,5},{8,6},{9,7},{10,... | collective-permute-start | bytes 1179656 | tf_op jit(solution)/shard_map/ppermute | solution.py:394
  146.1 10.1 %collective-permute-start.24 = (bf16[192,1024]{1,0:T(8,128)(2,1)S(1)}, bf16[192,1024]{1,0:T(8,128)(2,1)S(1)}, u32[]{:S(2)}, u32[]{:S(2)}) collective-permute-start(bf16[192,1024]{1,0:T(8,128)(2,1)S(1)} %pad_maximum_fusion.refs_8_), channel_id=1, source_target_pairs={{0,1},{1,0},{2,3},{3,2},{4,5},{5,4},{6,7},{7,6},{8,9},{9,8},{10,11... | collective-permute-start | bytes 1179656 | tf_op jit(solution)/shard_map/ppermute | solution.py:401
  151.0 5.3 %collective-permute-start.25 = (bf16[192,1024]{1,0:T(8,128)(2,1)S(1)}, bf16[192,1024]{1,0:T(8,128)(2,1)S(1)}, u32[]{:S(2)}, u32[]{:S(2)}) collective-permute-start(bf16[192,1024]{1,0:T(8,128)(2,1)S(1)} %collective-permute-done.10.refs_9_), channel_id=1, source_target_pairs={{0,1},{1,0},{2,3},{3,2},{4,5},{5,4},{6,7},{7,6},{8,9},{9,8},{10,11... | collective-permute-start | bytes 1179656 | tf_op jit(solution)/shard_map/ppermute | solution.py:401
  153.7 5.8 %collective-permute-start.26 = (bf16[192,1024]{1,0:T(8,128)(2,1)S(1)}, bf16[192,1024]{1,0:T(8,128)(2,1)S(1)}, u32[]{:S(2)}, u32[]{:S(2)}) collective-permute-start(bf16[192,1024]{1,0:T(8,128)(2,1)S(1)} %collective-permute-done.13.refs_10_), channel_id=1, source_target_pairs={{0,1},{1,0},{2,3},{3,2},{4,5},{5,4},{6,7},{7,6},{8,9},{9,8},{10,11... | collective-permute-start | bytes 1179656 | tf_op jit(solution)/shard_map/ppermute | solution.py:401
  155.7 4.1 %collective-permute-start.22 = (bf16[192,1024]{1,0:T(8,128)(2,1)S(1)}, bf16[192,1024]{1,0:T(8,128)(2,1)S(1)}, u32[]{:S(2)}, u32[]{:S(2)}) collective-permute-start(bf16[192,1024]{1,0:T(8,128)(2,1)S(1)} %collective-permute-done.11.refs_8_), channel_id=1, source_target_pairs={{0,1},{1,0},{2,3},{3,2},{4,5},{5,4},{6,7},{7,6},{8,9},{9,8},{10,11... | collective-permute-start | bytes 1179656 | tf_op jit(solution)/shard_map/ppermute | solution.py:401
  155.7 9.9 %collective-permute-start.23 = (bf16[192,1024]{1,0:T(8,128)(2,1)S(1)}, bf16[192,1024]{1,0:T(8,128)(2,1)S(1)}, u32[]{:S(2)}, u32[]{:S(2)}) collective-permute-start(bf16[192,1024]{1,0:T(8,128)(2,1)S(1)} %collective-permute-done.14.refs_9_), channel_id=1, source_target_pairs={{0,1},{1,0},{2,3},{3,2},{4,5},{5,4},{6,7},{7,6},{8,9},{9,8},{10,11... | collective-permute-start | bytes 1179656 | tf_op jit(solution)/shard_map/ppermute | solution.py:401
  156.2 8.7 %collective-permute-start.16 = (bf16[96,1024]{1,0:T(8,128)(2,1)S(1)}, bf16[96,1024]{1,0:T(8,128)(2,1)S(1)}, u32[]{:S(2)}, u32[]{:S(2)}) collective-permute-start(bf16[96,1024]{1,0:T(8,128)(2,1)S(1)} %slice.20), channel_id=1, source_target_pairs={{0,2},{1,3},{2,4},{3,5},{4,6},{5,7},{6,8},{7,9},{8,10},{9,11},{10,... | collective-permute-start | bytes 589832 | tf_op jit(solution)/shard_map/ppermute | solution.py:397
  156.3 9.0 %collective-permute-start.17 = (bf16[96,1024]{1,0:T(8,128)(2,1)S(1)}, bf16[96,1024]{1,0:T(8,128)(2,1)S(1)}, u32[]{:S(2)}, u32[]{:S(2)}) collective-permute-start(bf16[96,1024]{1,0:T(8,128)(2,1)S(1)} %slice.21), channel_id=1, source_target_pairs={{0,14},{1,15},{2,0},{3,1},{4,2},{5,3},{6,4},{7,5},{8,6},{9,7},{10,... | collective-permute-start | bytes 589832 | tf_op jit(solution)/shard_map/ppermute | solution.py:397
  159.5 9.2 %collective-permute-start.18 = (bf16[192,1024]{1,0:T(8,128)(2,1)S(1)}, bf16[192,1024]{1,0:T(8,128)(2,1)S(1)}, u32[]{:S(2)}, u32[]{:S(2)}) collective-permute-start(bf16[192,1024]{1,0:T(8,128)(2,1)S(1)} %collective-permute-done.12.refs_8_), channel_id=1, source_target_pairs={{0,1},{1,0},{2,3},{3,2},{4,5},{5,4},{6,7},{7,6},{8,9},{9,8},{10,11... | collective-permute-start | bytes 1179656 | tf_op jit(solution)/shard_map/ppermute | solution.py:401
  159.8 8.9 %collective-permute-start.19 = (bf16[192,1024]{1,0:T(8,128)(2,1)S(1)}, bf16[192,1024]{1,0:T(8,128)(2,1)S(1)}, u32[]{:S(2)}, u32[]{:S(2)}) collective-permute-start(bf16[192,1024]{1,0:T(8,128)(2,1)S(1)} %collective-permute-done.15.refs_9_), channel_id=1, source_target_pairs={{0,1},{1,0},{2,3},{3,2},{4,5},{5,4},{6,7},{7,6},{8,9},{9,8},{10,11... | collective-permute-start | bytes 1179656 | tf_op jit(solution)/shard_map/ppermute | solution.py:401
  165.0 3.8 %collective-permute-start.20 = (bf16[96,1024]{1,0:T(8,128)(2,1)S(1)}, bf16[96,1024]{1,0:T(8,128)(2,1)S(1)}, u32[]{:S(2)}, u32[]{:S(2)}) collective-permute-start(bf16[96,1024]{1,0:T(8,128)(2,1)S(1)} %collective-permute-done.16.refs_10_), channel_id=1, source_target_pairs={{0,1},{1,0},{2,3},{3,2},{4,5},{5,4},{6,7},{7,6},{8,9},{9,8},{10,11... | collective-permute-start | bytes 589832 | tf_op jit(solution)/shard_map/ppermute | solution.py:401
  165.3 3.4 %collective-permute-start.21 = (bf16[96,1024]{1,0:T(8,128)(2,1)S(1)}, bf16[96,1024]{1,0:T(8,128)(2,1)S(1)}, u32[]{:S(2)}, u32[]{:S(2)}) collective-permute-start(bf16[96,1024]{1,0:T(8,128)(2,1)S(1)} %collective-permute-done.17.refs_11_), channel_id=1, source_target_pairs={{0,1},{1,0},{2,3},{3,2},{4,5},{5,4},{6,7},{7,6},{8,9},{9,8},{10,11... | collective-permute-start | bytes 589832 | tf_op jit(solution)/shard_map/ppermute | solution.py:401
  173.6 8.3 %collective-permute-start.27 = (bf16[96,1152]{1,0:T(8,128)(2,1)S(1)}, bf16[96,1152]{1,0:T(8,128)(2,1)S(1)}, u32[]{:S(2)}, u32[]{:S(2)}) collective-permute-start(bf16[96,1152]{1,0:T(8,128)(2,1)S(1)} %get-tuple-element.27), channel_id=1, source_target_pairs={{0,32},{1,33},{2,34},{3,35},{4,36},{5,37},{6,38},{7,39},{8,40},{9,... | collective-permute-start | bytes 663560 | tf_op jit(solution)/shard_map/ppermute | solution.py:406
  174.4 13.3 %collective-permute-start.28 = (bf16[96,1152]{1,0:T(8,128)(2,1)S(1)}, bf16[96,1152]{1,0:T(8,128)(2,1)S(1)}, u32[]{:S(2)}, u32[]{:S(2)}) collective-permute-start(bf16[96,1152]{1,0:T(8,128)(2,1)S(1)} %get-tuple-element.28), channel_id=1, source_target_pairs={{0,96},{1,97},{2,98},{3,99},{4,100},{5,101},{6,102},{7,103},{8,104... | collective-permute-start | bytes 663560 | tf_op jit(solution)/shard_map/ppermute | solution.py:406
  177.2 16.3 %collective-permute-start.29 = (bf16[96,1152]{1,0:T(8,128)(2,1)S(1)}, bf16[96,1152]{1,0:T(8,128)(2,1)S(1)}, u32[]{:S(2)}, u32[]{:S(2)}) collective-permute-start(bf16[96,1152]{1,0:T(8,128)(2,1)S(1)} %get-tuple-element.29), channel_id=1, source_target_pairs={{0,160},{1,161},{2,162},{3,163},{4,164},{5,165},{6,166},{7,167},{8... | collective-permute-start | bytes 663560 | tf_op jit(solution)/shard_map/ppermute | solution.py:406
  179.2 17.4 %collective-permute-start.30 = (bf16[96,1152]{1,0:T(8,128)(2,1)S(1)}, bf16[96,1152]{1,0:T(8,128)(2,1)S(1)}, u32[]{:S(2)}, u32[]{:S(2)}) collective-permute-start(bf16[96,1152]{1,0:T(8,128)(2,1)S(1)} %get-tuple-element.30), channel_id=1, source_target_pairs={{0,224},{1,225},{2,226},{3,227},{4,228},{5,229},{6,230},{7,231},{8... | collective-permute-start | bytes 663560 | tf_op jit(solution)/shard_map/ppermute | solution.py:406
  181.9 16.6 %collective-permute-start.31 = (bf16[96,1152]{1,0:T(8,128)(2,1)S(1)}, bf16[96,1152]{1,0:T(8,128)(2,1)S(1)}, u32[]{:S(2)}, u32[]{:S(2)}) collective-permute-start(bf16[96,1152]{1,0:T(8,128)(2,1)S(1)} %get-tuple-element.31), channel_id=1, source_target_pairs={{0,64},{1,65},{2,66},{3,67},{4,68},{5,69},{6,70},{7,71},{8,72},{9,... | collective-permute-start | bytes 663560 | tf_op jit(solution)/shard_map/ppermute | solution.py:406
  181.9 19.7 %collective-permute-start.32 = (bf16[96,1152]{1,0:T(8,128)(2,1)S(1)}, bf16[96,1152]{1,0:T(8,128)(2,1)S(1)}, u32[]{:S(2)}, u32[]{:S(2)}) collective-permute-start(bf16[96,1152]{1,0:T(8,128)(2,1)S(1)} %get-tuple-element.32), channel_id=1, source_target_pairs={{0,128},{1,129},{2,130},{3,131},{4,132},{5,133},{6,134},{7,135},{8... | collective-permute-start | bytes 663560 | tf_op jit(solution)/shard_map/ppermute | solution.py:406
  187.6 16.6 %collective-permute-start.33 = (bf16[96,1152]{1,0:T(8,128)(2,1)S(1)}, bf16[96,1152]{1,0:T(8,128)(2,1)S(1)}, u32[]{:S(2)}, u32[]{:S(2)}) collective-permute-start(bf16[96,1152]{1,0:T(8,128)(2,1)S(1)} %get-tuple-element.33), channel_id=1, source_target_pairs={{0,192},{1,193},{2,194},{3,195},{4,196},{5,197},{6,198},{7,199},{8... | collective-permute-start | bytes 663560 | tf_op jit(solution)/shard_map/ppermute | solution.py:406
